TPU v7x, 32 devices: a whole 2x2x4 slice. The times are simulated.
32 devices in a mesh: grp: 2 (over x), idx: 16 (over z, y, core).
Axes of the slice: x: 2, y: 2, z: 4, core: 2. Of those that a mesh axis runs over, the one named last changes fastest.
Arguments:
- queries: bfloat16 [4096, 1024], P(('grp', 'idx')), parts along dimension 0, may hold values from -6 to 6
- rotation: float32 [1024, 1024], replicated, may hold values from -0.1875 to 0.1875
- codes: bfloat16 [1024, 128, 256], P(('grp', 'idx')), parts along dimension 0, may hold values from -0.375 to 0.375
- vectors: float32 [1024, 128, 1024], P(('grp', 'idx')), parts along dimension 0, may hold values from -0.1875 to 0.1875
- probes: int32 [128, 16], P(('grp', 'idx')), parts along dimension 0, may hold values from 0 to 511, as said below
- cand_pages: int32 [4096, 8], P(('grp', 'idx')), parts along dimension 0, may hold values from 0 to 511, as said below
- cand_rows: int32 [4096, 8], P(('grp', 'idx')), parts along dimension 0, may hold values from 0 to 127
Outputs:
- coarse: bfloat16 [4096, 2048], P(('grp', 'idx')), parts along dimension 0
- rerank: float32 [4096, 8], P(('grp', 'idx')), parts along dimension 0
There are 2 independent parts, one for each index of `grp`. A program takes and returns all parts, laid end to end along the dimension named above; an argument that names none is the same for every part. Nothing has to cross between parts.
Inputs may be any that keep to these rules, and one draw needn't show every extreme that they name: Page j lies on index device j // 32. Among the probes of the 4 blocks of one index device, at most 8 name pages of any one index device, and the pages of one particular index device (the same one for all senders) receive exactly 8 probes from every index device. `cand_pages`: among the candidates of the 128 queries of one index device, at most 128 lie on pages of any one index device, and the pages of one particular index device (the same one for all senders) receive exactly 128 candidates from every index device.
All inputs are finite; a program needn't handle non-finite values.
Results may differ from a plain program's by a relative error of at most 0.0049.
Values may be sent and summed in bfloat16 or wider, within the bound.
No kernel may reach another device: no remote copies, remote signals or barrier semaphores. Data moves between devices by JAX's collectives and lax.ppermute only.
A program may use at most 128 MiB of HBM per device.

v0:
```python
import jax
import jax.numpy as jnp
from jax import lax
from jax.sharding import PartitionSpec as P


def slot_places(owners, shards, capacity):
    one_hot = (owners[:, None] == jnp.arange(shards, dtype=jnp.int32)[None, :]).astype(jnp.int32)
    slot_rank = jnp.sum((jnp.cumsum(one_hot, axis=0) - 1) * one_hot, axis=1)
    return owners * capacity + slot_rank


def body(queries, rotation, codes, vectors, probes, cand_pages, cand_rows):
    shards = lax.axis_size("idx")
    own_index = lax.axis_index("idx")
    query_rows, full_width = queries.shape
    page_count, page_rows, proj_width = codes.shape
    block_count, probe_count = probes.shape
    block_rows = query_rows // block_count
    cand_count = cand_pages.shape[1]
    slot_count = block_count * probe_count
    capacity = 2 * slot_count // shards
    row_slots = query_rows * cand_count
    row_capacity = 2 * row_slots // shards
    rotated = jnp.dot(
        queries.astype(jnp.float32),
        rotation,
        precision=lax.Precision.HIGHEST,
        preferred_element_type=jnp.float32,
    )
    projected = rotated[:, :proj_width].astype(jnp.bfloat16)
    query_block_rows = projected.reshape(block_count, block_rows, proj_width)
    flat_probes = probes.reshape(slot_count)
    probe_owner = flat_probes // page_count
    probe_place = slot_places(probe_owner, shards, capacity)
    every_block, every_probe = (
        lax.all_gather(query_block_rows, "idx", axis=0, tiled=True),
        lax.all_gather(probes, "idx", axis=0, tiled=True),
    )
    per_source = every_probe.reshape(shards, slot_count)
    locally_owned = per_source // page_count == own_index
    slot_rank = jnp.cumsum(locally_owned.astype(jnp.int32), axis=1) - 1
    target_column = jnp.where(locally_owned, slot_rank, capacity)
    source_ids = jnp.broadcast_to(
        jnp.arange(shards, dtype=jnp.int32)[:, None], (shards, slot_count)
    )
    slot_ids = jnp.broadcast_to(
        jnp.arange(slot_count, dtype=jnp.int32)[None, :], (shards, slot_count)
    )
    slot_table = (
        jnp.zeros((shards, capacity), jnp.int32)
        .at[source_ids, target_column]
        .set(slot_ids, mode="drop")
    )
    source_rows = (
        jnp.arange(shards, dtype=jnp.int32)[:, None] * block_count + slot_table // probe_count
    )
    held_queries = every_block[source_rows]
    page_local = jnp.take_along_axis(per_source, slot_table, axis=1) % page_count
    page_codes = codes[page_local]
    similarity_scores = jnp.einsum(
        "nkqd,nkrd->nkqr", held_queries, page_codes, preferred_element_type=jnp.float32
    )
    scored = similarity_scores.astype(jnp.bfloat16)
    returned = lax.all_to_all(scored, "idx", split_axis=0, concat_axis=0, tiled=True)
    selected_index = returned.reshape(shards * capacity, block_rows, page_rows)[probe_place]
    selected_index = selected_index.reshape(block_count, probe_count, block_rows, page_rows)
    coarse = selected_index.transpose(0, 2, 1, 3).reshape(query_rows, probe_count * page_rows)
    flat_pages = cand_pages.reshape(row_slots)
    row_owner = flat_pages // page_count
    row_local = flat_pages % page_count * page_rows + cand_rows.reshape(row_slots)
    row_place = slot_places(row_owner, shards, row_capacity)
    needed_row_flags = (
        jnp.zeros((shards * row_capacity,), jnp.int32)
        .at[row_place]
        .set(row_local)
        .reshape(shards, row_capacity)
    )
    flat_vectors = vectors.reshape(page_count * page_rows, full_width)
    row_asked = lax.all_to_all(needed_row_flags, "idx", split_axis=0, concat_axis=0, tiled=True)
    row_sent = flat_vectors[row_asked]
    row_got = lax.all_to_all(row_sent, "idx", split_axis=0, concat_axis=0, tiled=True)
    gathered = row_got.reshape(shards * row_capacity, full_width)[row_place].reshape(
        query_rows, cand_count, full_width
    )
    rerank = jnp.einsum("qd,qcd->qc", rotated, gathered, precision=lax.Precision.HIGHEST)
    return (coarse, rerank)


def solution(mesh):
    in_specs = (
        P(("grp", "idx"), None),
        P(),
        P(("grp", "idx"), None, None),
        P(("grp", "idx"), None, None),
        P(("grp", "idx"), None),
        P(("grp", "idx"), None),
        P(("grp", "idx"), None),
    )
    out_specs = (P(("grp", "idx"), None), P(("grp", "idx"), None))
    return jax.shard_map(body, mesh=mesh, in_specs=in_specs, out_specs=out_specs, check_vma=False)
```

profile of v0, /device:TPU:13, one launch (start us, length us, event | category | flops | bytes accessed | tf_op | source)
XLA Modules:
  0.0 322.3 jit_solution(11777183075623743349)
XLA Ops:
  7.3 4.0 %fusion.31 = f32[128,1024]{1,0:T(8,128)S(1)} fusion(bf16[128,1024]{1,0:T(8,128)(2,1)} %param.7, f32[1024,1024]{1,0:T(8,128)} %param.8), kind=kOutput, calls=%fused_computation.102 | convolution fusion | flops 1610612736 | bytes 4980736 | tf_op jit(solution)/shard_map/dot_general | solution.py:25
  11.3 0.6 slice.29
  11.9 0.1 copy.83
  12.2 0.1 reshape.450
  12.3 4.5 %reduce-window.6 = s32[16,8,128]{2,1,0:T(8,128)S(1)} reduce-window(s32[16,8,128]{2,1,0:T(8,128)S(1)} %fusion.5, s32[]{:T(128)} %constant.111.clone.1), window={size=1x1x128 pad=0_0x0_0x127_0}, to_apply=%region_4.5 | reduce-window | flops 2080768 | bytes 131076 | tf_op jit(solution)/shard_map/reduce-window
  16.9 0.1 copy.86
  17.3 0.1 copy.88
  17.6 4.9 %scatter_custom_fusion = s32[2048]{0:T(1024)} fusion(s32[1024]{0:T(1024)S(1)} %bitcast.94, s32[1024]{0:T(1024)S(1)} %get-tuple-element.4, s32[]{:T(128)} %constant.111.clone.1), kind=kCustom, calls=%fused_computation.79 | custom fusion | bytes 8196 | tf_op jit(solution)/shard_map/scatter | solution.py:76
  22.4 6.5 %all-to-all-start.1 = ((s32[16,1,128]{2,1,0:T(1,128)}), s32[16,1,128]{2,1,0:T(1,128)S(1)}, u32[]{:S(2)}, u32[]{:S(2)}) async-start(s32[16,1,128]{2,1,0:T(1,128)} %bitcast.17), calls=%async_computation.1 | async-start | bytes 16384 | tf_op jit(solution)/shard_map/all_to_all | solution.py:80
  29.0 15.3 %all-gather = s32[16,4,16]{2,1,0:T(4,128)S(1)} all-gather(s32[1,4,16]{2,1,0:T(4,128)S(1)} %bitcast.91), channel_id=1, replica_groups=mesh['grp'=2,'idx'=16] {'idx'}, dimensions={0}, use_global_device_ids=true | all-gather | bytes 4352 | tf_op jit(solution)/shard_map/all_gather | solution.py:38
  44.5 0.3 copy.73
  44.8 0.9 fusion.30
  45.7 1.3 copy.74
  47.2 0.1 copy.91
  47.6 4.3 %scatter_custom_fusion.1 = s32[128]{0:T(128)S(1)} fusion(s32[1024]{0:T(1024)S(1)} %reshape.515, s32[1024]{0:T(1024)S(1)} %reshape.517, s32[]{:T(128)} %constant.111.clone.1), kind=kCustom, calls=%fused_computation.98 | custom fusion | bytes 516
  52.2 1.3 gather_fusion.5
  54.0 6.7 %gather_fusion.1 = bf16[128,128,256]{2,1,0:T(8,128)(2,1)} fusion(bf16[32,128,256]{2,1,0:T(8,128)(2,1)S(1)} %copy-done, s32[1024]{0:T(1024)S(1)} %pad_clamp_fusion.1), kind=kCustom, calls=%fused_computation.1 | custom fusion | bytes 16777728 | tf_op jit(solution)/shard_map/gather | solution.py:60
  60.7 3.2 %gather_fusion = bf16[128,32,256]{2,1,0:T(8,128)(2,1)} fusion(bf16[64,32,256]{2,1,0:T(8,128)(2,1)} %all-gather.3.cloned.1.call-done, s32[1024]{0:T(1024)S(1)} %pad_clamp_fusion.2), kind=kCustom, calls=%fused_computation | custom fusion | bytes 4194816 | tf_op jit(solution)/shard_map/gather | solution.py:58
  63.9 8.0 %convolution_convert_fusion = bf16[16,8,32,128]{3,2,1,0:T(8,128)(2,1)} fusion(bf16[16,8,32,256]{3,2,1,0:T(8,128)(2,1)} %bitcast.83, bf16[16,8,128,256]{3,2,1,0:T(8,128)(2,1)} %bitcast.82), kind=kOutput, calls=%fused_computation.10 | convolution fusion | flops 268959744 | bytes 11534336 | tf_op jit(solution)/shard_map/nkqd,nkrd->nkqr/dot_general | solution.py:61
  71.9 10.8 %all-to-all-start = ((bf16[16,8,32,128]{3,2,1,0:T(8,128)(2,1)}), bf16[16,8,32,128]{3,2,1,0:T(8,128)(2,1)}, u32[]{:S(2)}, u32[]{:S(2)}) async-start(bf16[16,8,32,128]{3,2,1,0:T(8,128)(2,1)} %convolution_convert_fusion), calls=%async_computation | async-start | bytes 2097152 | tf_op jit(solution)/shard_map/all_to_all | solution.py:65
  82.7 17.6 %gather_fusion.3 = f32[2048,1024]{1,0:T(8,128)} fusion(f32[4096,1024]{1,0:T(8,128)} %bitcast.80, s32[2048]{0:T(1024)S(1)} %fusion.10), kind=kCustom, calls=%fused_computation.3 | custom fusion | bytes 16785408 | tf_op jit(solution)/shard_map/gather | solution.py:81
  100.2 7.4 %all-to-all-done = bf16[16,8,32,128]{3,2,1,0:T(8,128)(2,1)} async-done(((bf16[16,8,32,128]{3,2,1,0:T(8,128)(2,1)}), bf16[16,8,32,128]{3,2,1,0:T(8,128)(2,1)}, u32[]{:S(2)}, u32[]{:S(2)}) %all-to-all-start) | async-done | bytes 1048608 | tf_op jit(solution)/shard_map/all_to_all | solution.py:65
  107.7 4.9 %all-to-all-start.2 = ((f32[16,128,1024]{2,1,0:T(8,128)}), f32[16,128,1024]{2,1,0:T(8,128)}, u32[]{:S(2)}, u32[]{:S(2)}) async-start(f32[16,128,1024]{2,1,0:T(8,128)} %bitcast.81), calls=%async_computation.2 | async-start | bytes 16777216 | tf_op jit(solution)/shard_map/all_to_all | solution.py:82
  112.9 0.1 reduce_window_sum.36
  112.9 0.2 select_reduce_fusion
  113.2 1.9 gather_fusion.2
  115.1 0.2 copy.82
  115.3 0.9 copy.99
  116.2 178.7 %all-to-all-done.2 = f32[16,128,1024]{2,1,0:T(8,128)} async-done(((f32[16,128,1024]{2,1,0:T(8,128)}), f32[16,128,1024]{2,1,0:T(8,128)}, u32[]{:S(2)}, u32[]{:S(2)}) %all-to-all-start.2) | async-done | bytes 8388640 | tf_op jit(solution)/shard_map/all_to_all | solution.py:82
  294.9 9.8 %gather_fusion.4 = f32[1024,1024]{1,0:T(8,128)} fusion(f32[2048,1024]{1,0:T(8,128)} %bitcast.21, s32[1024]{0:T(1024)S(1)} %broadcast_clamp_fusion), kind=kCustom, calls=%fused_computation.4 | custom fusion | bytes 8392704 | tf_op jit(solution)/shard_map/gather | solution.py:83
  304.8 10.0 %fusion = f32[128,1,8]{2,1,0:T(1,128)S(1)} fusion(f32[1024,1024]{1,0:T(8,128)} %gather_fusion.4, f32[128,1024,1]{1,0,2:T(8,128)S(1)} %bitcast.84), kind=kOutput, calls=%fused_computation.8 | convolution fusion | flops 12582912 | bytes 4722688 | tf_op jit(solution)/shard_map/qd,qcd->qc/dot_general | solution.py:86
  314.8 0.7 copy.90
  (64 shorter events, 2.4 us)
Async XLA Ops:
  7.2 46.8 %copy-start = (bf16[32,128,256]{2,1,0:T(8,128)(2,1)S(1)}, bf16[32,128,256]{2,1,0:T(8,128)(2,1)}, u32[]{:S(2)}) copy-start(bf16[32,128,256]{2,1,0:T(8,128)(2,1)} %param.9) | copy-start | bytes 6291460
  7.2 39.8 %copy-start.5 = (s32[2]{0:T(128)S(1)}, s32[2]{0:T(128)}, u32[]{:S(2)}) copy-start(s32[2]{0:T(128)} %constant.127) | copy-start | bytes 28
  7.2 40.0 %copy-start.4 = (s32[2]{0:T(128)S(1)}, s32[2]{0:T(128)}, u32[]{:S(2)}) copy-start(s32[2]{0:T(128)} %constant.130) | copy-start | bytes 28
  7.2 4.7 %copy-start.2 = (s32[128,8]{0,1:T(8,128)S(1)}, s32[128,8]{0,1:T(8,128)}, u32[]{:S(2)}) copy-start(s32[128,8]{0,1:T(8,128)} %param.12) | copy-start | bytes 12292
  7.2 10.1 %copy-start.3 = (s32[128,8]{0,1:T(8,128)S(1)}, s32[128,8]{0,1:T(8,128)}, u32[]{:S(2)}) copy-start(s32[128,8]{0,1:T(8,128)} %param.13) | copy-start | bytes 12292
  7.2 21.8 %copy-start.1 = (s32[4,16]{1,0:T(4,128)S(1)}, s32[4,16]{1,0:T(4,128)}, u32[]{:S(2)}) copy-start(s32[4,16]{1,0:T(4,128)} %param.11) | copy-start | bytes 772
  7.2 53.4 %all-gather.3.cloned.1.call-start = ((), (), s32[]{:S(2)}) async-start(), calls=%async_computation.3 | async-start | bytes 1114112 | tf_op jit(solution)/shard_map/all_gather | solution.py:37
  22.4 49.4 %all-to-all-start.1 = ((s32[16,1,128]{2,1,0:T(1,128)}), s32[16,1,128]{2,1,0:T(1,128)S(1)}, u32[]{:S(2)}, u32[]{:S(2)}) async-start(s32[16,1,128]{2,1,0:T(1,128)} %bitcast.17), calls=%async_computation.1 | async-start | bytes 16384 | tf_op jit(solution)/shard_map/all_to_all | solution.py:80
  71.9 35.8 %all-to-all-start = ((bf16[16,8,32,128]{3,2,1,0:T(8,128)(2,1)}), bf16[16,8,32,128]{3,2,1,0:T(8,128)(2,1)}, u32[]{:S(2)}, u32[]{:S(2)}) async-start(bf16[16,8,32,128]{3,2,1,0:T(8,128)(2,1)} %convolution_convert_fusion), calls=%async_computation | async-start | bytes 2097152 | tf_op jit(solution)/shard_map/all_to_all | solution.py:65
  107.7 187.3 %all-to-all-start.2 = ((f32[16,128,1024]{2,1,0:T(8,128)}), f32[16,128,1024]{2,1,0:T(8,128)}, u32[]{:S(2)}, u32[]{:S(2)}) async-start(f32[16,128,1024]{2,1,0:T(8,128)} %bitcast.81), calls=%async_computation.2 | async-start | bytes 16777216 | tf_op jit(solution)/shard_map/all_to_all | solution.py:82
Sparse Core Ops, SparseCore 0:
  12.0 38.2 all-gather.2
where the time goes:
time: 323 us; the launch traced here: 322 us
  waiting for transfers between devices  186 us (58%)
  local copies, waits for them, and re-layouts  56 us (17%)
  starting transfers between devices  22.3 us (7%)
  matrix products  22 us (7%)
  blocking collectives  15.3 us (5%)
  between operations  14.3 us (4%)
  other arithmetic  6.21 us (2%)
    all_to_all x1, waiting for transfers between devices, body(): lax.all_to_all(row_sent, 'idx', split_axis=0, concat_axis=0, tiled=True)  179 us
    gather x1, local copies, waits for them, and re-layouts, body(): row_sent = flat_vectors[row_asked]  17.6 us
    all_gather x1, blocking collectives, body(): lax.all_gather(probes, 'idx', axis=0, tiled=True)  15.3 us
    all_to_all x1, starting transfers between devices, body(): lax.all_to_all(scored, 'idx', split_axis=0, concat_axis=0, tiled=True)  10.8 us
    dot_general x1, matrix products, body(): jnp.einsum('qd,qcd->qc', rotated, gathered, precision=lax.Precision.HIGHEST)  10 us
    gather x1, local copies, waits for them, and re-layouts, body(): row_got.reshape(shards * row_capacity, full_width)[row_place]  9.82 us
    dot_general x1, matrix products, body(): jnp.einsum('nkqd,nkrd->nkqr', held_queries, page_codes, preferred_element...  7.98 us
    all_to_all x1, waiting for transfers between devices, body(): lax.all_to_all(scored, 'idx', split_axis=0, concat_axis=0, tiled=True)  7.44 us
  transfers between devices with their start and end apart: 4, of which 2 were waited for; matrix products, arithmetic and copies ran while one was open for 18% of the time, Pallas kernels for 0%

commit v1 on v0

v1 whole, which is shorter than its diff:
```python
import functools

import jax
import jax.numpy as jnp
from jax import lax
from jax.experimental import pallas as pl
from jax.experimental.pallas import tpu as pltpu
from jax.sharding import PartitionSpec as P

LANES = 128
MIB = 1 << 20
F32, BF16, I32 = jnp.float32, jnp.bfloat16, jnp.int32
VMEM, SMEM, HBM = pltpu.VMEM, pltpu.SMEM, pl.ANY


def iota(shape, axis):
    return lax.broadcasted_iota(I32, shape, axis)


def dot(a, b, over_a=1, over_b=0):
    return lax.dot_general(a, b, (((over_a,), (over_b,)), ((), ())), preferred_element_type=F32)


def params(limit, **more):
    return pltpu.CompilerParams(vmem_limit_bytes=limit, **more)


def whole(space):
    return pl.BlockSpec(memory_space=space)


def thirds(x):
    high = x.astype(BF16)
    rest = x - high.astype(F32)
    middle = rest.astype(BF16)
    return high, middle, (rest - middle.astype(F32)).astype(BF16)


def rotate(queries, rotation):
    high, middle, low = thirds(rotation)
    return dot(queries, low) + dot(queries, middle) + dot(queries, high)


def owner_hot(owner, shards):
    cands = owner.shape[1]
    lanes = cands * shards
    spread = (iota((cands, lanes), 1) // shards == iota((cands, lanes), 0)).astype(BF16)
    wide = dot(owner.astype(BF16), spread)
    return (wide == (iota(wide.shape, 1) % shards).astype(F32)).astype(BF16), spread


def ranks(owner, shards):
    hot, spread = owner_hot(owner, shards)
    rows, lanes = hot.shape
    before = (iota((rows, rows), 1) < iota((rows, rows), 0)).astype(BF16)
    above = dot(before, hot)
    total = jnp.sum(hot.astype(F32), axis=0, keepdims=True)
    r, c = iota((lanes, lanes), 0), iota((lanes, lanes), 1)
    earlier = ((r % shards == c % shards) & (r // shards < c // shards)).astype(BF16)
    base = dot(jnp.broadcast_to(total, (8, lanes)).astype(BF16), earlier)[:1]
    rank = dot((hot.astype(F32) * (above + base)).astype(BF16), spread, 1, 1)
    return rank.astype(I32)


def plan_kernel(shards, page_count, q_ref, rot_ref, probes_ref, pages_ref, rows_ref, chunk_ref, probe_ref, place_ref):
    rows, cands = pages_ref.shape
    blocks, probes = probes_ref.shape
    chunk_ref[:rows, :] = rotate(q_ref[...], rot_ref[...]).astype(BF16)

    pages = pages_ref[...]
    owner = pages // page_count
    rank = ranks(owner, shards)
    place_ref[...] = jnp.concatenate([owner, rank], axis=1)
    local = (pages % page_count).astype(F32)
    line = rows_ref[...].astype(F32)

    lane = iota((rows, LANES), 1)
    kind, who = lane // shards, lane % shards
    query = iota((rows, LANES), 0).astype(F32)
    left, right = [], []
    for c in range(cands):
        value = jnp.where(kind == 0, query, jnp.where(kind == 1, local[:, c : c + 1], jnp.where(kind == 2, line[:, c : c + 1], 0.0)))
        left.append(jnp.where(owner[:, c : c + 1] == who, value, 0.0))
        right.append((rank[:, c : c + 1] == lane).astype(F32))
    table = dot(jnp.concatenate(left, 0).astype(BF16), jnp.concatenate(right, 0).astype(BF16), 0, 0)

    probe_pages = probes_ref[...]
    probe_owner = probe_pages // page_count
    probe_rank = ranks(probe_owner, shards)
    capacity = 2 * blocks * probes // shards
    probe_ref[...] = probe_owner * capacity + probe_rank
    value = (probe_pages % page_count + iota(probe_pages.shape, 0) * page_count).astype(F32)
    lane = iota((blocks, LANES), 1)
    kind, who = lane // shards, lane % shards
    left, right = [], []
    for c in range(probes):
        left.append(jnp.where((probe_owner[:, c : c + 1] == who) & (kind == 3), value[:, c : c + 1], 0.0))
        right.append((probe_rank[:, c : c + 1] == lane).astype(F32))
    table += dot(jnp.concatenate(left, 0).astype(BF16), jnp.concatenate(right, 0).astype(BF16), 0, 0)
    table = table.astype(BF16)
    chunk_ref[rows:, :LANES] = table[: 2 * shards]
    chunk_ref[rows:, LANES : 2 * LANES] = table[2 * shards : 4 * shards]


def rotate_kernel(q_ref, rot_ref, out_ref):
    out_ref[...] = rotate(q_ref[...], rot_ref[...]).astype(BF16)


def coarse_kernel(shards, capacity, block_rows, me_ref, *refs):
    pieces = refs[:shards]
    codes_ref, score_ref, line_ref, query_ref, slot_vec, slot_ref, sem = refs[shards:]
    page_count, page_rows, _ = codes_ref.shape
    me = me_ref[0]
    rows = pieces[0].shape[0] - 2 * shards
    mine = iota((shards, 1), 0) == me
    for m, piece in enumerate(pieces):
        first = jnp.sum(jnp.where(mine, piece[rows : rows + shards, :].astype(F32), 0.0), axis=0, keepdims=True).astype(I32)
        second = jnp.sum(jnp.where(mine, piece[rows + shards :, :].astype(F32), 0.0), axis=0, keepdims=True).astype(I32)
        query_ref[m : m + 1, :] = first[:, :LANES]
        line_ref[m : m + 1, :] = second[:, :LANES] * page_rows + first[:, LANES : 2 * LANES]
        slot_vec[m : m + 1, :] = second[:, LANES : 2 * LANES]
    copy = pltpu.make_async_copy(slot_vec, slot_ref, sem)
    copy.start()
    copy.wait()
    for m, piece in enumerate(pieces):
        source = me ^ m
        for s in range(capacity):
            slot = slot_ref[m, s]
            start = pl.multiple_of(slot // page_count * block_rows, block_rows)
            held = piece[pl.ds(start, block_rows), :]
            score_ref[source, s] = dot(held, codes_ref[slot % page_count], 1, 1).astype(BF16)


def gather_kernel(unroll, index_ref, vectors_ref, out_ref, sem):
    count = out_ref.shape[0]

    def issue(i, carry):
        for k in range(unroll):
            j = i * unroll + k
            row = index_ref[j // LANES, j % LANES]
            pltpu.make_async_copy(vectors_ref.at[pl.ds(row, 1)], out_ref.at[pl.ds(j, 1)], sem).start()
        return carry

    lax.fori_loop(0, count // unroll, issue, 0)
    pltpu.make_async_copy(vectors_ref.at[pl.ds(0, count)], out_ref, sem).wait()


def rerank_kernel(shards, capacity, me_ref, query_ref, rows_ref, *refs):
    heads, tails = refs[:shards], refs[shards : 2 * shards]
    out_ref, held, sems = refs[2 * shards :]
    me = me_ref[0]
    queries, split = tails[0].shape[0], heads[0].shape[1]
    copies = [
        pltpu.make_async_copy(rows_ref.at[pl.ds(m * capacity, capacity)], held.at[pl.ds(m * capacity, capacity)], sems.at[m])
        for m in range(shards)
    ]
    for copy in copies:
        copy.start()
    for m in range(shards):
        copies[m].wait()
        rows = held[m * capacity : (m + 1) * capacity, :]
        high = rows.astype(BF16)
        low = (rows - high.astype(F32)).astype(BF16)
        head, tail = heads[m][:queries, :], tails[m][...]
        score = dot(head, high[:, :split], 1, 1) + dot(tail, high[:, split:], 1, 1)
        score += dot(head, low[:, :split], 1, 1) + dot(tail, low[:, split:], 1, 1)
        picked = iota(score.shape, 0) == query_ref[m : m + 1, :capacity]
        out_ref[pl.ds(me ^ m, 1), :] = jnp.sum(jnp.where(picked, score, 0.0), axis=0, keepdims=True)


def pick_kernel(got_ref, place_ref, out_ref):
    shards, capacity = got_ref.shape
    rows, cands = out_ref.shape
    owner, rank = place_ref[:, :cands], place_ref[:, cands:]
    hot = jnp.concatenate(
        [(owner[:, c : c + 1] == iota((rows, shards), 1)).astype(F32) for c in range(cands)], axis=0
    ).astype(BF16)
    high, middle, low = thirds(got_ref[...])
    lines = dot(hot, low) + dot(hot, middle) + dot(hot, high)
    result = jnp.zeros((rows, cands), F32)
    for c in range(cands):
        here = jnp.where(rank[:, c : c + 1] == iota((rows, capacity), 1), lines[c * rows : (c + 1) * rows], 0.0)
        result = jnp.where(iota((rows, cands), 1) == c, jnp.sum(here, axis=1, keepdims=True), result)
    out_ref[...] = result


def place_kernel(place_ref, got_ref, out_ref):
    blocks, probes = place_ref.shape
    _, block_rows, page_rows = got_ref.shape
    for b in range(blocks):
        for p in range(probes):
            out_ref[b * block_rows : (b + 1) * block_rows, p * page_rows : (p + 1) * page_rows] = got_ref[place_ref[b, p]]


def exchange(x, mask, shards):
    return lax.ppermute(x, "idx", [(i, i ^ mask) for i in range(shards)])


def gather_all(x, shards):
    pieces = {0: x}
    for mask in range(4, shards, 4):
        pieces[mask] = exchange(x, mask, shards)
    for mask in range(0, shards, 4):
        pieces[mask ^ 2] = exchange(pieces[mask], 2, shards)
    for mask in range(0, shards, 2):
        pieces[mask ^ 1] = exchange(pieces[mask], 1, shards)
    return [pieces[m] for m in range(shards)]


def body(queries, rotation, codes, vectors, probes, cand_pages, cand_rows):
    shards = lax.axis_size("idx")
    me = lax.axis_index("idx").astype(I32).reshape(1)
    query_rows, full_width = queries.shape
    page_count, page_rows, proj_width = codes.shape
    block_count, probe_count = probes.shape
    block_rows = query_rows // block_count
    cand_count = cand_pages.shape[1]
    slot_count = block_count * probe_count
    capacity = 2 * slot_count // shards
    row_capacity = 2 * query_rows * cand_count // shards
    rest = full_width - proj_width
    assert proj_width == 2 * LANES and rest % proj_width == 0 and row_capacity <= LANES
    assert 4 * shards <= LANES and block_count * page_count <= 256 and query_rows <= 256 and page_rows <= 256

    chunk_rows = query_rows + 2 * shards
    chunk, probe_place, cand_place = pl.pallas_call(
        functools.partial(plan_kernel, shards, page_count),
        grid=(1,),
        in_specs=[
            pl.BlockSpec((query_rows, full_width), lambda i: (0, 0)),
            pl.BlockSpec((full_width, proj_width), lambda i: (0, 0)),
            pl.BlockSpec((block_count, probe_count), lambda i: (0, 0)),
            pl.BlockSpec((query_rows, cand_count), lambda i: (0, 0)),
            pl.BlockSpec((query_rows, cand_count), lambda i: (0, 0)),
        ],
        out_specs=[
            pl.BlockSpec((chunk_rows, proj_width), lambda i: (0, 0)),
            pl.BlockSpec((block_count, probe_count), lambda i: (0, 0)),
            pl.BlockSpec((query_rows, 2 * cand_count), lambda i: (0, 0)),
        ],
        out_shape=[
            jax.ShapeDtypeStruct((chunk_rows, proj_width), BF16),
            jax.ShapeDtypeStruct((block_count, probe_count), I32),
            jax.ShapeDtypeStruct((query_rows, 2 * cand_count), I32),
        ],
        compiler_params=params(32 * MIB),
        name="plan",
    )(queries, rotation, probes, cand_pages, cand_rows)
    tail = pl.pallas_call(
        rotate_kernel,
        grid=(rest // proj_width,),
        in_specs=[
            pl.BlockSpec((query_rows, full_width), lambda i: (0, 0)),
            pl.BlockSpec((full_width, proj_width), lambda i: (0, i + 1)),
        ],
        out_specs=pl.BlockSpec((query_rows, proj_width), lambda i: (0, i)),
        out_shape=jax.ShapeDtypeStruct((query_rows, rest), BF16),
        compiler_params=params(32 * MIB),
        name="rotate_rest",
    )(queries, rotation)

    heads = gather_all(chunk, shards)
    tails = gather_all(tail, shards)

    scored, lines, wanted = pl.pallas_call(
        functools.partial(coarse_kernel, shards, capacity, block_rows),
        in_specs=[whole(SMEM)] + [whole(VMEM)] * (shards + 1),
        out_specs=[whole(VMEM)] * 3,
        out_shape=[
            jax.ShapeDtypeStruct((shards, capacity, block_rows, page_rows), BF16),
            jax.ShapeDtypeStruct((shards, LANES), I32),
            jax.ShapeDtypeStruct((shards, LANES), I32),
        ],
        scratch_shapes=[pltpu.VMEM((shards, LANES), I32), pltpu.SMEM((shards, LANES), I32), pltpu.SemaphoreType.DMA],
        compiler_params=params(32 * MIB),
        name="coarse_scores",
    )(me, *heads, codes)
    returned = lax.all_to_all(scored, "idx", split_axis=0, concat_axis=0, tiled=True)

    flat = vectors.reshape(page_count * page_rows, full_width)
    line_list = lines[:, :row_capacity].reshape(-1, LANES)
    found = pl.pallas_call(
        functools.partial(gather_kernel, 16),
        in_specs=[whole(SMEM), whole(HBM)],
        out_specs=whole(HBM),
        out_shape=jax.ShapeDtypeStruct((shards * row_capacity, full_width), F32),
        scratch_shapes=[pltpu.SemaphoreType.DMA],
        compiler_params=params(32 * MIB),
        name="gather_rows",
    )(line_list, flat)

    answers = pl.pallas_call(
        functools.partial(rerank_kernel, shards, row_capacity),
        in_specs=[whole(SMEM), whole(VMEM), whole(HBM)] + [whole(VMEM)] * (2 * shards),
        out_specs=whole(VMEM),
        out_shape=jax.ShapeDtypeStruct((shards, row_capacity), F32),
        scratch_shapes=[pltpu.VMEM((shards * row_capacity, full_width), F32), pltpu.SemaphoreType.DMA((shards,))],
        compiler_params=params(48 * MIB),
        name="rerank_scores",
    )(me, wanted, found, *heads, *tails)
    answered = lax.all_to_all(answers, "idx", split_axis=0, concat_axis=0, tiled=True)

    rerank = pl.pallas_call(
        pick_kernel,
        in_specs=[whole(VMEM), whole(VMEM)],
        out_specs=whole(VMEM),
        out_shape=jax.ShapeDtypeStruct((query_rows, cand_count), F32),
        compiler_params=params(32 * MIB),
        name="pick_answers",
    )(answered, cand_place)
    coarse = pl.pallas_call(
        place_kernel,
        in_specs=[whole(SMEM), whole(VMEM)],
        out_specs=whole(VMEM),
        out_shape=jax.ShapeDtypeStruct((query_rows, probe_count * page_rows), BF16),
        compiler_params=params(32 * MIB),
        name="place_scores",
    )(probe_place, returned.reshape(shards * capacity, block_rows, page_rows))
    return coarse, rerank


def solution(mesh):
    split = P(("grp", "idx"))
    in_specs = (split, P(), split, split, split, split, split)
    return jax.shard_map(body, mesh=mesh, in_specs=in_specs, out_specs=(split, split), check_vma=False)
```

time: 323 us -> 163 us (0.50)
  the two profiles are of different devices: /device:TPU:13 before, /device:TPU:0 now
where the time goes in v1:
time: 163 us; the launch traced here: 161 us
  Pallas kernels  61.7 us (38%)
  waiting for transfers between devices  44.7 us (27%)
  starting transfers between devices  26.8 us (16%)
  local copies, waits for them, and re-layouts  14.9 us (9%)
  blocking collectives  12.3 us (8%)
    pallas_call x1, Pallas kernels, body(): pl.pallas_call(functools.partial(gather_kernel, 16), in_specs=[whole(SMEM...  42.1 us
    ppermute x30, waiting for transfers between devices, exchange(): return lax.ppermute(x, 'idx', [(i, i ^ mask) for i in range(shards)])  23.5 us
    ppermute x30, starting transfers between devices, exchange(): return lax.ppermute(x, 'idx', [(i, i ^ mask) for i in range(shards)])  23.1 us
    all_to_all x1, waiting for transfers between devices, body(): lax.all_to_all(scored, 'idx', split_axis=0, concat_axis=0, tiled=True)  21.2 us
    unnamed x43, local copies, waits for them, and re-layouts  14.9 us
    all_to_all x1, blocking collectives, body(): lax.all_to_all(answers, 'idx', split_axis=0, concat_axis=0, tiled=True)  12.3 us
    pallas_call x1, Pallas kernels, body(): pl.pallas_call(functools.partial(rerank_kernel, shards, row_capacity), in...  9.65 us
    pallas_call x1, Pallas kernels, body(): pl.pallas_call(functools.partial(coarse_kernel, shards, capacity, block_r...  4.55 us
  transfers between devices with their start and end apart: 31, of which 9 were waited for; matrix products, arithmetic and copies ran while one was open for 0% of the time, Pallas kernels for 31%

profile of v1, /device:TPU:0, one launch (start us, length us, event | category | flops | bytes accessed | tf_op | source)
XLA Modules:
  0.0 161.4 jit_solution(457082773746951889)
XLA Ops:
  0.6 0.8 copy.12.pages_ref
  1.4 0.8 copy.13.rows_ref
  2.2 2.2 %copy-done.1 = f32[1024,1024]{1,0:T(8,128)S(1)} copy-done((f32[1024,1024]{1,0:T(8,128)S(1)}, f32[1024,1024]{1,0:T(8,128)}, u32[]{:S(2)}) %copy-start.1) | copy-done | bytes 4194328
  4.4 0.9 copy-done.3
  6.0 1.3 plan.1
  7.9 5.0 %collective-permute-start.11 = (bf16[160,256]{1,0:T(8,128)(2,1)S(1)}, bf16[160,256]{1,0:T(8,128)(2,1)S(1)}, u32[]{:S(2)}, u32[]{:S(2)}) collective-permute-start(bf16[160,256]{1,0:T(8,128)(2,1)S(1)} %get-tuple-element.9.refs_0_), channel_id=1, source_target_pairs={{0,12},{1,13},{2,14},{3,15},{4,8},{5,9},{6,10},{7,11},{8,4},{9,5},... | collective-permute-start | bytes 245768 | tf_op jit(solution)/shard_map/ppermute | solution.py:196
  13.6 1.7 %collective-permute-start.1 = (bf16[160,256]{1,0:T(8,128)(2,1)S(1)}, bf16[160,256]{1,0:T(8,128)(2,1)S(1)}, u32[]{:S(2)}, u32[]{:S(2)}) collective-permute-start(bf16[160,256]{1,0:T(8,128)(2,1)S(1)} %get-tuple-element.9.refs_0_), channel_id=1, source_target_pairs={{0,2},{1,3},{2,0},{3,1},{4,6},{5,7},{6,4},{7,5},{8,10},{9,11},{10,... | collective-permute-start | bytes 245768 | tf_op jit(solution)/shard_map/ppermute | solution.py:196
  16.0 1.8 %collective-permute-start.13 = (bf16[160,256]{1,0:T(8,128)(2,1)S(1)}, bf16[160,256]{1,0:T(8,128)(2,1)S(1)}, u32[]{:S(2)}, u32[]{:S(2)}) collective-permute-start(bf16[160,256]{1,0:T(8,128)(2,1)S(1)} %collective-permute-done.11.refs_12_), channel_id=1, source_target_pairs={{0,2},{1,3},{2,0},{3,1},{4,6},{5,7},{6,4},{7,5},{8,10},{9,11},{10,... | collective-permute-start | bytes 245768 | tf_op jit(solution)/shard_map/ppermute | solution.py:196
  17.8 2.1 %collective-permute-done.7.refs_8_ = bf16[160,256]{1,0:T(8,128)(2,1)S(1)} collective-permute-done((bf16[160,256]{1,0:T(8,128)(2,1)S(1)}, bf16[160,256]{1,0:T(8,128)(2,1)S(1)}, u32[]{:S(2)}, u32[]{:S(2)}) %collective-permute-start.7) | collective-permute-done | bytes 81952 | tf_op jit(solution)/shard_map/ppermute | solution.py:196
  19.9 1.5 collective-permute-start.9
  22.1 1.7 %rotate_rest.1.refs_16_ = bf16[128,768]{1,0:T(8,128)(2,1)S(1)} custom-call(bf16[128,1024]{1,0:T(8,128)(2,1)S(1)} %copy-done.3, f32[1024,1024]{1,0:T(8,128)S(1)} %copy-done.1), custom_call_target="tpu_custom_call" | custom-call | tf_op jit(solution)/shard_map/rotate_rest/pallas_call | solution.py:249
  24.9 2.6 %collective-permute-start.26 = (bf16[128,768]{1,0:T(8,128)(2,1)S(1)}, bf16[128,768]{1,0:T(8,128)(2,1)S(1)}, u32[]{:S(2)}, u32[]{:S(2)}) collective-permute-start(bf16[128,768]{1,0:T(8,128)(2,1)S(1)} %rotate_rest.1.refs_16_), channel_id=1, source_target_pairs={{0,12},{1,13},{2,14},{3,15},{4,8},{5,9},{6,10},{7,11},{8,4},{9,5},... | collective-permute-start | bytes 589832 | tf_op jit(solution)/shard_map/ppermute | solution.py:196
  27.6 1.8 %collective-permute-start.18 = (bf16[128,768]{1,0:T(8,128)(2,1)S(1)}, bf16[128,768]{1,0:T(8,128)(2,1)}, u32[]{:S(2)}, u32[]{:S(2)}) collective-permute-start(bf16[128,768]{1,0:T(8,128)(2,1)S(1)} %rotate_rest.1.refs_16_), channel_id=1, source_target_pairs={{0,4},{1,5},{2,6},{3,7},{4,0},{5,1},{6,2},{7,3},{8,12},{9,13},{10,... | collective-permute-start | bytes 589832 | tf_op jit(solution)/shard_map/ppermute | solution.py:196
  29.3 1.7 %collective-permute-start.16 = (bf16[128,768]{1,0:T(8,128)(2,1)S(1)}, bf16[128,768]{1,0:T(8,128)(2,1)}, u32[]{:S(2)}, u32[]{:S(2)}) collective-permute-start(bf16[128,768]{1,0:T(8,128)(2,1)S(1)} %rotate_rest.1.refs_16_), channel_id=1, source_target_pairs={{0,2},{1,3},{2,0},{3,1},{4,6},{5,7},{6,4},{7,5},{8,10},{9,11},{10,... | collective-permute-start | bytes 589832 | tf_op jit(solution)/shard_map/ppermute | solution.py:196
  31.0 3.6 %collective-permute-done.26.refs_28_ = bf16[128,768]{1,0:T(8,128)(2,1)S(1)} collective-permute-done((bf16[128,768]{1,0:T(8,128)(2,1)S(1)}, bf16[128,768]{1,0:T(8,128)(2,1)S(1)}, u32[]{:S(2)}, u32[]{:S(2)}) %collective-permute-start.26) | collective-permute-done | bytes 196640 | tf_op jit(solution)/shard_map/ppermute | solution.py:196
  34.7 9.7 %collective-permute-done.22.refs_24_ = bf16[128,768]{1,0:T(8,128)(2,1)S(1)} collective-permute-done((bf16[128,768]{1,0:T(8,128)(2,1)S(1)}, bf16[128,768]{1,0:T(8,128)(2,1)S(1)}, u32[]{:S(2)}, u32[]{:S(2)}) %collective-permute-start.22) | collective-permute-done | bytes 196640 | tf_op jit(solution)/shard_map/ppermute | solution.py:196
  44.9 1.3 collective-permute-start.28
  47.6 0.7 collective-permute-start.24
  49.8 1.3 collective-permute-start.20
  51.2 1.6 %collective-permute-done.28.refs_30_ = bf16[128,768]{1,0:T(8,128)(2,1)} collective-permute-done((bf16[128,768]{1,0:T(8,128)(2,1)S(1)}, bf16[128,768]{1,0:T(8,128)(2,1)}, u32[]{:S(2)}, u32[]{:S(2)}) %collective-permute-start.28) | collective-permute-done | bytes 196640 | tf_op jit(solution)/shard_map/ppermute | solution.py:196
  54.0 3.0 %collective-permute-done.24.refs_26_ = bf16[128,768]{1,0:T(8,128)(2,1)} collective-permute-done((bf16[128,768]{1,0:T(8,128)(2,1)S(1)}, bf16[128,768]{1,0:T(8,128)(2,1)}, u32[]{:S(2)}, u32[]{:S(2)}) %collective-permute-start.24) | collective-permute-done | bytes 196640 | tf_op jit(solution)/shard_map/ppermute | solution.py:196
  58.2 2.1 %collective-permute-done.20.refs_22_ = bf16[128,768]{1,0:T(8,128)(2,1)} collective-permute-done((bf16[128,768]{1,0:T(8,128)(2,1)}, bf16[128,768]{1,0:T(8,128)(2,1)}, u32[]{:S(2)}, u32[]{:S(2)}) %collective-permute-start.20) | collective-permute-done | bytes 196640 | tf_op jit(solution)/shard_map/ppermute | solution.py:196
  60.3 0.9 copy-done.5
  61.2 4.5 %coarse_scores.1 = (bf16[16,8,32,128]{3,2,1,0:T(8,128)(2,1)}, s32[16,128]{1,0:T(8,128)S(1)}, s32[16,128]{1,0:T(8,128)S(1)}) custom-call(s32[1]{0:T(128)} %bitcast.me_ref, bf16[160,256]{1,0:T(8,128)(2,1)S(1)} %get-tuple-element.9.refs_0_, bf16[160,256]{1,0:T(8,128)(2,1)S(1)} %collective-permute-done.refs_1_, ...), custom_call_target="tpu_custom_call" | custom-call | tf_op jit(solution)/shard_map/coarse_scores/pallas_call | solution.py:265
  65.8 42.1 %gather_rows.1.rows_ref = f32[2048,1024]{1,0:T(8,128)S(1)} custom-call(s32[16,128]{1,0:T(8,128)S(1)} %get-tuple-element.12.index_ref, f32[4096,1024]{1,0:T(8,128)} %bitcast.10), custom_call_target="tpu_custom_call" | custom-call | tf_op jit(solution)/shard_map/gather_rows/pallas_call | solution.py:282
  108.0 3.3 %copy-done = f32[2048,1024]{1,0:T(8,128)} copy-done((f32[2048,1024]{1,0:T(8,128)}, f32[2048,1024]{1,0:T(8,128)S(1)}, u32[]{:S(2)}) %copy-start) | copy-done | bytes 8388632
  111.4 9.7 %rerank_scores.1 = f32[16,128]{1,0:T(8,128)S(1)} custom-call(s32[1]{0:T(128)} %bitcast.me_ref, s32[16,128]{1,0:T(8,128)S(1)} %get-tuple-element.11.query_ref, f32[2048,1024]{1,0:T(8,128)} %copy-done, bf16[160,256]{1,0:T(8,128)(2,1)S(1)} %get-tuple-element.9.refs_0_, bf16[160,256]{1,0:T(8,128)(2,1)S(1)} %collective-permute-done.refs_1_, ...), custom_call_target="tpu_custom_call" | custom-call | tf_op jit(solution)/shard_map/rerank_scores/pallas_call | solution.py:292
  121.0 12.3 %all_to_all.16 = f32[16,1,128]{2,1,0:T(1,128)S(1)} all-to-all(f32[16,1,128]{2,1,0:T(1,128)S(1)} %bitcast.8), channel_id=1, replica_groups=mesh['grp'=2,'idx'=16] {'idx'}, dimensions={0} | all-to-all | bytes 16384 | tf_op jit(solution)/shard_map/all_to_all | solution.py:301
  133.3 3.7 %all-to-all-start = ((bf16[16,8,32,128]{3,2,1,0:T(8,128)(2,1)}), bf16[16,8,32,128]{3,2,1,0:T(8,128)(2,1)S(1)}, u32[]{:S(2)}, u32[]{:S(2)}) async-start(bf16[16,8,32,128]{3,2,1,0:T(8,128)(2,1)} %get-tuple-element.10), calls=%async_computation | async-start | bytes 2097152 | tf_op jit(solution)/shard_map/all_to_all | solution.py:278
  137.0 1.0 pick_answers.1
  138.7 21.2 %all-to-all-done = bf16[16,8,32,128]{3,2,1,0:T(8,128)(2,1)S(1)} async-done(((bf16[16,8,32,128]{3,2,1,0:T(8,128)(2,1)}), bf16[16,8,32,128]{3,2,1,0:T(8,128)(2,1)S(1)}, u32[]{:S(2)}, u32[]{:S(2)}) %all-to-all-start) | async-done | bytes 1048608 | tf_op jit(solution)/shard_map/all_to_all | solution.py:278
  159.9 1.5 place_scores.1
  (81 shorter events, 10.9 us)
Async XLA Ops:
  6.0 54.3 %copy-start.2 = (bf16[32,128,256]{2,1,0:T(8,128)(2,1)S(1)}, bf16[32,128,256]{2,1,0:T(8,128)(2,1)}, u32[]{:S(2)}) copy-start(bf16[32,128,256]{2,1,0:T(8,128)(2,1)} %refs_16_.1) | copy-start | bytes 6291460
  7.9 8.1 %collective-permute-start.11 = (bf16[160,256]{1,0:T(8,128)(2,1)S(1)}, bf16[160,256]{1,0:T(8,128)(2,1)S(1)}, u32[]{:S(2)}, u32[]{:S(2)}) collective-permute-start(bf16[160,256]{1,0:T(8,128)(2,1)S(1)} %get-tuple-element.9.refs_0_), channel_id=1, source_target_pairs={{0,12},{1,13},{2,14},{3,15},{4,8},{5,9},{6,10},{7,11},{8,4},{9,5},... | collective-permute-start | bytes 245768 | tf_op jit(solution)/shard_map/ppermute | solution.py:196
  13.0 6.9 %collective-permute-start.7 = (bf16[160,256]{1,0:T(8,128)(2,1)S(1)}, bf16[160,256]{1,0:T(8,128)(2,1)S(1)}, u32[]{:S(2)}, u32[]{:S(2)}) collective-permute-start(bf16[160,256]{1,0:T(8,128)(2,1)S(1)} %get-tuple-element.9.refs_0_), channel_id=1, source_target_pairs={{0,8},{1,9},{2,10},{3,11},{4,12},{5,13},{6,14},{7,15},{8,0},{9,1},... | collective-permute-start | bytes 245768 | tf_op jit(solution)/shard_map/ppermute | solution.py:196
  13.0 6.9 %collective-permute-start.3 = (bf16[160,256]{1,0:T(8,128)(2,1)S(1)}, bf16[160,256]{1,0:T(8,128)(2,1)S(1)}, u32[]{:S(2)}, u32[]{:S(2)}) collective-permute-start(bf16[160,256]{1,0:T(8,128)(2,1)S(1)} %get-tuple-element.9.refs_0_), channel_id=1, source_target_pairs={{0,4},{1,5},{2,6},{3,7},{4,0},{5,1},{6,2},{7,3},{8,12},{9,13},{10,... | collective-permute-start | bytes 245768 | tf_op jit(solution)/shard_map/ppermute | solution.py:196
  13.6 7.8 %collective-permute-start.1 = (bf16[160,256]{1,0:T(8,128)(2,1)S(1)}, bf16[160,256]{1,0:T(8,128)(2,1)S(1)}, u32[]{:S(2)}, u32[]{:S(2)}) collective-permute-start(bf16[160,256]{1,0:T(8,128)(2,1)S(1)} %get-tuple-element.9.refs_0_), channel_id=1, source_target_pairs={{0,2},{1,3},{2,0},{3,1},{4,6},{5,7},{6,4},{7,5},{8,10},{9,11},{10,... | collective-permute-start | bytes 245768 | tf_op jit(solution)/shard_map/ppermute | solution.py:196
  15.3 6.3 %collective-permute-start = (bf16[160,256]{1,0:T(8,128)(2,1)S(1)}, bf16[160,256]{1,0:T(8,128)(2,1)S(1)}, u32[]{:S(2)}, u32[]{:S(2)}) collective-permute-start(bf16[160,256]{1,0:T(8,128)(2,1)S(1)} %get-tuple-element.9.refs_0_), channel_id=1, source_target_pairs={{0,1},{1,0},{2,3},{3,2},{4,5},{5,4},{6,7},{7,6},{8,9},{9,8},{10,11... | collective-permute-start | bytes 245768 | tf_op jit(solution)/shard_map/ppermute | solution.py:196
  16.0 7.8 %collective-permute-start.13 = (bf16[160,256]{1,0:T(8,128)(2,1)S(1)}, bf16[160,256]{1,0:T(8,128)(2,1)S(1)}, u32[]{:S(2)}, u32[]{:S(2)}) collective-permute-start(bf16[160,256]{1,0:T(8,128)(2,1)S(1)} %collective-permute-done.11.refs_12_), channel_id=1, source_target_pairs={{0,2},{1,3},{2,0},{3,1},{4,6},{5,7},{6,4},{7,5},{8,10},{9,11},{10,... | collective-permute-start | bytes 245768 | tf_op jit(solution)/shard_map/ppermute | solution.py:196
  19.9 4.1 %collective-permute-start.12 = (bf16[160,256]{1,0:T(8,128)(2,1)S(1)}, bf16[160,256]{1,0:T(8,128)(2,1)S(1)}, u32[]{:S(2)}, u32[]{:S(2)}) collective-permute-start(bf16[160,256]{1,0:T(8,128)(2,1)S(1)} %collective-permute-done.11.refs_12_), channel_id=1, source_target_pairs={{0,1},{1,0},{2,3},{3,2},{4,5},{5,4},{6,7},{7,6},{8,9},{9,8},{10,11... | collective-permute-start | bytes 245768 | tf_op jit(solution)/shard_map/ppermute | solution.py:196
  19.9 5.1 %collective-permute-start.9 = (bf16[160,256]{1,0:T(8,128)(2,1)S(1)}, bf16[160,256]{1,0:T(8,128)(2,1)S(1)}, u32[]{:S(2)}, u32[]{:S(2)}) collective-permute-start(bf16[160,256]{1,0:T(8,128)(2,1)S(1)} %collective-permute-done.7.refs_8_), channel_id=1, source_target_pairs={{0,2},{1,3},{2,0},{3,1},{4,6},{5,7},{6,4},{7,5},{8,10},{9,11},{10,... | collective-permute-start | bytes 245768 | tf_op jit(solution)/shard_map/ppermute | solution.py:196
  21.4 6.2 %collective-permute-start.8 = (bf16[160,256]{1,0:T(8,128)(2,1)S(1)}, bf16[160,256]{1,0:T(8,128)(2,1)S(1)}, u32[]{:S(2)}, u32[]{:S(2)}) collective-permute-start(bf16[160,256]{1,0:T(8,128)(2,1)S(1)} %collective-permute-done.7.refs_8_), channel_id=1, source_target_pairs={{0,1},{1,0},{2,3},{3,2},{4,5},{5,4},{6,7},{7,6},{8,9},{9,8},{10,11... | collective-permute-start | bytes 245768 | tf_op jit(solution)/shard_map/ppermute | solution.py:196
  21.6 5.9 %collective-permute-start.5 = (bf16[160,256]{1,0:T(8,128)(2,1)S(1)}, bf16[160,256]{1,0:T(8,128)(2,1)S(1)}, u32[]{:S(2)}, u32[]{:S(2)}) collective-permute-start(bf16[160,256]{1,0:T(8,128)(2,1)S(1)} %collective-permute-done.3.refs_4_), channel_id=1, source_target_pairs={{0,2},{1,3},{2,0},{3,1},{4,6},{5,7},{6,4},{7,5},{8,10},{9,11},{10,... | collective-permute-start | bytes 245768 | tf_op jit(solution)/shard_map/ppermute | solution.py:196
  23.8 5.5 %collective-permute-start.4 = (bf16[160,256]{1,0:T(8,128)(2,1)S(1)}, bf16[160,256]{1,0:T(8,128)(2,1)S(1)}, u32[]{:S(2)}, u32[]{:S(2)}) collective-permute-start(bf16[160,256]{1,0:T(8,128)(2,1)S(1)} %collective-permute-done.3.refs_4_), channel_id=1, source_target_pairs={{0,1},{1,0},{2,3},{3,2},{4,5},{5,4},{6,7},{7,6},{8,9},{9,8},{10,11... | collective-permute-start | bytes 245768 | tf_op jit(solution)/shard_map/ppermute | solution.py:196
  23.9 7.1 %collective-permute-start.2 = (bf16[160,256]{1,0:T(8,128)(2,1)S(1)}, bf16[160,256]{1,0:T(8,128)(2,1)S(1)}, u32[]{:S(2)}, u32[]{:S(2)}) collective-permute-start(bf16[160,256]{1,0:T(8,128)(2,1)S(1)} %collective-permute-done.1.refs_2_), channel_id=1, source_target_pairs={{0,1},{1,0},{2,3},{3,2},{4,5},{5,4},{6,7},{7,6},{8,9},{9,8},{10,11... | collective-permute-start | bytes 245768 | tf_op jit(solution)/shard_map/ppermute | solution.py:196
  24.9 9.7 %collective-permute-start.26 = (bf16[128,768]{1,0:T(8,128)(2,1)S(1)}, bf16[128,768]{1,0:T(8,128)(2,1)S(1)}, u32[]{:S(2)}, u32[]{:S(2)}) collective-permute-start(bf16[128,768]{1,0:T(8,128)(2,1)S(1)} %rotate_rest.1.refs_16_), channel_id=1, source_target_pairs={{0,12},{1,13},{2,14},{3,15},{4,8},{5,9},{6,10},{7,11},{8,4},{9,5},... | collective-permute-start | bytes 589832 | tf_op jit(solution)/shard_map/ppermute | solution.py:196
  27.6 16.8 %collective-permute-start.22 = (bf16[128,768]{1,0:T(8,128)(2,1)S(1)}, bf16[128,768]{1,0:T(8,128)(2,1)S(1)}, u32[]{:S(2)}, u32[]{:S(2)}) collective-permute-start(bf16[128,768]{1,0:T(8,128)(2,1)S(1)} %rotate_rest.1.refs_16_), channel_id=1, source_target_pairs={{0,8},{1,9},{2,10},{3,11},{4,12},{5,13},{6,14},{7,15},{8,0},{9,1},... | collective-permute-start | bytes 589832 | tf_op jit(solution)/shard_map/ppermute | solution.py:196
  27.6 16.8 %collective-permute-start.18 = (bf16[128,768]{1,0:T(8,128)(2,1)S(1)}, bf16[128,768]{1,0:T(8,128)(2,1)}, u32[]{:S(2)}, u32[]{:S(2)}) collective-permute-start(bf16[128,768]{1,0:T(8,128)(2,1)S(1)} %rotate_rest.1.refs_16_), channel_id=1, source_target_pairs={{0,4},{1,5},{2,6},{3,7},{4,0},{5,1},{6,2},{7,3},{8,12},{9,13},{10,... | collective-permute-start | bytes 589832 | tf_op jit(solution)/shard_map/ppermute | solution.py:196
  29.3 15.6 %collective-permute-start.16 = (bf16[128,768]{1,0:T(8,128)(2,1)S(1)}, bf16[128,768]{1,0:T(8,128)(2,1)}, u32[]{:S(2)}, u32[]{:S(2)}) collective-permute-start(bf16[128,768]{1,0:T(8,128)(2,1)S(1)} %rotate_rest.1.refs_16_), channel_id=1, source_target_pairs={{0,2},{1,3},{2,0},{3,1},{4,6},{5,7},{6,4},{7,5},{8,10},{9,11},{10,... | collective-permute-start | bytes 589832 | tf_op jit(solution)/shard_map/ppermute | solution.py:196
  31.0 15.2 %collective-permute-start.15 = (bf16[128,768]{1,0:T(8,128)(2,1)S(1)}, bf16[128,768]{1,0:T(8,128)(2,1)S(1)}, u32[]{:S(2)}, u32[]{:S(2)}) collective-permute-start(bf16[128,768]{1,0:T(8,128)(2,1)S(1)} %rotate_rest.1.refs_16_), channel_id=1, source_target_pairs={{0,1},{1,0},{2,3},{3,2},{4,5},{5,4},{6,7},{7,6},{8,9},{9,8},{10,11... | collective-permute-start | bytes 589832 | tf_op jit(solution)/shard_map/ppermute | solution.py:196
  34.7 12.9 %collective-permute-start.14 = (bf16[160,256]{1,0:T(8,128)(2,1)S(1)}, bf16[160,256]{1,0:T(8,128)(2,1)S(1)}, u32[]{:S(2)}, u32[]{:S(2)}) collective-permute-start(bf16[160,256]{1,0:T(8,128)(2,1)S(1)} %collective-permute-done.13.refs_14_), channel_id=1, source_target_pairs={{0,1},{1,0},{2,3},{3,2},{4,5},{5,4},{6,7},{7,6},{8,9},{9,8},{10,11... | collective-permute-start | bytes 245768 | tf_op jit(solution)/shard_map/ppermute | solution.py:196
  44.4 3.9 %collective-permute-start.10 = (bf16[160,256]{1,0:T(8,128)(2,1)S(1)}, bf16[160,256]{1,0:T(8,128)(2,1)S(1)}, u32[]{:S(2)}, u32[]{:S(2)}) collective-permute-start(bf16[160,256]{1,0:T(8,128)(2,1)S(1)} %collective-permute-done.9.refs_10_), channel_id=1, source_target_pairs={{0,1},{1,0},{2,3},{3,2},{4,5},{5,4},{6,7},{7,6},{8,9},{9,8},{10,11... | collective-permute-start | bytes 245768 | tf_op jit(solution)/shard_map/ppermute | solution.py:196
  44.4 4.8 %collective-permute-start.6 = (bf16[160,256]{1,0:T(8,128)(2,1)S(1)}, bf16[160,256]{1,0:T(8,128)(2,1)S(1)}, u32[]{:S(2)}, u32[]{:S(2)}) collective-permute-start(bf16[160,256]{1,0:T(8,128)(2,1)S(1)} %collective-permute-done.5.refs_6_), channel_id=1, source_target_pairs={{0,1},{1,0},{2,3},{3,2},{4,5},{5,4},{6,7},{7,6},{8,9},{9,8},{10,11... | collective-permute-start | bytes 245768 | tf_op jit(solution)/shard_map/ppermute | solution.py:196
  44.9 7.9 %collective-permute-start.28 = (bf16[128,768]{1,0:T(8,128)(2,1)S(1)}, bf16[128,768]{1,0:T(8,128)(2,1)}, u32[]{:S(2)}, u32[]{:S(2)}) collective-permute-start(bf16[128,768]{1,0:T(8,128)(2,1)S(1)} %collective-permute-done.26.refs_28_), channel_id=1, source_target_pairs={{0,2},{1,3},{2,0},{3,1},{4,6},{5,7},{6,4},{7,5},{8,10},{9,11},{10,... | collective-permute-start | bytes 589832 | tf_op jit(solution)/shard_map/ppermute | solution.py:196
  46.9 5.9 %collective-permute-start.27 = (bf16[128,768]{1,0:T(8,128)(2,1)S(1)}, bf16[128,768]{1,0:T(8,128)(2,1)S(1)}, u32[]{:S(2)}, u32[]{:S(2)}) collective-permute-start(bf16[128,768]{1,0:T(8,128)(2,1)S(1)} %collective-permute-done.26.refs_28_), channel_id=1, source_target_pairs={{0,1},{1,0},{2,3},{3,2},{4,5},{5,4},{6,7},{7,6},{8,9},{9,8},{10,11... | collective-permute-start | bytes 589832 | tf_op jit(solution)/shard_map/ppermute | solution.py:196
  47.6 9.4 %collective-permute-start.24 = (bf16[128,768]{1,0:T(8,128)(2,1)S(1)}, bf16[128,768]{1,0:T(8,128)(2,1)}, u32[]{:S(2)}, u32[]{:S(2)}) collective-permute-start(bf16[128,768]{1,0:T(8,128)(2,1)S(1)} %collective-permute-done.22.refs_24_), channel_id=1, source_target_pairs={{0,2},{1,3},{2,0},{3,1},{4,6},{5,7},{6,4},{7,5},{8,10},{9,11},{10,... | collective-permute-start | bytes 589832 | tf_op jit(solution)/shard_map/ppermute | solution.py:196
  48.3 8.7 %collective-permute-start.23 = (bf16[128,768]{1,0:T(8,128)(2,1)S(1)}, bf16[128,768]{1,0:T(8,128)(2,1)S(1)}, u32[]{:S(2)}, u32[]{:S(2)}) collective-permute-start(bf16[128,768]{1,0:T(8,128)(2,1)S(1)} %collective-permute-done.22.refs_24_), channel_id=1, source_target_pairs={{0,1},{1,0},{2,3},{3,2},{4,5},{5,4},{6,7},{7,6},{8,9},{9,8},{10,11... | collective-permute-start | bytes 589832 | tf_op jit(solution)/shard_map/ppermute | solution.py:196
  49.8 10.5 %collective-permute-start.20 = (bf16[128,768]{1,0:T(8,128)(2,1)}, bf16[128,768]{1,0:T(8,128)(2,1)}, u32[]{:S(2)}, u32[]{:S(2)}) collective-permute-start(bf16[128,768]{1,0:T(8,128)(2,1)} %collective-permute-done.18.refs_20_), channel_id=1, source_target_pairs={{0,2},{1,3},{2,0},{3,1},{4,6},{5,7},{6,4},{7,5},{8,10},{9,11},{10,... | collective-permute-start | bytes 589832 | tf_op jit(solution)/shard_map/ppermute | solution.py:196
  52.8 58.5 %collective-permute-start.19 = (bf16[128,768]{1,0:T(8,128)(2,1)}, bf16[128,768]{1,0:T(8,128)(2,1)}, u32[]{:S(2)}, u32[]{:S(2)}) collective-permute-start(bf16[128,768]{1,0:T(8,128)(2,1)} %collective-permute-done.18.refs_20_), channel_id=1, source_target_pairs={{0,1},{1,0},{2,3},{3,2},{4,5},{5,4},{6,7},{7,6},{8,9},{9,8},{10,11... | collective-permute-start | bytes 589832 | tf_op jit(solution)/shard_map/ppermute | solution.py:196
  53.5 57.8 %collective-permute-start.17 = (bf16[128,768]{1,0:T(8,128)(2,1)}, bf16[128,768]{1,0:T(8,128)(2,1)}, u32[]{:S(2)}, u32[]{:S(2)}) collective-permute-start(bf16[128,768]{1,0:T(8,128)(2,1)} %collective-permute-done.16.refs_18_), channel_id=1, source_target_pairs={{0,1},{1,0},{2,3},{3,2},{4,5},{5,4},{6,7},{7,6},{8,9},{9,8},{10,11... | collective-permute-start | bytes 589832 | tf_op jit(solution)/shard_map/ppermute | solution.py:196
  57.0 54.3 %collective-permute-start.29 = (bf16[128,768]{1,0:T(8,128)(2,1)}, bf16[128,768]{1,0:T(8,128)(2,1)}, u32[]{:S(2)}, u32[]{:S(2)}) collective-permute-start(bf16[128,768]{1,0:T(8,128)(2,1)} %collective-permute-done.28.refs_30_), channel_id=1, source_target_pairs={{0,1},{1,0},{2,3},{3,2},{4,5},{5,4},{6,7},{7,6},{8,9},{9,8},{10,11... | collective-permute-start | bytes 589832 | tf_op jit(solution)/shard_map/ppermute | solution.py:196
  57.7 53.6 %collective-permute-start.25 = (bf16[128,768]{1,0:T(8,128)(2,1)}, bf16[128,768]{1,0:T(8,128)(2,1)}, u32[]{:S(2)}, u32[]{:S(2)}) collective-permute-start(bf16[128,768]{1,0:T(8,128)(2,1)} %collective-permute-done.24.refs_26_), channel_id=1, source_target_pairs={{0,1},{1,0},{2,3},{3,2},{4,5},{5,4},{6,7},{7,6},{8,9},{9,8},{10,11... | collective-permute-start | bytes 589832 | tf_op jit(solution)/shard_map/ppermute | solution.py:196
  60.3 51.0 %collective-permute-start.21 = (bf16[128,768]{1,0:T(8,128)(2,1)}, bf16[128,768]{1,0:T(8,128)(2,1)}, u32[]{:S(2)}, u32[]{:S(2)}) collective-permute-start(bf16[128,768]{1,0:T(8,128)(2,1)} %collective-permute-done.20.refs_22_), channel_id=1, source_target_pairs={{0,1},{1,0},{2,3},{3,2},{4,5},{5,4},{6,7},{7,6},{8,9},{9,8},{10,11... | collective-permute-start | bytes 589832 | tf_op jit(solution)/shard_map/ppermute | solution.py:196
  133.3 26.6 %all-to-all-start = ((bf16[16,8,32,128]{3,2,1,0:T(8,128)(2,1)}), bf16[16,8,32,128]{3,2,1,0:T(8,128)(2,1)S(1)}, u32[]{:S(2)}, u32[]{:S(2)}) async-start(bf16[16,8,32,128]{3,2,1,0:T(8,128)(2,1)} %get-tuple-element.10), calls=%async_computation | async-start | bytes 2097152 | tf_op jit(solution)/shard_map/all_to_all | solution.py:278
  (19 other events, 311.6 us)

commit v2 on v1

v2 whole, which is shorter than its diff:
```python
import functools

import jax
import jax.numpy as jnp
from jax import lax
from jax.experimental import pallas as pl
from jax.experimental.pallas import tpu as pltpu
from jax.sharding import PartitionSpec as P

LANES = 128
MIB = 1 << 20
F32, BF16, I32 = jnp.float32, jnp.bfloat16, jnp.int32
VMEM, SMEM, HBM = pltpu.VMEM, pltpu.SMEM, pl.ANY


def iota(shape, axis):
    return lax.broadcasted_iota(I32, shape, axis)


def dot(a, b, over_a=1, over_b=0):
    return lax.dot_general(a, b, (((over_a,), (over_b,)), ((), ())), preferred_element_type=F32)


def params(limit, **more):
    return pltpu.CompilerParams(vmem_limit_bytes=limit, **more)


def whole(space):
    return pl.BlockSpec(memory_space=space)


def cost(us):
    return pl.CostEstimate(flops=0, bytes_accessed=us * 3_000_000, transcendentals=0)


def thirds(x):
    high = x.astype(BF16)
    rest = x - high.astype(F32)
    middle = rest.astype(BF16)
    return high, middle, (rest - middle.astype(F32)).astype(BF16)


def rotate(queries, rotation):
    high, middle, low = thirds(rotation)
    return dot(queries, low) + dot(queries, middle) + dot(queries, high)


def ranks(owner, shards):
    rows, lanes = owner.shape
    tall = rows * shards
    spread = (iota((tall, rows), 0) // shards == iota((tall, rows), 1)).astype(BF16)
    hot = (dot(spread, owner.astype(BF16)) == (iota((tall, lanes), 0) % shards).astype(F32)).astype(BF16)
    before = (iota((lanes, lanes), 0) < iota((lanes, lanes), 1)).astype(BF16)
    r, c = iota((tall, tall), 0), iota((tall, tall), 1)
    earlier = ((r % shards == c % shards) & (c // shards < r // shards)).astype(BF16)
    count = dot(hot, before) + jnp.sum(dot(earlier, hot), axis=1, keepdims=True)
    return dot(spread, (hot.astype(F32) * count).astype(BF16), 0, 0).astype(I32)


def table_part(owner, rank, values, shards, kinds):
    rows, lanes = owner.shape
    line = iota((LANES, lanes), 0)
    kind, who = line // shards, line % shards
    left, right = [], []
    for c in range(rows):
        value = jnp.zeros((LANES, lanes), F32)
        for k, v in zip(kinds, values, strict=True):
            value = jnp.where(kind == k, v[c : c + 1], value)
        left.append(jnp.where(owner[c : c + 1] == who, value, 0.0))
        right.append((rank[c : c + 1] == line).astype(F32))
    total = jnp.zeros((LANES, LANES), F32)
    if lanes % LANES == 0:
        return dot(jnp.concatenate(left, 1).astype(BF16), jnp.concatenate(right, 1).astype(BF16), 1, 1)
    for l, r in zip(left, right, strict=True):
        total += dot(l.astype(BF16), r.astype(BF16), 1, 1)
    return total


def plan_kernel(shards, page_count, q_ref, rot_ref, probes_ref, pages_ref, rows_ref, chunk_ref, probe_ref, place_ref, held, sem):
    cands, rows = pages_ref.shape
    blocks, probes = probes_ref.shape
    copy = pltpu.make_async_copy(rot_ref.at[:, pl.ds(0, held.shape[1])], held, sem)
    copy.start()
    pages = pages_ref[...]
    owner = pages // page_count
    rank = ranks(owner, shards)
    place_ref[:cands] = owner
    place_ref[cands:] = rank
    query = iota((cands, rows), 1).astype(F32)
    values = (query, (pages % page_count).astype(F32), rows_ref[...].astype(F32))
    table = table_part(owner, rank, values, shards, (0, 1, 2))

    probe_pages = probes_ref[...]
    probe_owner = probe_pages // page_count
    probe_rank = ranks(probe_owner, shards)
    probe_ref[...] = probe_owner * (2 * blocks * probes // shards) + probe_rank
    value = (probe_pages % page_count + iota(probe_pages.shape, 0) * page_count).astype(F32)
    table += table_part(probe_owner, probe_rank, (value,), shards, (3,))
    table = table.astype(BF16)
    chunk_ref[rows:, :LANES] = table[: 2 * shards]
    chunk_ref[rows:, LANES : 2 * LANES] = table[2 * shards : 4 * shards]
    copy.wait()
    chunk_ref[:rows, :] = rotate(q_ref[...], held[...]).astype(BF16)


def rotate_kernel(q_ref, rot_ref, out_ref):
    out_ref[...] = rotate(q_ref[...], rot_ref[...]).astype(BF16)


def coarse_kernel(shards, capacity, block_rows, me_ref, *refs):
    parts = refs[:shards]
    codes_ref, score_ref, line_ref, query_ref, held, slot_vec, slot_ref, sems, sem = refs[shards:]
    page_count, page_rows, _ = codes_ref.shape
    me = me_ref[0]
    rows = held.shape[1] - 2 * shards
    loads = [pltpu.make_async_copy(part, held.at[m], sems.at[m]) for m, part in enumerate(parts)]
    for load in loads:
        load.start()
    mine = iota((shards, 1), 0) == me
    for m in range(shards):
        loads[m].wait()
        first = jnp.sum(jnp.where(mine, held[m, rows : rows + shards, :].astype(F32), 0.0), axis=0, keepdims=True).astype(I32)
        second = jnp.sum(jnp.where(mine, held[m, rows + shards :, :].astype(F32), 0.0), axis=0, keepdims=True).astype(I32)
        line = second[:, :LANES] * page_rows + first[:, LANES : 2 * LANES]
        query_ref[m : m + 1, :] = first[:, :LANES]
        line_ref[m : m + 1, :] = line
        slot_vec[m : m + 1, :] = second[:, LANES : 2 * LANES]
    copy = pltpu.make_async_copy(slot_vec, slot_ref, sem)
    copy.start()
    copy.wait()
    for m in range(shards):
        source = me ^ m
        for s in range(capacity):
            slot = slot_ref[m, s]
            start = pl.multiple_of(slot // page_count * block_rows, block_rows)
            score_ref[source, s] = dot(held[m, pl.ds(start, block_rows), :], codes_ref[slot % page_count], 1, 1).astype(BF16)


def gather_kernel(shards, capacity, index_ref, lines_ref, out_ref, lines, picked, sems, out_sem):
    tiles = out_ref.shape[2] // LANES
    parts = sems.shape[0]
    size = lines.shape[0] // parts
    loads = [
        pltpu.make_async_copy(lines_ref.at[pl.ds(i * size, size)], lines.at[pl.ds(i * size, size)], sems.at[i])
        for i in range(parts)
    ]
    for load in loads:
        load.start()
    for load in loads:
        load.wait()

    @pl.loop(0, shards)
    def _(m):
        for j in range(capacity):
            row = index_ref[m, j]
            start = (row // 8) * (8 * tiles) + row % 8
            picked[pl.ds(j // 8 * 8 * tiles + j % 8, tiles, stride=8), :] = lines[pl.ds(start, tiles, stride=8), :]
        for k in range(tiles):
            for g in range(0, capacity, 16):
                pair = [picked[(g + h) * tiles + k * 8 : (g + h) * tiles + k * 8 + 8, :] for h in (0, 8)]
                part = jnp.concatenate(pair, axis=0)
                high = part.astype(BF16)
                out_ref[m, g : g + 16, k * LANES : (k + 1) * LANES] = high
                low = (part - high.astype(F32)).astype(BF16)
                out_ref[m, capacity + g : capacity + g + 16, k * LANES : (k + 1) * LANES] = low


def rerank_kernel(shards, capacity, me_ref, query_ref, rows_ref, *refs):
    heads, tails = refs[:shards], refs[shards : 2 * shards]
    outs = refs[2 * shards : 2 * shards + shards // 4]
    rows, head, tail, sems = refs[2 * shards + shards // 4 :]
    queries, split = head.shape[1:]
    copies = [
        (
            pltpu.make_async_copy(rows_ref.at[m], rows.at[m], sems.at[m, 0]),
            pltpu.make_async_copy(heads[m].at[pl.ds(0, queries)], head.at[m], sems.at[m, 1]),
            pltpu.make_async_copy(tails[m], tail.at[m], sems.at[m, 2]),
        )
        for m in range(shards)
    ]
    for trio in copies:
        for copy in trio:
            copy.start()
    for m in range(shards):
        for copy in copies[m]:
            copy.wait()
        score = dot(head[m], rows[m, :, :split], 1, 1) + dot(tail[m], rows[m, :, split:], 1, 1)
        score = score[:, :capacity] + score[:, capacity:]
        picked = iota(score.shape, 0) == query_ref[m : m + 1, :capacity]
        outs[m // 4][m % 4 : m % 4 + 1, :] = jnp.sum(jnp.where(picked, score, 0.0), axis=0, keepdims=True)


def pick_kernel(shards, me_ref, own_ref, y_ref, core_ref, both_ref, place_ref, out_ref, got):
    cands, rows = out_ref.shape
    capacity = got.shape[1]
    for a in range(shards // 4):
        for low, ref in enumerate((own_ref, core_ref, y_ref, both_ref)):
            got[4 * a + low : 4 * a + low + 1, :] = ref[a, low : low + 1, :]
    piece, rank = place_ref[:cands] ^ me_ref[0], place_ref[cands:]
    hot = [(piece[c : c + 1] == iota((shards, rows), 0)).astype(F32) for c in range(cands)]
    hot = jnp.concatenate(hot, axis=1).astype(BF16)
    high, middle, low = thirds(got[...])
    lines = dot(low, hot, 0, 0) + dot(middle, hot, 0, 0) + dot(high, hot, 0, 0)
    for c in range(cands):
        here = rank[c : c + 1] == iota((capacity, rows), 0)
        out_ref[c : c + 1, :] = jnp.sum(jnp.where(here, lines[:, c * rows : (c + 1) * rows], 0.0), axis=0, keepdims=True)


def place_kernel(place_ref, got_ref, out_ref):
    blocks, probes = place_ref.shape
    _, block_rows, page_rows = got_ref.shape
    for b in range(blocks):
        for p in range(probes):
            out_ref[b * block_rows : (b + 1) * block_rows, p * page_rows : (p + 1) * page_rows] = got_ref[place_ref[b, p]]


def exchange(x, mask, shards):
    return lax.ppermute(x, "idx", [(i, i ^ mask) for i in range(shards)])


def gather_all(x, shards):
    pieces = {0: x}
    for mask in range(4, shards, 4):
        pieces[mask] = exchange(x, mask, shards)
    for mask in range(0, shards, 4):
        pieces[mask ^ 2] = exchange(pieces[mask], 2, shards)
    for mask in range(0, shards, 2):
        pieces[mask ^ 1] = exchange(pieces[mask], 1, shards)
    return [pieces[m] for m in range(shards)]


def body(queries, rotation, codes, vectors, probes, cand_pages, cand_rows):
    shards = lax.axis_size("idx")
    me = lax.axis_index("idx").astype(I32).reshape(1)
    query_rows, full_width = queries.shape
    page_count, page_rows, proj_width = codes.shape
    block_count, probe_count = probes.shape
    block_rows = query_rows // block_count
    cand_count = cand_pages.shape[1]
    slot_count = block_count * probe_count
    capacity = 2 * slot_count // shards
    row_capacity = 2 * query_rows * cand_count // shards
    rest = full_width - proj_width
    assert proj_width == 2 * LANES and rest % proj_width == 0 and row_capacity <= LANES
    assert 4 * shards <= LANES and block_count * page_count <= 256 and query_rows <= 256 and page_rows <= 256

    chunk_rows = query_rows + 2 * shards
    chunk, probe_place, cand_place = pl.pallas_call(
        functools.partial(plan_kernel, shards, page_count),
        in_specs=[whole(VMEM), whole(HBM), whole(VMEM), whole(VMEM), whole(VMEM)],
        out_specs=[whole(VMEM)] * 3,
        out_shape=[
            jax.ShapeDtypeStruct((chunk_rows, proj_width), BF16),
            jax.ShapeDtypeStruct((block_count, probe_count), I32),
            jax.ShapeDtypeStruct((2 * cand_count, query_rows), I32),
        ],
        scratch_shapes=[pltpu.VMEM((full_width, proj_width), F32), pltpu.SemaphoreType.DMA],
        compiler_params=params(32 * MIB),
        cost_estimate=cost(2),
        name="plan",
    )(queries, rotation, probes, cand_pages.T, cand_rows.T)
    tail = pl.pallas_call(
        rotate_kernel,
        grid=(rest // proj_width,),
        in_specs=[
            pl.BlockSpec((query_rows, full_width), lambda i: (0, 0)),
            pl.BlockSpec((full_width, proj_width), lambda i: (0, i + 1)),
        ],
        out_specs=pl.BlockSpec((query_rows, proj_width), lambda i: (0, i)),
        out_shape=jax.ShapeDtypeStruct((query_rows, rest), BF16),
        compiler_params=params(32 * MIB),
        cost_estimate=cost(2),
        name="rotate_rest",
    )(queries, rotation)

    heads = gather_all(chunk, shards)
    tails = gather_all(tail, shards)

    scored, lines, wanted = pl.pallas_call(
        functools.partial(coarse_kernel, shards, capacity, block_rows),
        in_specs=[whole(SMEM)] + [whole(HBM)] * shards + [whole(VMEM)],
        out_specs=[whole(VMEM)] * 3,
        out_shape=[
            jax.ShapeDtypeStruct((shards, capacity, block_rows, page_rows), BF16),
            jax.ShapeDtypeStruct((shards, LANES), I32),
            jax.ShapeDtypeStruct((shards, LANES), I32),
        ],
        scratch_shapes=[
            pltpu.VMEM((shards, chunk_rows, proj_width), BF16),
            pltpu.VMEM((shards, LANES), I32),
            pltpu.SMEM((shards, LANES), I32),
            pltpu.SemaphoreType.DMA((shards,)),
            pltpu.SemaphoreType.DMA,
        ],
        compiler_params=params(32 * MIB),
        cost_estimate=cost(6),
        name="coarse_scores",
    )(me, *heads, codes)
    returned = lax.all_to_all(scored, "idx", split_axis=0, concat_axis=0, tiled=True)

    tiles = full_width // LANES
    flat = vectors.reshape(page_count * page_rows // 8, 8, tiles, LANES).transpose(0, 2, 1, 3).reshape(-1, LANES)
    found = pl.pallas_call(
        functools.partial(gather_kernel, shards, row_capacity),
        in_specs=[whole(SMEM), whole(HBM)],
        out_specs=whole(VMEM),
        out_shape=jax.ShapeDtypeStruct((shards, 2 * row_capacity, full_width), BF16),
        scratch_shapes=[
            pltpu.VMEM(flat.shape, F32),
            pltpu.VMEM((row_capacity * tiles, LANES), F32),
            pltpu.SemaphoreType.DMA((4,)),
            pltpu.SemaphoreType.DMA,
        ],
        compiler_params=params(48 * MIB),
        cost_estimate=cost(15),
        name="gather_rows",
    )(lines, flat)

    answers = pl.pallas_call(
        functools.partial(rerank_kernel, shards, row_capacity),
        in_specs=[whole(SMEM), whole(VMEM), whole(HBM)] + [whole(HBM)] * (2 * shards),
        out_specs=[whole(VMEM)] * (shards // 4),
        out_shape=[jax.ShapeDtypeStruct((4, row_capacity), F32)] * (shards // 4),
        scratch_shapes=[
            pltpu.VMEM((shards, 2 * row_capacity, full_width), BF16),
            pltpu.VMEM((shards, query_rows, proj_width), BF16),
            pltpu.VMEM((shards, query_rows, rest), BF16),
            pltpu.SemaphoreType.DMA((shards, 3)),
        ],
        compiler_params=params(48 * MIB),
        cost_estimate=cost(8),
        name="rerank_scores",
    )(me, wanted, found, *heads, *tails)
    own = jnp.stack([answers[0]] + [exchange(answers[a], 4 * a, shards) for a in range(1, shards // 4)])
    across = exchange(own, 2, shards)
    rerank = pl.pallas_call(
        functools.partial(pick_kernel, shards),
        in_specs=[whole(SMEM)] + [whole(VMEM)] * 5,
        out_specs=whole(VMEM),
        out_shape=jax.ShapeDtypeStruct((cand_count, query_rows), F32),
        scratch_shapes=[pltpu.VMEM((shards, row_capacity), F32)],
        compiler_params=params(32 * MIB),
        cost_estimate=cost(1),
        name="pick_answers",
    )(me, own, across, exchange(own, 1, shards), exchange(across, 1, shards), cand_place).T
    coarse = pl.pallas_call(
        place_kernel,
        in_specs=[whole(SMEM), whole(VMEM)],
        out_specs=whole(VMEM),
        out_shape=jax.ShapeDtypeStruct((query_rows, probe_count * page_rows), BF16),
        compiler_params=params(32 * MIB),
        cost_estimate=cost(1),
        name="place_scores",
    )(probe_place, returned.reshape(shards * capacity, block_rows, page_rows))
    return coarse, rerank


def solution(mesh):
    split = P(("grp", "idx"))
    in_specs = (split, P(), split, split, split, split, split)
    return jax.shard_map(body, mesh=mesh, in_specs=in_specs, out_specs=(split, split), check_vma=False)
```

time: 163 us -> 150 us (0.920)
  blocking collectives: 12.3 us -> 0 us
  Pallas kernels: 61.7 us -> 51.6 us
  waiting for transfers between devices: 44.7 us -> 53.7 us
  starting transfers between devices: 26.8 us -> 34.6 us
  local copies, waits for them, and re-layouts: 14.9 us -> 8.96 us
    ppermute x30 -> x36, waiting for transfers between devices: 23.5 us -> 53.7 us  [exchange(): return lax.ppermute(x, 'idx', [(i, i ^ mask) for i in range(shards)])]
    all_to_all x1, waiting for transfers between devices: 21.2 us -> 0.01 us  [body(): lax.all_to_all(scored, 'idx', split_axis=0, concat_axis=0, tiled=True)]
    pallas_call x3, Pallas kernels: 44.3 us -> 28.1 us  [the longest x1 25.3 us: body(): pl.pallas_call(functools.partial(gather_kernel, shards, row_capacity), in...]
    all_to_all x1 -> x0, blocking collectives: 12.3 us -> none  [body(): lax.all_to_all(answers, 'idx', split_axis=0, concat_axis=0, tiled=True)]
    ppermute x30 -> x36, starting transfers between devices: 23.1 us -> 29.5 us  [exchange(): return lax.ppermute(x, 'idx', [(i, i ^ mask) for i in range(shards)])]
    unnamed x43 -> x16, local copies, waits for them, and re-layouts: 14.9 us -> 8.96 us
    pallas_call x1, Pallas kernels: 9.65 us -> 13.6 us  [body(): pl.pallas_call(functools.partial(rerank_kernel, shards, row_capacity), in...]
    pallas_call x1, Pallas kernels: 4.55 us -> 6.68 us  [body(): pl.pallas_call(functools.partial(coarse_kernel, shards, capacity, block_r...]
  transfers between devices with their start and end apart: 31 -> 37, of which waited for: 9 -> 13; matrix products, arithmetic and copies ran while one was open for 0% -> 0% of each run, Pallas kernels for 31% -> 28%
where the time goes in v2:
time: 150 us
  waiting for transfers between devices  53.7 us (36%)
  Pallas kernels  51.6 us (34%)
  starting transfers between devices  34.6 us (23%)
  local copies, waits for them, and re-layouts  8.96 us (6%)
    ppermute x36, waiting for transfers between devices, exchange(): return lax.ppermute(x, 'idx', [(i, i ^ mask) for i in range(shards)])  53.7 us
    ppermute x36, starting transfers between devices, exchange(): return lax.ppermute(x, 'idx', [(i, i ^ mask) for i in range(shards)])  29.5 us
    pallas_call x1, Pallas kernels, body(): pl.pallas_call(functools.partial(gather_kernel, shards, row_capacity), in...  25.3 us
    pallas_call x1, Pallas kernels, body(): pl.pallas_call(functools.partial(rerank_kernel, shards, row_capacity), in...  13.6 us
    unnamed x16, local copies, waits for them, and re-layouts  8.96 us
    pallas_call x1, Pallas kernels, body(): pl.pallas_call(functools.partial(coarse_kernel, shards, capacity, block_r...  6.68 us
    all_to_all x1, starting transfers between devices, body(): lax.all_to_all(scored, 'idx', split_axis=0, concat_axis=0, tiled=True)  5.04 us
  transfers between devices with their start and end apart: 37, of which 13 were waited for; matrix products, arithmetic and copies ran while one was open for 0% of the time, Pallas kernels for 28%

profile of v2, /device:TPU:0, one launch (start us, length us, event | category | flops | bytes accessed | tf_op | source)
XLA Modules:
  0.0 149.6 jit_solution(1625758307554492440)
XLA Ops:
  0.6 2.2 %copy-done = f32[1024,1024]{1,0:T(8,128)S(1)} copy-done((f32[1024,1024]{1,0:T(8,128)S(1)}, f32[1024,1024]{1,0:T(8,128)}, u32[]{:S(2)}) %copy-start) | copy-done | bytes 4194328
  5.8 1.8 %plan.1 = (bf16[160,256]{1,0:T(8,128)(2,1)S(1)}, s32[4,16]{1,0:T(4,128)S(1)}, s32[16,128]{1,0:T(8,128)S(1)}) custom-call(bf16[128,1024]{1,0:T(8,128)(2,1)S(1)} %copy-done.3, f32[1024,1024]{1,0:T(8,128)S(1)} %copy-done, s32[4,16]{1,0:T(4,128)S(1)} %copy-done.7, s32[8,128]{1,0:T(8,128)S(1)} %bitcast.15, s32[8,128]{1,0:T(8,128)S(1)} %bitcast.16), custom_call_target="tpu_custom_call" | custom-call | bytes 6000000 | tf_op jit(solution)/shard_map/plan/pallas_call | solution.py:248
  7.7 5.1 %collective-permute-start.11 = (bf16[160,256]{1,0:T(8,128)(2,1)S(1)}, bf16[160,256]{1,0:T(8,128)(2,1)S(1)}, u32[]{:S(2)}, u32[]{:S(2)}) collective-permute-start(bf16[160,256]{1,0:T(8,128)(2,1)S(1)} %get-tuple-element.13.refs_0_), channel_id=1, source_target_pairs={{0,12},{1,13},{2,14},{3,15},{4,8},{5,9},{6,10},{7,11},{8,4},{9,5},... | collective-permute-start | bytes 245768 | tf_op jit(solution)/shard_map/ppermute | solution.py:218
  13.4 1.7 %collective-permute-start.1 = (bf16[160,256]{1,0:T(8,128)(2,1)S(1)}, bf16[160,256]{1,0:T(8,128)(2,1)S(1)}, u32[]{:S(2)}, u32[]{:S(2)}) collective-permute-start(bf16[160,256]{1,0:T(8,128)(2,1)S(1)} %get-tuple-element.13.refs_0_), channel_id=1, source_target_pairs={{0,2},{1,3},{2,0},{3,1},{4,6},{5,7},{6,4},{7,5},{8,10},{9,11},{10,... | collective-permute-start | bytes 245768 | tf_op jit(solution)/shard_map/ppermute | solution.py:218
  15.8 1.8 %collective-permute-start.13 = (bf16[160,256]{1,0:T(8,128)(2,1)S(1)}, bf16[160,256]{1,0:T(8,128)(2,1)S(1)}, u32[]{:S(2)}, u32[]{:S(2)}) collective-permute-start(bf16[160,256]{1,0:T(8,128)(2,1)S(1)} %collective-permute-done.11.refs_12_), channel_id=1, source_target_pairs={{0,2},{1,3},{2,0},{3,1},{4,6},{5,7},{6,4},{7,5},{8,10},{9,11},{10,... | collective-permute-start | bytes 245768 | tf_op jit(solution)/shard_map/ppermute | solution.py:218
  17.6 2.0 %collective-permute-done.7.refs_8_ = bf16[160,256]{1,0:T(8,128)(2,1)S(1)} collective-permute-done((bf16[160,256]{1,0:T(8,128)(2,1)S(1)}, bf16[160,256]{1,0:T(8,128)(2,1)S(1)}, u32[]{:S(2)}, u32[]{:S(2)}) %collective-permute-start.7) | collective-permute-done | bytes 81952 | tf_op jit(solution)/shard_map/ppermute | solution.py:218
  19.7 1.5 %collective-permute-start.9 = (bf16[160,256]{1,0:T(8,128)(2,1)S(1)}, bf16[160,256]{1,0:T(8,128)(2,1)S(1)}, u32[]{:S(2)}, u32[]{:S(2)}) collective-permute-start(bf16[160,256]{1,0:T(8,128)(2,1)S(1)} %collective-permute-done.7.refs_8_), channel_id=1, source_target_pairs={{0,2},{1,3},{2,0},{3,1},{4,6},{5,7},{6,4},{7,5},{8,10},{9,11},{10,... | collective-permute-start | bytes 245768 | tf_op jit(solution)/shard_map/ppermute | solution.py:218
  22.4 2.3 %collective-permute-done.9.refs_10_ = bf16[160,256]{1,0:T(8,128)(2,1)S(1)} collective-permute-done((bf16[160,256]{1,0:T(8,128)(2,1)S(1)}, bf16[160,256]{1,0:T(8,128)(2,1)S(1)}, u32[]{:S(2)}, u32[]{:S(2)}) %collective-permute-start.9) | collective-permute-done | bytes 81952 | tf_op jit(solution)/shard_map/ppermute | solution.py:218
  25.2 1.0 collective-permute-done.5.refs_6_
  26.3 1.2 collective-permute-done.6.refs_7_
  27.6 1.6 %copy-done.2 = bf16[32,128,256]{2,1,0:T(8,128)(2,1)S(1)} copy-done((bf16[32,128,256]{2,1,0:T(8,128)(2,1)S(1)}, bf16[32,128,256]{2,1,0:T(8,128)(2,1)}, u32[]{:S(2)}) %copy-start.2) | copy-done | bytes 2097176
  29.1 6.7 %coarse_scores.1 = (bf16[16,8,32,128]{3,2,1,0:T(8,128)(2,1)}, s32[16,128]{1,0:T(8,128)S(1)}, s32[16,128]{1,0:T(8,128)S(1)}) custom-call(s32[1]{0:T(128)} %bitcast.2.me_ref, bf16[160,256]{1,0:T(8,128)(2,1)S(1)} %get-tuple-element.13.refs_0_, bf16[160,256]{1,0:T(8,128)(2,1)S(1)} %collective-permute-done.refs_1_, ...), custom_call_target="tpu_custom_call" | custom-call | bytes 18000000 | tf_op jit(solution)/shard_map/coarse_scores/pallas_call | solution.py:279
  35.8 5.0 %all-to-all-start = ((bf16[16,8,32,128]{3,2,1,0:T(8,128)(2,1)}), bf16[16,8,32,128]{3,2,1,0:T(8,128)(2,1)S(1)}, u32[]{:S(2)}, u32[]{:S(2)}) async-start(bf16[16,8,32,128]{3,2,1,0:T(8,128)(2,1)} %get-tuple-element.14), calls=%async_computation | async-start | bytes 2097152 | tf_op jit(solution)/shard_map/all_to_all | solution.py:299
  40.9 2.2 %copy-done.1 = f32[1024,1024]{1,0:T(8,128)S(1)} copy-done((f32[1024,1024]{1,0:T(8,128)S(1)}, f32[1024,1024]{1,0:T(8,128)}, u32[]{:S(2)}) %copy-start.1) | copy-done | bytes 4194328
  43.1 1.7 %rotate_rest.1.refs_16_ = bf16[128,768]{1,0:T(8,128)(2,1)S(1)} custom-call(bf16[128,1024]{1,0:T(8,128)(2,1)S(1)} %copy-done.4, f32[1024,1024]{1,0:T(8,128)S(1)} %copy-done.1), custom_call_target="tpu_custom_call" | custom-call | bytes 6000000 | tf_op jit(solution)/shard_map/rotate_rest/pallas_call | solution.py:262
  44.8 3.8 %collective-permute-start.26 = (bf16[128,768]{1,0:T(8,128)(2,1)S(1)}, bf16[128,768]{1,0:T(8,128)(2,1)S(1)}, u32[]{:S(2)}, u32[]{:S(2)}) collective-permute-start(bf16[128,768]{1,0:T(8,128)(2,1)S(1)} %rotate_rest.1.refs_16_), channel_id=1, source_target_pairs={{0,12},{1,13},{2,14},{3,15},{4,8},{5,9},{6,10},{7,11},{8,4},{9,5},... | collective-permute-start | bytes 589832 | tf_op jit(solution)/shard_map/ppermute | solution.py:218
  49.2 1.9 %collective-permute-start.16 = (bf16[128,768]{1,0:T(8,128)(2,1)S(1)}, bf16[128,768]{1,0:T(8,128)(2,1)S(1)}, u32[]{:S(2)}, u32[]{:S(2)}) collective-permute-start(bf16[128,768]{1,0:T(8,128)(2,1)S(1)} %rotate_rest.1.refs_16_), channel_id=1, source_target_pairs={{0,2},{1,3},{2,0},{3,1},{4,6},{5,7},{6,4},{7,5},{8,10},{9,11},{10,... | collective-permute-start | bytes 589832 | tf_op jit(solution)/shard_map/ppermute | solution.py:218
  51.2 16.4 %collective-permute-done.26.refs_28_ = bf16[128,768]{1,0:T(8,128)(2,1)S(1)} collective-permute-done((bf16[128,768]{1,0:T(8,128)(2,1)S(1)}, bf16[128,768]{1,0:T(8,128)(2,1)S(1)}, u32[]{:S(2)}, u32[]{:S(2)}) %collective-permute-start.26) | collective-permute-done | bytes 196640 | tf_op jit(solution)/shard_map/ppermute | solution.py:218
  67.6 1.5 collective-permute-start.28
  69.1 15.2 %collective-permute-done.22.refs_24_ = bf16[128,768]{1,0:T(8,128)(2,1)S(1)} collective-permute-done((bf16[128,768]{1,0:T(8,128)(2,1)S(1)}, bf16[128,768]{1,0:T(8,128)(2,1)S(1)}, u32[]{:S(2)}, u32[]{:S(2)}) %collective-permute-start.22) | collective-permute-done | bytes 196640 | tf_op jit(solution)/shard_map/ppermute | solution.py:218
  84.3 1.5 collective-permute-start.24
  87.1 4.9 %collective-permute-done.24.refs_26_ = bf16[128,768]{1,0:T(8,128)(2,1)S(1)} collective-permute-done((bf16[128,768]{1,0:T(8,128)(2,1)S(1)}, bf16[128,768]{1,0:T(8,128)(2,1)S(1)}, u32[]{:S(2)}, u32[]{:S(2)}) %collective-permute-start.24) | collective-permute-done | bytes 196640 | tf_op jit(solution)/shard_map/ppermute | solution.py:218
  92.5 3.3 %collective-permute-done.20.refs_22_ = bf16[128,768]{1,0:T(8,128)(2,1)S(1)} collective-permute-done((bf16[128,768]{1,0:T(8,128)(2,1)S(1)}, bf16[128,768]{1,0:T(8,128)(2,1)S(1)}, u32[]{:S(2)}, u32[]{:S(2)}) %collective-permute-start.20) | collective-permute-done | bytes 196640 | tf_op jit(solution)/shard_map/ppermute | solution.py:218
  95.9 25.3 %gather_rows.1.rows_ref = bf16[16,256,1024]{2,1,0:T(8,128)(2,1)} custom-call(s32[16,128]{1,0:T(8,128)S(1)} %get-tuple-element.16.index_ref, f32[32768,128]{1,0:T(8,128)} %bitcast.18), custom_call_target="tpu_custom_call" | custom-call | bytes 45000000 | tf_op jit(solution)/shard_map/gather_rows/pallas_call | solution.py:303
  121.2 13.6 %rerank_scores.1 = (f32[4,128]{1,0:T(4,128)S(1)}, f32[4,128]{1,0:T(4,128)S(1)}, f32[4,128]{1,0:T(4,128)S(1)}, f32[4,128]{1,0:T(4,128)S(1)}) custom-call(s32[1]{0:T(128)} %bitcast.2.me_ref, s32[16,128]{1,0:T(8,128)S(1)} %get-tuple-element.15.query_ref, bf16[16,256,1024]{2,1,0:T(8,128)(2,1)} %gather_rows.1.rows_ref, ...), custom_call_target="tpu_custom_call" | custom-call | bytes 24000000 | tf_op jit(solution)/shard_map/rerank_scores/pallas_call | solution.py:319
  134.9 2.0 %collective-permute-start.31 = (f32[4,128]{1,0:T(4,128)S(1)}, f32[4,128]{1,0:T(4,128)S(1)}, u32[]{:S(2)}, u32[]{:S(2)}) collective-permute-start(f32[4,128]{1,0:T(4,128)S(1)} %get-tuple-element.19), channel_id=1, source_target_pairs={{0,8},{1,9},{2,10},{3,11},{4,12},{5,13},{6,14},{7,15},{8,0},{9,1},... | collective-permute-start | bytes 6152 | tf_op jit(solution)/shard_map/ppermute | solution.py:218
  136.9 2.4 %collective-permute-start.32 = (f32[4,128]{1,0:T(4,128)S(1)}, f32[4,128]{1,0:T(4,128)S(1)}, u32[]{:S(2)}, u32[]{:S(2)}) collective-permute-start(f32[4,128]{1,0:T(4,128)S(1)} %get-tuple-element.20), channel_id=1, source_target_pairs={{0,12},{1,13},{2,14},{3,15},{4,8},{5,9},{6,10},{7,11},{8,4},{9,5},... | collective-permute-start | bytes 6152 | tf_op jit(solution)/shard_map/ppermute | solution.py:218
  139.4 2.8 %collective-permute-done.32 = f32[4,128]{1,0:T(4,128)S(1)} collective-permute-done((f32[4,128]{1,0:T(4,128)S(1)}, f32[4,128]{1,0:T(4,128)S(1)}, u32[]{:S(2)}, u32[]{:S(2)}) %collective-permute-start.32) | collective-permute-done | bytes 2080 | tf_op jit(solution)/shard_map/ppermute | solution.py:218
  142.3 1.5 collective-permute-start.33
  143.7 2.2 %collective-permute-done.33.y_ref = f32[4,4,128]{2,1,0:T(4,128)S(1)} collective-permute-done((f32[4,4,128]{2,1,0:T(4,128)S(1)}, f32[4,4,128]{2,1,0:T(4,128)S(1)}, u32[]{:S(2)}, u32[]{:S(2)}) %collective-permute-start.33) | collective-permute-done | bytes 8224 | tf_op jit(solution)/shard_map/ppermute | solution.py:218
  145.9 1.2 collective-permute-done.35.both_ref
  148.1 1.5 place_scores.1
  (66 shorter events, 9.9 us)
Async XLA Ops:
  7.7 8.1 %collective-permute-start.11 = (bf16[160,256]{1,0:T(8,128)(2,1)S(1)}, bf16[160,256]{1,0:T(8,128)(2,1)S(1)}, u32[]{:S(2)}, u32[]{:S(2)}) collective-permute-start(bf16[160,256]{1,0:T(8,128)(2,1)S(1)} %get-tuple-element.13.refs_0_), channel_id=1, source_target_pairs={{0,12},{1,13},{2,14},{3,15},{4,8},{5,9},{6,10},{7,11},{8,4},{9,5},... | collective-permute-start | bytes 245768 | tf_op jit(solution)/shard_map/ppermute | solution.py:218
  12.8 6.9 %collective-permute-start.7 = (bf16[160,256]{1,0:T(8,128)(2,1)S(1)}, bf16[160,256]{1,0:T(8,128)(2,1)S(1)}, u32[]{:S(2)}, u32[]{:S(2)}) collective-permute-start(bf16[160,256]{1,0:T(8,128)(2,1)S(1)} %get-tuple-element.13.refs_0_), channel_id=1, source_target_pairs={{0,8},{1,9},{2,10},{3,11},{4,12},{5,13},{6,14},{7,15},{8,0},{9,1},... | collective-permute-start | bytes 245768 | tf_op jit(solution)/shard_map/ppermute | solution.py:218
  12.8 6.9 %collective-permute-start.3 = (bf16[160,256]{1,0:T(8,128)(2,1)S(1)}, bf16[160,256]{1,0:T(8,128)(2,1)S(1)}, u32[]{:S(2)}, u32[]{:S(2)}) collective-permute-start(bf16[160,256]{1,0:T(8,128)(2,1)S(1)} %get-tuple-element.13.refs_0_), channel_id=1, source_target_pairs={{0,4},{1,5},{2,6},{3,7},{4,0},{5,1},{6,2},{7,3},{8,12},{9,13},{10,... | collective-permute-start | bytes 245768 | tf_op jit(solution)/shard_map/ppermute | solution.py:218
  13.4 7.7 %collective-permute-start.1 = (bf16[160,256]{1,0:T(8,128)(2,1)S(1)}, bf16[160,256]{1,0:T(8,128)(2,1)S(1)}, u32[]{:S(2)}, u32[]{:S(2)}) collective-permute-start(bf16[160,256]{1,0:T(8,128)(2,1)S(1)} %get-tuple-element.13.refs_0_), channel_id=1, source_target_pairs={{0,2},{1,3},{2,0},{3,1},{4,6},{5,7},{6,4},{7,5},{8,10},{9,11},{10,... | collective-permute-start | bytes 245768 | tf_op jit(solution)/shard_map/ppermute | solution.py:218
  15.1 6.3 %collective-permute-start = (bf16[160,256]{1,0:T(8,128)(2,1)S(1)}, bf16[160,256]{1,0:T(8,128)(2,1)S(1)}, u32[]{:S(2)}, u32[]{:S(2)}) collective-permute-start(bf16[160,256]{1,0:T(8,128)(2,1)S(1)} %get-tuple-element.13.refs_0_), channel_id=1, source_target_pairs={{0,1},{1,0},{2,3},{3,2},{4,5},{5,4},{6,7},{7,6},{8,9},{9,8},{10,11... | collective-permute-start | bytes 245768 | tf_op jit(solution)/shard_map/ppermute | solution.py:218
  15.8 6.1 %collective-permute-start.13 = (bf16[160,256]{1,0:T(8,128)(2,1)S(1)}, bf16[160,256]{1,0:T(8,128)(2,1)S(1)}, u32[]{:S(2)}, u32[]{:S(2)}) collective-permute-start(bf16[160,256]{1,0:T(8,128)(2,1)S(1)} %collective-permute-done.11.refs_12_), channel_id=1, source_target_pairs={{0,2},{1,3},{2,0},{3,1},{4,6},{5,7},{6,4},{7,5},{8,10},{9,11},{10,... | collective-permute-start | bytes 245768 | tf_op jit(solution)/shard_map/ppermute | solution.py:218
  19.7 2.3 %collective-permute-start.12 = (bf16[160,256]{1,0:T(8,128)(2,1)S(1)}, bf16[160,256]{1,0:T(8,128)(2,1)S(1)}, u32[]{:S(2)}, u32[]{:S(2)}) collective-permute-start(bf16[160,256]{1,0:T(8,128)(2,1)S(1)} %collective-permute-done.11.refs_12_), channel_id=1, source_target_pairs={{0,1},{1,0},{2,3},{3,2},{4,5},{5,4},{6,7},{7,6},{8,9},{9,8},{10,11... | collective-permute-start | bytes 245768 | tf_op jit(solution)/shard_map/ppermute | solution.py:218
  19.7 5.1 %collective-permute-start.9 = (bf16[160,256]{1,0:T(8,128)(2,1)S(1)}, bf16[160,256]{1,0:T(8,128)(2,1)S(1)}, u32[]{:S(2)}, u32[]{:S(2)}) collective-permute-start(bf16[160,256]{1,0:T(8,128)(2,1)S(1)} %collective-permute-done.7.refs_8_), channel_id=1, source_target_pairs={{0,2},{1,3},{2,0},{3,1},{4,6},{5,7},{6,4},{7,5},{8,10},{9,11},{10,... | collective-permute-start | bytes 245768 | tf_op jit(solution)/shard_map/ppermute | solution.py:218
  21.2 3.6 %collective-permute-start.8 = (bf16[160,256]{1,0:T(8,128)(2,1)S(1)}, bf16[160,256]{1,0:T(8,128)(2,1)S(1)}, u32[]{:S(2)}, u32[]{:S(2)}) collective-permute-start(bf16[160,256]{1,0:T(8,128)(2,1)S(1)} %collective-permute-done.7.refs_8_), channel_id=1, source_target_pairs={{0,1},{1,0},{2,3},{3,2},{4,5},{5,4},{6,7},{7,6},{8,9},{9,8},{10,11... | collective-permute-start | bytes 245768 | tf_op jit(solution)/shard_map/ppermute | solution.py:218
  21.4 4.9 %collective-permute-start.5 = (bf16[160,256]{1,0:T(8,128)(2,1)S(1)}, bf16[160,256]{1,0:T(8,128)(2,1)S(1)}, u32[]{:S(2)}, u32[]{:S(2)}) collective-permute-start(bf16[160,256]{1,0:T(8,128)(2,1)S(1)} %collective-permute-done.3.refs_4_), channel_id=1, source_target_pairs={{0,2},{1,3},{2,0},{3,1},{4,6},{5,7},{6,4},{7,5},{8,10},{9,11},{10,... | collective-permute-start | bytes 245768 | tf_op jit(solution)/shard_map/ppermute | solution.py:218
  21.9 4.4 %collective-permute-start.4 = (bf16[160,256]{1,0:T(8,128)(2,1)S(1)}, bf16[160,256]{1,0:T(8,128)(2,1)S(1)}, u32[]{:S(2)}, u32[]{:S(2)}) collective-permute-start(bf16[160,256]{1,0:T(8,128)(2,1)S(1)} %collective-permute-done.3.refs_4_), channel_id=1, source_target_pairs={{0,1},{1,0},{2,3},{3,2},{4,5},{5,4},{6,7},{7,6},{8,9},{9,8},{10,11... | collective-permute-start | bytes 245768 | tf_op jit(solution)/shard_map/ppermute | solution.py:218
  21.9 4.3 %collective-permute-start.2 = (bf16[160,256]{1,0:T(8,128)(2,1)S(1)}, bf16[160,256]{1,0:T(8,128)(2,1)S(1)}, u32[]{:S(2)}, u32[]{:S(2)}) collective-permute-start(bf16[160,256]{1,0:T(8,128)(2,1)S(1)} %collective-permute-done.1.refs_2_), channel_id=1, source_target_pairs={{0,1},{1,0},{2,3},{3,2},{4,5},{5,4},{6,7},{7,6},{8,9},{9,8},{10,11... | collective-permute-start | bytes 245768 | tf_op jit(solution)/shard_map/ppermute | solution.py:218
  35.8 112.3 %all-to-all-start = ((bf16[16,8,32,128]{3,2,1,0:T(8,128)(2,1)}), bf16[16,8,32,128]{3,2,1,0:T(8,128)(2,1)S(1)}, u32[]{:S(2)}, u32[]{:S(2)}) async-start(bf16[16,8,32,128]{3,2,1,0:T(8,128)(2,1)} %get-tuple-element.14), calls=%async_computation | async-start | bytes 2097152 | tf_op jit(solution)/shard_map/all_to_all | solution.py:299
  44.8 22.8 %collective-permute-start.26 = (bf16[128,768]{1,0:T(8,128)(2,1)S(1)}, bf16[128,768]{1,0:T(8,128)(2,1)S(1)}, u32[]{:S(2)}, u32[]{:S(2)}) collective-permute-start(bf16[128,768]{1,0:T(8,128)(2,1)S(1)} %rotate_rest.1.refs_16_), channel_id=1, source_target_pairs={{0,12},{1,13},{2,14},{3,15},{4,8},{5,9},{6,10},{7,11},{8,4},{9,5},... | collective-permute-start | bytes 589832 | tf_op jit(solution)/shard_map/ppermute | solution.py:218
  48.6 35.7 %collective-permute-start.22 = (bf16[128,768]{1,0:T(8,128)(2,1)S(1)}, bf16[128,768]{1,0:T(8,128)(2,1)S(1)}, u32[]{:S(2)}, u32[]{:S(2)}) collective-permute-start(bf16[128,768]{1,0:T(8,128)(2,1)S(1)} %rotate_rest.1.refs_16_), channel_id=1, source_target_pairs={{0,8},{1,9},{2,10},{3,11},{4,12},{5,13},{6,14},{7,15},{8,0},{9,1},... | collective-permute-start | bytes 589832 | tf_op jit(solution)/shard_map/ppermute | solution.py:218
  48.6 35.8 %collective-permute-start.18 = (bf16[128,768]{1,0:T(8,128)(2,1)S(1)}, bf16[128,768]{1,0:T(8,128)(2,1)S(1)}, u32[]{:S(2)}, u32[]{:S(2)}) collective-permute-start(bf16[128,768]{1,0:T(8,128)(2,1)S(1)} %rotate_rest.1.refs_16_), channel_id=1, source_target_pairs={{0,4},{1,5},{2,6},{3,7},{4,0},{5,1},{6,2},{7,3},{8,12},{9,13},{10,... | collective-permute-start | bytes 589832 | tf_op jit(solution)/shard_map/ppermute | solution.py:218
  49.2 36.6 %collective-permute-start.16 = (bf16[128,768]{1,0:T(8,128)(2,1)S(1)}, bf16[128,768]{1,0:T(8,128)(2,1)S(1)}, u32[]{:S(2)}, u32[]{:S(2)}) collective-permute-start(bf16[128,768]{1,0:T(8,128)(2,1)S(1)} %rotate_rest.1.refs_16_), channel_id=1, source_target_pairs={{0,2},{1,3},{2,0},{3,1},{4,6},{5,7},{6,4},{7,5},{8,10},{9,11},{10,... | collective-permute-start | bytes 589832 | tf_op jit(solution)/shard_map/ppermute | solution.py:218
  51.2 34.9 %collective-permute-start.15 = (bf16[128,768]{1,0:T(8,128)(2,1)S(1)}, bf16[128,768]{1,0:T(8,128)(2,1)S(1)}, u32[]{:S(2)}, u32[]{:S(2)}) collective-permute-start(bf16[128,768]{1,0:T(8,128)(2,1)S(1)} %rotate_rest.1.refs_16_), channel_id=1, source_target_pairs={{0,1},{1,0},{2,3},{3,2},{4,5},{5,4},{6,7},{7,6},{8,9},{9,8},{10,11... | collective-permute-start | bytes 589832 | tf_op jit(solution)/shard_map/ppermute | solution.py:218
  67.6 19.0 %collective-permute-start.28 = (bf16[128,768]{1,0:T(8,128)(2,1)S(1)}, bf16[128,768]{1,0:T(8,128)(2,1)S(1)}, u32[]{:S(2)}, u32[]{:S(2)}) collective-permute-start(bf16[128,768]{1,0:T(8,128)(2,1)S(1)} %collective-permute-done.26.refs_28_), channel_id=1, source_target_pairs={{0,2},{1,3},{2,0},{3,1},{4,6},{5,7},{6,4},{7,5},{8,10},{9,11},{10,... | collective-permute-start | bytes 589832 | tf_op jit(solution)/shard_map/ppermute | solution.py:218
  84.3 2.3 %collective-permute-start.27 = (bf16[128,768]{1,0:T(8,128)(2,1)S(1)}, bf16[128,768]{1,0:T(8,128)(2,1)S(1)}, u32[]{:S(2)}, u32[]{:S(2)}) collective-permute-start(bf16[128,768]{1,0:T(8,128)(2,1)S(1)} %collective-permute-done.26.refs_28_), channel_id=1, source_target_pairs={{0,1},{1,0},{2,3},{3,2},{4,5},{5,4},{6,7},{7,6},{8,9},{9,8},{10,11... | collective-permute-start | bytes 589832 | tf_op jit(solution)/shard_map/ppermute | solution.py:218
  84.3 7.7 %collective-permute-start.24 = (bf16[128,768]{1,0:T(8,128)(2,1)S(1)}, bf16[128,768]{1,0:T(8,128)(2,1)S(1)}, u32[]{:S(2)}, u32[]{:S(2)}) collective-permute-start(bf16[128,768]{1,0:T(8,128)(2,1)S(1)} %collective-permute-done.22.refs_24_), channel_id=1, source_target_pairs={{0,2},{1,3},{2,0},{3,1},{4,6},{5,7},{6,4},{7,5},{8,10},{9,11},{10,... | collective-permute-start | bytes 589832 | tf_op jit(solution)/shard_map/ppermute | solution.py:218
  85.8 6.2 %collective-permute-start.23 = (bf16[128,768]{1,0:T(8,128)(2,1)S(1)}, bf16[128,768]{1,0:T(8,128)(2,1)S(1)}, u32[]{:S(2)}, u32[]{:S(2)}) collective-permute-start(bf16[128,768]{1,0:T(8,128)(2,1)S(1)} %collective-permute-done.22.refs_24_), channel_id=1, source_target_pairs={{0,1},{1,0},{2,3},{3,2},{4,5},{5,4},{6,7},{7,6},{8,9},{9,8},{10,11... | collective-permute-start | bytes 589832 | tf_op jit(solution)/shard_map/ppermute | solution.py:218
  86.0 9.8 %collective-permute-start.20 = (bf16[128,768]{1,0:T(8,128)(2,1)S(1)}, bf16[128,768]{1,0:T(8,128)(2,1)S(1)}, u32[]{:S(2)}, u32[]{:S(2)}) collective-permute-start(bf16[128,768]{1,0:T(8,128)(2,1)S(1)} %collective-permute-done.18.refs_20_), channel_id=1, source_target_pairs={{0,2},{1,3},{2,0},{3,1},{4,6},{5,7},{6,4},{7,5},{8,10},{9,11},{10,... | collective-permute-start | bytes 589832 | tf_op jit(solution)/shard_map/ppermute | solution.py:218
  86.6 34.6 %collective-permute-start.19 = (bf16[128,768]{1,0:T(8,128)(2,1)S(1)}, bf16[128,768]{1,0:T(8,128)(2,1)S(1)}, u32[]{:S(2)}, u32[]{:S(2)}) collective-permute-start(bf16[128,768]{1,0:T(8,128)(2,1)S(1)} %collective-permute-done.18.refs_20_), channel_id=1, source_target_pairs={{0,1},{1,0},{2,3},{3,2},{4,5},{5,4},{6,7},{7,6},{8,9},{9,8},{10,11... | collective-permute-start | bytes 589832 | tf_op jit(solution)/shard_map/ppermute | solution.py:218
  86.6 34.6 %collective-permute-start.17 = (bf16[128,768]{1,0:T(8,128)(2,1)S(1)}, bf16[128,768]{1,0:T(8,128)(2,1)S(1)}, u32[]{:S(2)}, u32[]{:S(2)}) collective-permute-start(bf16[128,768]{1,0:T(8,128)(2,1)S(1)} %collective-permute-done.16.refs_18_), channel_id=1, source_target_pairs={{0,1},{1,0},{2,3},{3,2},{4,5},{5,4},{6,7},{7,6},{8,9},{9,8},{10,11... | collective-permute-start | bytes 589832 | tf_op jit(solution)/shard_map/ppermute | solution.py:218
  92.0 29.2 %collective-permute-start.29 = (bf16[128,768]{1,0:T(8,128)(2,1)S(1)}, bf16[128,768]{1,0:T(8,128)(2,1)S(1)}, u32[]{:S(2)}, u32[]{:S(2)}) collective-permute-start(bf16[128,768]{1,0:T(8,128)(2,1)S(1)} %collective-permute-done.28.refs_30_), channel_id=1, source_target_pairs={{0,1},{1,0},{2,3},{3,2},{4,5},{5,4},{6,7},{7,6},{8,9},{9,8},{10,11... | collective-permute-start | bytes 589832 | tf_op jit(solution)/shard_map/ppermute | solution.py:218
  92.0 29.2 %collective-permute-start.25 = (bf16[128,768]{1,0:T(8,128)(2,1)S(1)}, bf16[128,768]{1,0:T(8,128)(2,1)S(1)}, u32[]{:S(2)}, u32[]{:S(2)}) collective-permute-start(bf16[128,768]{1,0:T(8,128)(2,1)S(1)} %collective-permute-done.24.refs_26_), channel_id=1, source_target_pairs={{0,1},{1,0},{2,3},{3,2},{4,5},{5,4},{6,7},{7,6},{8,9},{9,8},{10,11... | collective-permute-start | bytes 589832 | tf_op jit(solution)/shard_map/ppermute | solution.py:218
  95.9 25.3 %collective-permute-start.21 = (bf16[128,768]{1,0:T(8,128)(2,1)S(1)}, bf16[128,768]{1,0:T(8,128)(2,1)S(1)}, u32[]{:S(2)}, u32[]{:S(2)}) collective-permute-start(bf16[128,768]{1,0:T(8,128)(2,1)S(1)} %collective-permute-done.20.refs_22_), channel_id=1, source_target_pairs={{0,1},{1,0},{2,3},{3,2},{4,5},{5,4},{6,7},{7,6},{8,9},{9,8},{10,11... | collective-permute-start | bytes 589832 | tf_op jit(solution)/shard_map/ppermute | solution.py:218
  134.8 4.5 %collective-permute-start.30 = (f32[4,128]{1,0:T(4,128)S(1)}, f32[4,128]{1,0:T(4,128)S(1)}, u32[]{:S(2)}, u32[]{:S(2)}) collective-permute-start(f32[4,128]{1,0:T(4,128)S(1)} %get-tuple-element.18), channel_id=1, source_target_pairs={{0,4},{1,5},{2,6},{3,7},{4,0},{5,1},{6,2},{7,3},{8,12},{9,13},{10,... | collective-permute-start | bytes 6152 | tf_op jit(solution)/shard_map/ppermute | solution.py:218
  134.9 4.5 %collective-permute-start.31 = (f32[4,128]{1,0:T(4,128)S(1)}, f32[4,128]{1,0:T(4,128)S(1)}, u32[]{:S(2)}, u32[]{:S(2)}) collective-permute-start(f32[4,128]{1,0:T(4,128)S(1)} %get-tuple-element.19), channel_id=1, source_target_pairs={{0,8},{1,9},{2,10},{3,11},{4,12},{5,13},{6,14},{7,15},{8,0},{9,1},... | collective-permute-start | bytes 6152 | tf_op jit(solution)/shard_map/ppermute | solution.py:218
  136.9 5.4 %collective-permute-start.32 = (f32[4,128]{1,0:T(4,128)S(1)}, f32[4,128]{1,0:T(4,128)S(1)}, u32[]{:S(2)}, u32[]{:S(2)}) collective-permute-start(f32[4,128]{1,0:T(4,128)S(1)} %get-tuple-element.20), channel_id=1, source_target_pairs={{0,12},{1,13},{2,14},{3,15},{4,8},{5,9},{6,10},{7,11},{8,4},{9,5},... | collective-permute-start | bytes 6152 | tf_op jit(solution)/shard_map/ppermute | solution.py:218
  142.3 3.7 %collective-permute-start.33 = (f32[4,4,128]{2,1,0:T(4,128)S(1)}, f32[4,4,128]{2,1,0:T(4,128)S(1)}, u32[]{:S(2)}, u32[]{:S(2)}) collective-permute-start(f32[4,4,128]{2,1,0:T(4,128)S(1)} %pad_maximum_fusion.own_ref), channel_id=1, source_target_pairs={{0,2},{1,3},{2,0},{3,1},{4,6},{5,7},{6,4},{7,5},{8,10},{9,11},{10,... | collective-permute-start | bytes 24584 | tf_op jit(solution)/shard_map/ppermute | solution.py:218
  (13 other events, 51.8 us)

commit v3 on v2

v3 whole, which is shorter than its diff:
```python
import functools

import jax
import jax.numpy as jnp
from jax import lax
from jax.experimental import pallas as pl
from jax.experimental.pallas import tpu as pltpu
from jax.sharding import PartitionSpec as P

LANES = 128
MIB = 1 << 20
COARSE_COST, GATHER_COST, RERANK_COST = 3, 12, 1
F32, BF16, I32 = jnp.float32, jnp.bfloat16, jnp.int32
VMEM, SMEM, HBM, ANY = pltpu.VMEM, pltpu.SMEM, pltpu.HBM, pl.ANY


def iota(shape, axis):
    return lax.broadcasted_iota(I32, shape, axis)


def dot(a, b, over_a=1, over_b=0):
    return lax.dot_general(a, b, (((over_a,), (over_b,)), ((), ())), preferred_element_type=F32)


def params(limit, **more):
    return pltpu.CompilerParams(vmem_limit_bytes=limit, **more)


def whole(space):
    return pl.BlockSpec(memory_space=space)


def cost(us):
    return pl.CostEstimate(flops=0, bytes_accessed=us * 3_000_000, transcendentals=0)


def parts_of(x, count):
    parts = []
    for _ in range(count):
        parts.append(x.astype(BF16))
        x = x - parts[-1].astype(F32)
    return parts


def rotate(queries, rotation):
    high, low = parts_of(rotation, 2)
    return dot(queries, low) + dot(queries, high)


def ranks(owner, shards):
    rows, lanes = owner.shape
    tall = rows * shards
    spread = (iota((tall, rows), 0) // shards == iota((tall, rows), 1)).astype(BF16)
    hot = (dot(spread, owner.astype(BF16)) == (iota((tall, lanes), 0) % shards).astype(F32)).astype(BF16)
    before = (iota((lanes, lanes), 0) < iota((lanes, lanes), 1)).astype(BF16)
    r, c = iota((tall, tall), 0), iota((tall, tall), 1)
    earlier = ((r % shards == c % shards) & (c // shards < r // shards)).astype(BF16)
    count = dot(hot, before) + jnp.sum(dot(earlier, hot), axis=1, keepdims=True)
    return dot(spread, (hot.astype(F32) * count).astype(BF16), 0, 0).astype(I32)


def table_part(owner, rank, values, shards, kinds):
    rows, lanes = owner.shape
    line = iota((LANES, lanes), 0)
    kind, who = line // shards, line % shards
    left, right = [], []
    for c in range(rows):
        value = jnp.zeros((LANES, lanes), F32)
        for k, v in zip(kinds, values, strict=True):
            value = jnp.where(kind == k, v[c : c + 1], value)
        left.append(jnp.where(owner[c : c + 1] == who, value, 0.0))
        right.append((rank[c : c + 1] == line).astype(F32))
    total = jnp.zeros((LANES, LANES), F32)
    if lanes % LANES == 0:
        return dot(jnp.concatenate(left, 1).astype(BF16), jnp.concatenate(right, 1).astype(BF16), 1, 1)
    for l, r in zip(left, right, strict=True):
        total += dot(l.astype(BF16), r.astype(BF16), 1, 1)
    return total


def plan_kernel(shards, page_count, q_hbm, rot_hbm, probes_hbm, pages_hbm, rows_hbm, chunk_ref, tail_ref, probe_ref, place_ref, q_ref, held, probes_ref, pages_ref, rows_ref, sems):
    cands, rows = pages_ref.shape
    blocks, probes = probes_ref.shape
    width = chunk_ref.shape[1]
    count = held.shape[0]
    pairs = [(pages_hbm, pages_ref), (rows_hbm, rows_ref), (probes_hbm, probes_ref), (q_hbm, q_ref)]
    pairs += [(rot_hbm.at[:, pl.ds(i * width, width)], held.at[i]) for i in range(count)]
    copies = [pltpu.make_async_copy(source, target, sems.at[i]) for i, (source, target) in enumerate(pairs)]
    for copy in copies:
        copy.start()
    for copy in copies[:3]:
        copy.wait()
    pages = pages_ref[...]
    owner = pages // page_count
    rank = ranks(owner, shards)
    place_ref[:cands] = owner
    place_ref[cands:] = rank
    query = iota((cands, rows), 1).astype(F32)
    values = (query, (pages % page_count).astype(F32), rows_ref[...].astype(F32))
    table = table_part(owner, rank, values, shards, (0, 1, 2))

    probe_pages = probes_ref[...]
    probe_owner = probe_pages // page_count
    probe_rank = ranks(probe_owner, shards)
    probe_ref[...] = probe_owner * (2 * blocks * probes // shards) + probe_rank
    value = (probe_pages % page_count + iota(probe_pages.shape, 0) * page_count).astype(F32)
    table += table_part(probe_owner, probe_rank, (value,), shards, (3,))
    table = table.astype(BF16)
    chunk_ref[rows:, :LANES] = table[: 2 * shards]
    chunk_ref[rows:, LANES : 2 * LANES] = table[2 * shards : 4 * shards]
    copies[3].wait()
    for i in range(count):
        copies[4 + i].wait()
        part = rotate(q_ref[...], held[i]).astype(BF16)
        if i == 0:
            chunk_ref[:rows, :] = part
        else:
            tail_ref[:, (i - 1) * width : i * width] = part


def stack_kernel(others, *refs):
    *parts, out_ref = refs[others:]
    for i, part in enumerate(parts):
        out_ref[i] = part[...]


def coarse_kernel(shards, order, block_rows, me_ref, pieces, codes, *refs):
    score_ref, list_ref, lists, slots, slot_ref, sems = refs[-6:]
    capacity = score_ref.shape[1]
    page_count, page_rows, _ = codes.shape
    me = me_ref[0]
    rows = pieces.shape[1] - 2 * shards
    mine = iota((shards, 1), 0) == me
    for p in range(len(order)):
        first = jnp.sum(jnp.where(mine, pieces[p, rows : rows + shards, :].astype(F32), 0.0), axis=0, keepdims=True).astype(I32)
        second = jnp.sum(jnp.where(mine, pieces[p, rows + shards :, :].astype(F32), 0.0), axis=0, keepdims=True).astype(I32)
        lists[0, p : p + 1, :] = second[:, :LANES] * page_rows + first[:, LANES : 2 * LANES]
        lists[1, p : p + 1, :] = first[:, :LANES]
        slots[p : p + 1, :] = second[:, LANES : 2 * LANES]
    copy = pltpu.make_async_copy(slots, slot_ref, sems.at[0])
    copy.start()
    save = pltpu.make_async_copy(lists, list_ref, sems.at[1])
    save.start()
    copy.wait()
    for p, piece in enumerate(order):
        source = me ^ piece
        for s in range(capacity):
            slot = slot_ref[p, s]
            start = pl.multiple_of(slot // page_count * block_rows, block_rows)
            score_ref[source, s] = dot(pieces[p, pl.ds(start, block_rows), :], codes[slot % page_count], 1, 1).astype(BF16)
    save.wait()


def gather_kernel(list_a, list_b, lines_hbm, out_ref, index_ref, lines, sems):
    _, half, capacity, width = out_ref.shape
    count = sems.shape[0] - 2
    size = lines.shape[0] // count
    loads = [
        pltpu.make_async_copy(lines_hbm.at[pl.ds(i * size, size)], lines.at[pl.ds(i * size, size)], sems.at[i])
        for i in range(count)
    ]
    loads.append(pltpu.make_async_copy(list_a.at[0], index_ref.at[pl.ds(0, half)], sems.at[count]))
    loads.append(pltpu.make_async_copy(list_b.at[0], index_ref.at[pl.ds(half, half)], sems.at[count + 1]))
    for load in loads:
        load.start()
    for load in loads:
        load.wait()
    sublane = iota((8, width), 0)

    @pl.loop(0, 2 * half)
    def _(m):
        for g in range(0, capacity, 16):
            halves = []
            for h in range(g, g + 16, 8):
                eight = jnp.zeros((8, width), F32)
                for j in range(8):
                    row = jnp.broadcast_to(lines[pl.ds(index_ref[m, h + j], 1), :], (8, width))
                    eight = jnp.where(sublane == j, row, eight)
                halves.append(eight)
            out_ref[m // half, m % half, g : g + 16, :] = jnp.concatenate(halves, axis=0).astype(BF16)


def rerank_kernel(part, order, list_ref, rows_ref, heads_ref, tails_ref, *refs):
    *before, out_ref, query_ref, sem = refs
    capacity = rows_ref.shape[2]
    queries, split = tails_ref.shape[1], heads_ref.shape[2]
    copy = pltpu.make_async_copy(list_ref.at[1], query_ref, sem)
    copy.start()
    if before:
        out_ref[...] = before[0][...]
    copy.wait()
    for p, m in enumerate(order):
        score = dot(heads_ref[p, :queries, :], rows_ref[part, p, :, :split], 1, 1)
        score += dot(tails_ref[p], rows_ref[part, p, :, split:], 1, 1)
        picked = iota(score.shape, 0) == query_ref[p : p + 1, :capacity]
        out_ref[m // 4, m % 4 : m % 4 + 1, :] = jnp.sum(jnp.where(picked, score, 0.0), axis=0, keepdims=True)


def pick_kernel(shards, me_ref, own_ref, y_ref, core_ref, both_ref, place_ref, out_ref, got):
    cands, rows = out_ref.shape
    capacity = got.shape[1]
    for a in range(shards // 4):
        for low, ref in enumerate((own_ref, core_ref, y_ref, both_ref)):
            got[4 * a + low : 4 * a + low + 1, :] = ref[a, low : low + 1, :]
    piece, rank = place_ref[:cands] ^ me_ref[0], place_ref[cands:]
    hot = [(piece[c : c + 1] == iota((shards, rows), 0)).astype(F32) for c in range(cands)]
    hot = jnp.concatenate(hot, axis=1).astype(BF16)
    high, middle, low = parts_of(got[...], 3)
    lines = dot(low, hot, 0, 0) + dot(middle, hot, 0, 0) + dot(high, hot, 0, 0)
    for c in range(cands):
        here = rank[c : c + 1] == iota((capacity, rows), 0)
        out_ref[c : c + 1, :] = jnp.sum(jnp.where(here, lines[:, c * rows : (c + 1) * rows], 0.0), axis=0, keepdims=True)


def place_kernel(place_ref, got_ref, out_ref):
    blocks, probes = place_ref.shape
    _, block_rows, page_rows = got_ref.shape
    for b in range(blocks):
        for p in range(probes):
            out_ref[b * block_rows : (b + 1) * block_rows, p * page_rows : (p + 1) * page_rows] = got_ref[place_ref[b, p]]


def exchange(x, mask, shards):
    return lax.ppermute(x, "idx", [(i, i ^ mask) for i in range(shards)])


def planes(x, shards):
    along = {mask: exchange(x, mask, shards) if mask else x for mask in range(0, shards, 4)}
    return along, lambda: {mask ^ 2: exchange(along[mask], 2, shards) for mask in along}


def body(queries, rotation, codes, vectors, probes, cand_pages, cand_rows):
    shards = lax.axis_size("idx")
    me = lax.axis_index("idx").astype(I32).reshape(1)
    query_rows, full_width = queries.shape
    page_count, page_rows, proj_width = codes.shape
    block_count, probe_count = probes.shape
    block_rows = query_rows // block_count
    cand_count = cand_pages.shape[1]
    slot_count = block_count * probe_count
    capacity = 2 * slot_count // shards
    row_capacity = 2 * query_rows * cand_count // shards
    rest = full_width - proj_width
    assert proj_width == 2 * LANES and rest % proj_width == 0 and row_capacity <= LANES
    assert 4 * shards <= LANES and block_count * page_count <= 256 and query_rows <= 256 and page_rows <= 256

    chunk_rows = query_rows + 2 * shards
    chunk, tail, probe_place, cand_place = pl.pallas_call(
        functools.partial(plan_kernel, shards, page_count),
        in_specs=[whole(HBM)] * 5,
        out_specs=[whole(VMEM)] * 4,
        out_shape=[
            jax.ShapeDtypeStruct((chunk_rows, proj_width), BF16),
            jax.ShapeDtypeStruct((query_rows, rest), BF16),
            jax.ShapeDtypeStruct((block_count, probe_count), I32),
            jax.ShapeDtypeStruct((2 * cand_count, query_rows), I32),
        ],
        scratch_shapes=[
            pltpu.VMEM(queries.shape, BF16),
            pltpu.VMEM((full_width // proj_width, full_width, proj_width), F32),
            pltpu.VMEM(probes.shape, I32),
            pltpu.VMEM((cand_count, query_rows), I32),
            pltpu.VMEM((cand_count, query_rows), I32),
            pltpu.SemaphoreType.DMA((4 + full_width // proj_width,)),
        ],
        compiler_params=params(61 * MIB),
        cost_estimate=cost(2),
        name="plan",
    )(queries, rotation, probes, cand_pages.T, cand_rows.T)
    order = tuple(range(0, shards, 2))
    other = tuple(m ^ 1 for m in order)

    def stack(parts, waits, name):
        return pl.pallas_call(
            functools.partial(stack_kernel, len(waits)),
            in_specs=[whole(ANY)] * len(waits) + [whole(VMEM)] * len(parts),
            out_specs=whole(VMEM),
            out_shape=jax.ShapeDtypeStruct((len(parts), *parts[0].shape), BF16),
            compiler_params=params(10 * MIB),
            cost_estimate=cost(1),
            name=name,
        )(*waits, *parts)

    def coarse_scores(order, pieces, waits, before):
        count = 3 + len(waits)
        return pl.pallas_call(
            functools.partial(coarse_kernel, shards, order, block_rows),
            in_specs=[whole(SMEM), whole(VMEM), whole(VMEM)] + [whole(ANY)] * len(waits) + [whole(VMEM)] * len(before),
            out_specs=[whole(VMEM), whole(ANY)],
            out_shape=[
                jax.ShapeDtypeStruct((shards, capacity, block_rows, page_rows), BF16),
                jax.ShapeDtypeStruct((2, len(order), LANES), I32),
            ],
            scratch_shapes=[
                pltpu.VMEM((2, len(order), LANES), I32),
                pltpu.VMEM((len(order), LANES), I32),
                pltpu.SMEM((len(order), LANES), I32),
                pltpu.SemaphoreType.DMA((2,)),
            ],
            input_output_aliases={count: 0} if before else {},
            compiler_params=params(10 * MIB),
            cost_estimate=cost(COARSE_COST),
            name="coarse_scores",
        )(me, pieces, codes, *waits, *before)

    along, across = planes(chunk, shards)
    plane = along | across()
    tail_along = {mask: exchange(tail, mask, shards) for mask in range(4, shards, 4)}
    tail_across = {2: exchange(tail, 2, shards)}

    heads_a = stack([plane[m] for m in order], list(tail_along.values()), "stack_heads")
    heads_b = exchange(heads_a, 1, shards)
    scored, list_a = coarse_scores(order, heads_a, [], [])
    scored, list_b = coarse_scores(other, heads_b, [], [scored])
    returned = lax.all_to_all(scored, "idx", split_axis=0, concat_axis=0, tiled=True)

    tail_across |= {mask ^ 2: exchange(x, 2, shards) for mask, x in tail_along.items()}
    tails = {0: tail} | tail_along | tail_across

    flat = vectors.reshape(page_count * page_rows, full_width)
    found = pl.pallas_call(
        gather_kernel,
        in_specs=[whole(ANY)] * 3,
        out_specs=whole(VMEM),
        out_shape=jax.ShapeDtypeStruct((2, len(order), row_capacity, full_width), BF16),
        scratch_shapes=[
            pltpu.SMEM((shards, LANES), I32),
            pltpu.VMEM(flat.shape, F32),
            pltpu.SemaphoreType.DMA((6,)),
        ],
        compiler_params=params(34 * MIB),
        cost_estimate=cost(GATHER_COST),
        name="gather_rows",
    )(list_a, list_b, flat)
    tails_a = stack([tails[m] for m in order], [found], "stack_tails")
    tails_b = exchange(tails_a, 1, shards)

    def scores(part, order, list_ref, heads, tails, before):
        return pl.pallas_call(
            functools.partial(rerank_kernel, part, order),
            in_specs=[whole(ANY)] + [whole(VMEM)] * (3 + len(before)),
            out_specs=whole(VMEM),
            out_shape=jax.ShapeDtypeStruct((shards // 4, 4, row_capacity), F32),
            scratch_shapes=[pltpu.VMEM((len(order), LANES), I32), pltpu.SemaphoreType.DMA],
            compiler_params=params(10 * MIB),
            cost_estimate=cost(RERANK_COST),
            name="rerank_scores",
        )(list_ref, found, heads, tails, *before)

    answers = scores(0, order, list_a, heads_a, tails_a, [])
    answers = scores(1, other, list_b, heads_b, tails_b, [answers])
    own = jnp.stack([exchange(answers[a], 4 * a, shards) if a else answers[a] for a in range(shards // 4)])
    across = exchange(own, 2, shards)
    coarse = pl.pallas_call(
        place_kernel,
        in_specs=[whole(SMEM), whole(VMEM)],
        out_specs=whole(VMEM),
        out_shape=jax.ShapeDtypeStruct((query_rows, probe_count * page_rows), BF16),
        compiler_params=params(10 * MIB),
        cost_estimate=cost(1),
        name="place_scores",
    )(probe_place, returned.reshape(shards * capacity, block_rows, page_rows))
    rerank = pl.pallas_call(
        functools.partial(pick_kernel, shards),
        in_specs=[whole(SMEM)] + [whole(VMEM)] * 5,
        out_specs=whole(VMEM),
        out_shape=jax.ShapeDtypeStruct((cand_count, query_rows), F32),
        scratch_shapes=[pltpu.VMEM((shards, row_capacity), F32)],
        compiler_params=params(10 * MIB),
        cost_estimate=cost(1),
        name="pick_answers",
    )(me, own, across, exchange(own, 1, shards), exchange(across, 1, shards), cand_place).T
    return coarse, rerank


def solution(mesh):
    split = P(("grp", "idx"))
    in_specs = (split, P(), split, split, split, split, split)
    return jax.shard_map(body, mesh=mesh, in_specs=in_specs, out_specs=(split, split), check_vma=False)
```

time: 150 us -> 87.5 us (0.58)
  waiting for transfers between devices: 53.7 us -> 23.5 us
  Pallas kernels: 51.6 us -> 28 us
  local copies, waits for them, and re-layouts: 8.96 us -> 1.87 us
  starting transfers between devices: 34.6 us -> 33 us
    ppermute x36 -> x22, waiting for transfers between devices: 53.7 us -> 23.5 us  [exchange(): return lax.ppermute(x, 'idx', [(i, i ^ mask) for i in range(shards)])]
    pallas_call x4 -> x7, Pallas kernels: 47.3 us -> 21.1 us  [the longest x1 11.8 us: body(): pl.pallas_call(gather_kernel, in_specs=[whole(ANY)] * 3, out_specs=whole(...]
    unnamed x16 -> x12, local copies, waits for them, and re-layouts: 8.96 us -> 1.87 us
    pallas_call x1, Pallas kernels: 1.84 us -> 4.38 us  [body(): pl.pallas_call(functools.partial(plan_kernel, shards, page_count), in_spe...]
    ppermute x36 -> x22, starting transfers between devices: 29.5 us -> 29.1 us  [exchange(): return lax.ppermute(x, 'idx', [(i, i ^ mask) for i in range(shards)])]
  transfers between devices with their start and end apart: 37 -> 23, of which waited for: 13 -> 9; matrix products, arithmetic and copies ran while one was open for 0% -> 0% of each run, Pallas kernels for 28% -> 25%
where the time goes in v3:
time: 87.5 us; the launch traced here: 87.1 us
  starting transfers between devices  33 us (38%)
  Pallas kernels  28 us (32%)
  waiting for transfers between devices  23.5 us (27%)
  local copies, waits for them, and re-layouts  1.87 us (2%)
    ppermute x22, starting transfers between devices, exchange(): return lax.ppermute(x, 'idx', [(i, i ^ mask) for i in range(shards)])  29.1 us
    ppermute x22, waiting for transfers between devices, exchange(): return lax.ppermute(x, 'idx', [(i, i ^ mask) for i in range(shards)])  23.5 us
    pallas_call x1, Pallas kernels, body(): pl.pallas_call(gather_kernel, in_specs=[whole(ANY)] * 3, out_specs=whole(...  11.8 us
    pallas_call x2, Pallas kernels, coarse_scores(): pl.pallas_call(functools.partial(coarse_kernel, shards, order, block_rows...  5.36 us
    pallas_call x1, Pallas kernels, body(): pl.pallas_call(functools.partial(plan_kernel, shards, page_count), in_spe...  4.38 us
    all_to_all x1, starting transfers between devices, body(): lax.all_to_all(scored, 'idx', split_axis=0, concat_axis=0, tiled=True)  3.81 us
    pallas_call x2, Pallas kernels, scores(): pl.pallas_call(functools.partial(rerank_kernel, part, order), in_specs=[w...  2.54 us
    unnamed x12, local copies, waits for them, and re-layouts  1.87 us
  transfers between devices with their start and end apart: 23, of which 9 were waited for; matrix products, arithmetic and copies ran while one was open for 0% of the time, Pallas kernels for 25%

profile of v3, /device:TPU:0, one launch (start us, length us, event | category | flops | bytes accessed | tf_op | source)
XLA Modules:
  0.0 87.1 jit_solution(2111892015992417544)
XLA Ops:
  0.6 4.4 %plan.1 = (bf16[160,256]{1,0:T(8,128)(2,1)}, bf16[128,768]{1,0:T(8,128)(2,1)}, s32[4,16]{1,0:T(4,128)}, s32[16,128]{1,0:T(8,128)}) custom-call(bf16[128,1024]{1,0:T(8,128)(2,1)} %q_hbm.1, f32[1024,1024]{1,0:T(8,128)} %rot_hbm.1, s32[4,16]{1,0:T(4,128)} %probes_hbm.1, s32[8,128]{1,0:T(8,128)} %bitcast.18, s32[8,128]{1,0:T(8,128)} %bitcast.19), custom_call_target="tpu_custom_call" | custom-call | bytes 6000000 | tf_op jit(solution)/shard_map/plan/pallas_call | solution.py:248
  5.0 5.1 %collective-permute-start.8 = (bf16[160,256]{1,0:T(8,128)(2,1)}, bf16[160,256]{1,0:T(8,128)(2,1)S(1)}, u32[]{:S(2)}, u32[]{:S(2)}) collective-permute-start(bf16[160,256]{1,0:T(8,128)(2,1)} %get-tuple-element.12.refs_3_), channel_id=1, source_target_pairs={{0,12},{1,13},{2,14},{3,15},{4,8},{5,9},{6,10},{7,11},{8,4},{9,5},... | collective-permute-start | bytes 245768 | tf_op jit(solution)/shard_map/ppermute | solution.py:224
  10.8 3.7 %collective-permute-start.2 = (bf16[128,768]{1,0:T(8,128)(2,1)}, bf16[128,768]{1,0:T(8,128)(2,1)S(1)}, u32[]{:S(2)}, u32[]{:S(2)}) collective-permute-start(bf16[128,768]{1,0:T(8,128)(2,1)} %get-tuple-element.11.refs_1_), channel_id=1, source_target_pairs={{0,12},{1,13},{2,14},{3,15},{4,8},{5,9},{6,10},{7,11},{8,4},{9,5},... | collective-permute-start | bytes 589832 | tf_op jit(solution)/shard_map/ppermute | solution.py:224
  14.5 3.8 %collective-permute-start = (bf16[128,768]{1,0:T(8,128)(2,1)}, bf16[128,768]{1,0:T(8,128)(2,1)}, u32[]{:S(2)}, u32[]{:S(2)}) collective-permute-start(bf16[128,768]{1,0:T(8,128)(2,1)} %get-tuple-element.11.refs_1_), channel_id=1, source_target_pairs={{0,4},{1,5},{2,6},{3,7},{4,0},{5,1},{6,2},{7,3},{8,12},{9,13},{10,... | collective-permute-start | bytes 589832 | tf_op jit(solution)/shard_map/ppermute | solution.py:224
  18.3 8.1 %collective-permute-done.6.refs_7_ = bf16[160,256]{1,0:T(8,128)(2,1)S(1)} collective-permute-done((bf16[160,256]{1,0:T(8,128)(2,1)}, bf16[160,256]{1,0:T(8,128)(2,1)S(1)}, u32[]{:S(2)}, u32[]{:S(2)}) %collective-permute-start.6) | collective-permute-done | bytes 81952 | tf_op jit(solution)/shard_map/ppermute | solution.py:224
  26.4 1.2 %collective-permute-start.3 = (bf16[160,256]{1,0:T(8,128)(2,1)}, bf16[160,256]{1,0:T(8,128)(2,1)S(1)}, u32[]{:S(2)}, u32[]{:S(2)}) collective-permute-start(bf16[160,256]{1,0:T(8,128)(2,1)} %get-tuple-element.12.refs_3_), channel_id=1, source_target_pairs={{0,2},{1,3},{2,0},{3,1},{4,6},{5,7},{6,4},{7,5},{8,10},{9,11},{10,... | collective-permute-start | bytes 245768 | tf_op jit(solution)/shard_map/ppermute | solution.py:224
  27.6 0.8 collective-permute-start.9
  28.4 3.1 %collective-permute-done.3.refs_4_ = bf16[160,256]{1,0:T(8,128)(2,1)S(1)} collective-permute-done((bf16[160,256]{1,0:T(8,128)(2,1)}, bf16[160,256]{1,0:T(8,128)(2,1)S(1)}, u32[]{:S(2)}, u32[]{:S(2)}) %collective-permute-start.3) | collective-permute-done | bytes 81952 | tf_op jit(solution)/shard_map/ppermute | solution.py:224
  31.5 1.6 %collective-permute-start.7 = (bf16[160,256]{1,0:T(8,128)(2,1)S(1)}, bf16[160,256]{1,0:T(8,128)(2,1)S(1)}, u32[]{:S(2)}, u32[]{:S(2)}) collective-permute-start(bf16[160,256]{1,0:T(8,128)(2,1)S(1)} %collective-permute-done.6.refs_7_), channel_id=1, source_target_pairs={{0,2},{1,3},{2,0},{3,1},{4,6},{5,7},{6,4},{7,5},{8,10},{9,11},{10,... | collective-permute-start | bytes 245768 | tf_op jit(solution)/shard_map/ppermute | solution.py:224
  33.1 1.5 %collective-permute-start.5 = (bf16[160,256]{1,0:T(8,128)(2,1)S(1)}, bf16[160,256]{1,0:T(8,128)(2,1)S(1)}, u32[]{:S(2)}, u32[]{:S(2)}) collective-permute-start(bf16[160,256]{1,0:T(8,128)(2,1)S(1)} %collective-permute-done.4.refs_5_), channel_id=1, source_target_pairs={{0,2},{1,3},{2,0},{3,1},{4,6},{5,7},{6,4},{7,5},{8,10},{9,11},{10,... | collective-permute-start | bytes 245768 | tf_op jit(solution)/shard_map/ppermute | solution.py:224
  34.7 1.3 %collective-permute-done.7.refs_8_ = bf16[160,256]{1,0:T(8,128)(2,1)S(1)} collective-permute-done((bf16[160,256]{1,0:T(8,128)(2,1)S(1)}, bf16[160,256]{1,0:T(8,128)(2,1)S(1)}, u32[]{:S(2)}, u32[]{:S(2)}) %collective-permute-start.7) | collective-permute-done | bytes 81952 | tf_op jit(solution)/shard_map/ppermute | solution.py:224
  35.9 1.6 %collective-permute-done.5.refs_6_ = bf16[160,256]{1,0:T(8,128)(2,1)S(1)} collective-permute-done((bf16[160,256]{1,0:T(8,128)(2,1)S(1)}, bf16[160,256]{1,0:T(8,128)(2,1)S(1)}, u32[]{:S(2)}, u32[]{:S(2)}) %collective-permute-start.5) | collective-permute-done | bytes 81952 | tf_op jit(solution)/shard_map/ppermute | solution.py:224
  37.6 0.9 %copy-done.3 = bf16[160,256]{1,0:T(8,128)(2,1)S(1)} copy-done((bf16[160,256]{1,0:T(8,128)(2,1)S(1)}, bf16[160,256]{1,0:T(8,128)(2,1)}, u32[]{:S(2)}) %copy-start.3) | copy-done | bytes 81944
  38.6 1.6 %collective-permute-start.11 = (bf16[128,768]{1,0:T(8,128)(2,1)}, bf16[128,768]{1,0:T(8,128)(2,1)S(1)}, u32[]{:S(2)}, u32[]{:S(2)}) collective-permute-start(bf16[128,768]{1,0:T(8,128)(2,1)} %get-tuple-element.11.refs_1_), channel_id=1, source_target_pairs={{0,2},{1,3},{2,0},{3,1},{4,6},{5,7},{6,4},{7,5},{8,10},{9,11},{10,... | collective-permute-start | bytes 589832 | tf_op jit(solution)/shard_map/ppermute | solution.py:224
  40.7 1.5 %collective-permute-start.13 = (bf16[128,768]{1,0:T(8,128)(2,1)}, bf16[128,768]{1,0:T(8,128)(2,1)}, u32[]{:S(2)}, u32[]{:S(2)}) collective-permute-start(bf16[128,768]{1,0:T(8,128)(2,1)} %collective-permute-done.1.refs_1_.refs_5_), channel_id=1, source_target_pairs={{0,2},{1,3},{2,0},{3,1},{4,6},{5,7},{6,4},{7,5},{8,10},{9,11},{10,... | collective-permute-start | bytes 589832 | tf_op jit(solution)/shard_map/ppermute | solution.py:224
  42.7 2.1 %coarse_scores.2 = (bf16[16,8,32,128]{3,2,1,0:T(8,128)(2,1)S(1)}, s32[2,8,128]{2,1,0:T(8,128)S(1)}) custom-call(s32[1]{0:T(128)} %bitcast.2.me_ref, bf16[8,160,256]{2,1,0:T(8,128)(2,1)S(1)} %stack_heads.1.pieces.heads_ref, bf16[32,128,256]{2,1,0:T(8,128)(2,1)S(1)} %copy-done), custom_call_target="tpu_custom_call" | custom-call | bytes 9000000 | tf_op jit(solution)/shard_map/coarse_scores/pallas_call | solution.py:286
  44.9 3.2 %coarse_scores.3 = (bf16[16,8,32,128]{3,2,1,0:T(8,128)(2,1)S(1)}, s32[2,8,128]{2,1,0:T(8,128)S(1)}) custom-call(s32[1]{0:T(128)} %bitcast.2.me_ref, bf16[8,160,256]{2,1,0:T(8,128)(2,1)} %collective-permute-done.10.pieces.heads_ref, bf16[32,128,256]{2,1,0:T(8,128)(2,1)S(1)} %copy-done, ...), custom_call_target="tpu_custom_call", output_to_operand_aliasing={{0}: (3, {})} | custom-call | bytes 9000000 | tf_op jit(solution)/shard_map/coarse_scores/pallas_call | solution.py:286
  48.1 1.0 %copy-done.1 = bf16[16,8,32,128]{3,2,1,0:T(8,128)(2,1)} copy-done((bf16[16,8,32,128]{3,2,1,0:T(8,128)(2,1)}, bf16[16,8,32,128]{3,2,1,0:T(8,128)(2,1)S(1)}, u32[]{:S(2)}) %copy-start.1) | copy-done | bytes 1048600
  49.1 3.8 %all-to-all-start = ((bf16[16,8,32,128]{3,2,1,0:T(8,128)(2,1)}), bf16[16,8,32,128]{3,2,1,0:T(8,128)(2,1)S(1)}, u32[]{:S(2)}, u32[]{:S(2)}) async-start(bf16[16,8,32,128]{3,2,1,0:T(8,128)(2,1)} %copy-done.1), calls=%async_computation | async-start | bytes 2097152 | tf_op jit(solution)/shard_map/all_to_all | solution.py:315
  52.9 11.8 %gather_rows.1.refs_0_.rows_ref = bf16[2,8,128,1024]{3,2,1,0:T(8,128)(2,1)S(1)} custom-call(s32[2,8,128]{2,1,0:T(8,128)S(1)} %get-tuple-element.16.list_a.list_ref, s32[2,8,128]{2,1,0:T(8,128)S(1)} %get-tuple-element.15.list_b.list_ref, f32[4096,1024]{1,0:T(8,128)} %bitcast.16), custom_call_target="tpu_custom_call" | custom-call | bytes 36000000 | tf_op jit(solution)/shard_map/gather_rows/pallas_call | solution.py:321
  64.8 1.4 %stack_tails.1.tails_ref = bf16[8,128,768]{2,1,0:T(8,128)(2,1)S(1)} custom-call(bf16[2,8,128,1024]{3,2,1,0:T(8,128)(2,1)S(1)} %gather_rows.1.refs_0_.rows_ref, bf16[128,768]{1,0:T(8,128)(2,1)S(1)} %copy-done.2, bf16[128,768]{1,0:T(8,128)(2,1)S(1)} %collective-permute-done.11.refs_2_, bf16[128,768]{1,0:T(8,128)(2,1)} %collective-permute-done.refs_0_.refs_3_, ...), custom_call_target="tpu_custom_call" | custom-call | bytes 3000000 | tf_op jit(solution)/shard_map/stack_tails/pallas_call | solution.py:274
  66.6 0.7 rerank_scores.2.refs_0_
  67.4 2.3 %collective-permute-done.15.tails_ref = bf16[8,128,768]{2,1,0:T(8,128)(2,1)S(1)} collective-permute-done((bf16[8,128,768]{2,1,0:T(8,128)(2,1)S(1)}, bf16[8,128,768]{2,1,0:T(8,128)(2,1)S(1)}, u32[]{:S(2)}, u32[]{:S(2)}) %collective-permute-start.15) | collective-permute-done | bytes 1572896 | tf_op jit(solution)/shard_map/ppermute | solution.py:224
  69.7 1.8 %rerank_scores.3 = f32[4,4,128]{2,1,0:T(4,128)S(1)} custom-call(s32[2,8,128]{2,1,0:T(8,128)S(1)} %get-tuple-element.15.list_b.list_ref, bf16[2,8,128,1024]{3,2,1,0:T(8,128)(2,1)S(1)} %gather_rows.1.refs_0_.rows_ref, bf16[8,160,256]{2,1,0:T(8,128)(2,1)} %collective-permute-done.10.pieces.heads_ref, ...), custom_call_target="tpu_custom_call" | custom-call | bytes 3000000 | tf_op jit(solution)/shard_map/rerank_scores/pallas_call | solution.py:339
  71.5 3.8 %collective-permute-start.18 = (f32[4,128]{1,0:T(4,128)S(1)}, f32[4,128]{1,0:T(4,128)S(1)}, u32[]{:S(2)}, u32[]{:S(2)}) collective-permute-start(f32[4,128]{1,0:T(4,128)S(1)} %get-tuple-element.19), channel_id=1, source_target_pairs={{0,12},{1,13},{2,14},{3,15},{4,8},{5,9},{6,10},{7,11},{8,4},{9,5},... | collective-permute-start | bytes 6152 | tf_op jit(solution)/shard_map/ppermute | solution.py:224
  76.0 1.1 %collective-permute-done.18 = f32[4,128]{1,0:T(4,128)S(1)} collective-permute-done((f32[4,128]{1,0:T(4,128)S(1)}, f32[4,128]{1,0:T(4,128)S(1)}, u32[]{:S(2)}, u32[]{:S(2)}) %collective-permute-start.18) | collective-permute-done | bytes 2080 | tf_op jit(solution)/shard_map/ppermute | solution.py:224
  77.1 2.7 %collective-permute-done.17 = f32[4,128]{1,0:T(4,128)S(1)} collective-permute-done((f32[4,128]{1,0:T(4,128)S(1)}, f32[4,128]{1,0:T(4,128)S(1)}, u32[]{:S(2)}, u32[]{:S(2)}) %collective-permute-start.17) | collective-permute-done | bytes 2080 | tf_op jit(solution)/shard_map/ppermute | solution.py:224
  79.7 1.5 %collective-permute-start.19 = (f32[4,4,128]{2,1,0:T(4,128)S(1)}, f32[4,4,128]{2,1,0:T(4,128)S(1)}, u32[]{:S(2)}, u32[]{:S(2)}) collective-permute-start(f32[4,4,128]{2,1,0:T(4,128)S(1)} %pad_maximum_fusion.own_ref), channel_id=1, source_target_pairs={{0,2},{1,3},{2,0},{3,1},{4,6},{5,7},{6,4},{7,5},{8,10},{9,11},{10,... | collective-permute-start | bytes 24584 | tf_op jit(solution)/shard_map/ppermute | solution.py:224
  81.3 2.2 %collective-permute-done.19.y_ref = f32[4,4,128]{2,1,0:T(4,128)S(1)} collective-permute-done((f32[4,4,128]{2,1,0:T(4,128)S(1)}, f32[4,4,128]{2,1,0:T(4,128)S(1)}, u32[]{:S(2)}, u32[]{:S(2)}) %collective-permute-start.19) | collective-permute-done | bytes 8224 | tf_op jit(solution)/shard_map/ppermute | solution.py:224
  83.5 1.2 %collective-permute-done.21.both_ref = f32[4,4,128]{2,1,0:T(4,128)S(1)} collective-permute-done((f32[4,4,128]{2,1,0:T(4,128)S(1)}, f32[4,4,128]{2,1,0:T(4,128)S(1)}, u32[]{:S(2)}, u32[]{:S(2)}) %collective-permute-start.21) | collective-permute-done | bytes 8224 | tf_op jit(solution)/shard_map/ppermute | solution.py:224
  84.6 1.0 %pick_answers.1 = f32[8,128]{1,0:T(8,128)} custom-call(s32[1]{0:T(128)} %bitcast.2.me_ref, f32[4,4,128]{2,1,0:T(4,128)S(1)} %pad_maximum_fusion.own_ref, f32[4,4,128]{2,1,0:T(4,128)S(1)} %collective-permute-done.19.y_ref, f32[4,4,128]{2,1,0:T(4,128)S(1)} %collective-permute-done.20.core_ref, f32[4,4,128]{2,1,0:T(4,128)S(1)} %collective-permute-done.21.both_ref, ...), custom_call_target="tpu_custom_call" | custom-call | bytes 3000000 | tf_op jit(solution)/shard_map/pick_answers/pallas_call | solution.py:363
  85.6 1.5 %place_scores.1 = bf16[128,2048]{1,0:T(8,128)(2,1)} custom-call(s32[4,16]{1,0:T(4,128)S(1)} %copy-done.5, bf16[128,32,128]{2,1,0:T(8,128)(2,1)S(1)} %bitcast.15), custom_call_target="tpu_custom_call" | custom-call | bytes 3000000 | tf_op jit(solution)/shard_map/place_scores/pallas_call | solution.py:354
  (38 shorter events, 3.0 us)
Async XLA Ops:
  0.6 42.1 %copy-start = (bf16[32,128,256]{2,1,0:T(8,128)(2,1)S(1)}, bf16[32,128,256]{2,1,0:T(8,128)(2,1)}, u32[]{:S(2)}) copy-start(bf16[32,128,256]{2,1,0:T(8,128)(2,1)} %codes.3) | copy-start | bytes 6291460
  5.0 9.5 %collective-permute-start.8 = (bf16[160,256]{1,0:T(8,128)(2,1)}, bf16[160,256]{1,0:T(8,128)(2,1)S(1)}, u32[]{:S(2)}, u32[]{:S(2)}) collective-permute-start(bf16[160,256]{1,0:T(8,128)(2,1)} %get-tuple-element.12.refs_3_), channel_id=1, source_target_pairs={{0,12},{1,13},{2,14},{3,15},{4,8},{5,9},{6,10},{7,11},{8,4},{9,5},... | collective-permute-start | bytes 245768 | tf_op jit(solution)/shard_map/ppermute | solution.py:224
  10.2 16.2 %collective-permute-start.6 = (bf16[160,256]{1,0:T(8,128)(2,1)}, bf16[160,256]{1,0:T(8,128)(2,1)S(1)}, u32[]{:S(2)}, u32[]{:S(2)}) collective-permute-start(bf16[160,256]{1,0:T(8,128)(2,1)} %get-tuple-element.12.refs_3_), channel_id=1, source_target_pairs={{0,8},{1,9},{2,10},{3,11},{4,12},{5,13},{6,14},{7,15},{8,0},{9,1},... | collective-permute-start | bytes 245768 | tf_op jit(solution)/shard_map/ppermute | solution.py:224
  10.2 17.5 %collective-permute-start.4 = (bf16[160,256]{1,0:T(8,128)(2,1)}, bf16[160,256]{1,0:T(8,128)(2,1)S(1)}, u32[]{:S(2)}, u32[]{:S(2)}) collective-permute-start(bf16[160,256]{1,0:T(8,128)(2,1)} %get-tuple-element.12.refs_3_), channel_id=1, source_target_pairs={{0,4},{1,5},{2,6},{3,7},{4,0},{5,1},{6,2},{7,3},{8,12},{9,13},{10,... | collective-permute-start | bytes 245768 | tf_op jit(solution)/shard_map/ppermute | solution.py:224
  10.8 26.8 %collective-permute-start.2 = (bf16[128,768]{1,0:T(8,128)(2,1)}, bf16[128,768]{1,0:T(8,128)(2,1)S(1)}, u32[]{:S(2)}, u32[]{:S(2)}) collective-permute-start(bf16[128,768]{1,0:T(8,128)(2,1)} %get-tuple-element.11.refs_1_), channel_id=1, source_target_pairs={{0,12},{1,13},{2,14},{3,15},{4,8},{5,9},{6,10},{7,11},{8,4},{9,5},... | collective-permute-start | bytes 589832 | tf_op jit(solution)/shard_map/ppermute | solution.py:224
  14.5 23.0 %collective-permute-start.1 = (bf16[128,768]{1,0:T(8,128)(2,1)}, bf16[128,768]{1,0:T(8,128)(2,1)}, u32[]{:S(2)}, u32[]{:S(2)}) collective-permute-start(bf16[128,768]{1,0:T(8,128)(2,1)} %get-tuple-element.11.refs_1_), channel_id=1, source_target_pairs={{0,8},{1,9},{2,10},{3,11},{4,12},{5,13},{6,14},{7,15},{8,0},{9,1},... | collective-permute-start | bytes 589832 | tf_op jit(solution)/shard_map/ppermute | solution.py:224
  14.5 23.0 %collective-permute-start = (bf16[128,768]{1,0:T(8,128)(2,1)}, bf16[128,768]{1,0:T(8,128)(2,1)}, u32[]{:S(2)}, u32[]{:S(2)}) collective-permute-start(bf16[128,768]{1,0:T(8,128)(2,1)} %get-tuple-element.11.refs_1_), channel_id=1, source_target_pairs={{0,4},{1,5},{2,6},{3,7},{4,0},{5,1},{6,2},{7,3},{8,12},{9,13},{10,... | collective-permute-start | bytes 589832 | tf_op jit(solution)/shard_map/ppermute | solution.py:224
  26.4 5.1 %collective-permute-start.3 = (bf16[160,256]{1,0:T(8,128)(2,1)}, bf16[160,256]{1,0:T(8,128)(2,1)S(1)}, u32[]{:S(2)}, u32[]{:S(2)}) collective-permute-start(bf16[160,256]{1,0:T(8,128)(2,1)} %get-tuple-element.12.refs_3_), channel_id=1, source_target_pairs={{0,2},{1,3},{2,0},{3,1},{4,6},{5,7},{6,4},{7,5},{8,10},{9,11},{10,... | collective-permute-start | bytes 245768 | tf_op jit(solution)/shard_map/ppermute | solution.py:224
  27.6 5.5 %collective-permute-start.9 = (bf16[160,256]{1,0:T(8,128)(2,1)S(1)}, bf16[160,256]{1,0:T(8,128)(2,1)S(1)}, u32[]{:S(2)}, u32[]{:S(2)}) collective-permute-start(bf16[160,256]{1,0:T(8,128)(2,1)S(1)} %collective-permute-done.8.refs_9_), channel_id=1, source_target_pairs={{0,2},{1,3},{2,0},{3,1},{4,6},{5,7},{6,4},{7,5},{8,10},{9,11},{10,... | collective-permute-start | bytes 245768 | tf_op jit(solution)/shard_map/ppermute | solution.py:224
  31.5 4.4 %collective-permute-start.7 = (bf16[160,256]{1,0:T(8,128)(2,1)S(1)}, bf16[160,256]{1,0:T(8,128)(2,1)S(1)}, u32[]{:S(2)}, u32[]{:S(2)}) collective-permute-start(bf16[160,256]{1,0:T(8,128)(2,1)S(1)} %collective-permute-done.6.refs_7_), channel_id=1, source_target_pairs={{0,2},{1,3},{2,0},{3,1},{4,6},{5,7},{6,4},{7,5},{8,10},{9,11},{10,... | collective-permute-start | bytes 245768 | tf_op jit(solution)/shard_map/ppermute | solution.py:224
  33.1 4.4 %collective-permute-start.5 = (bf16[160,256]{1,0:T(8,128)(2,1)S(1)}, bf16[160,256]{1,0:T(8,128)(2,1)S(1)}, u32[]{:S(2)}, u32[]{:S(2)}) collective-permute-start(bf16[160,256]{1,0:T(8,128)(2,1)S(1)} %collective-permute-done.4.refs_5_), channel_id=1, source_target_pairs={{0,2},{1,3},{2,0},{3,1},{4,6},{5,7},{6,4},{7,5},{8,10},{9,11},{10,... | collective-permute-start | bytes 245768 | tf_op jit(solution)/shard_map/ppermute | solution.py:224
  37.6 0.9 %copy-start.3 = (bf16[160,256]{1,0:T(8,128)(2,1)S(1)}, bf16[160,256]{1,0:T(8,128)(2,1)}, u32[]{:S(2)}) copy-start(bf16[160,256]{1,0:T(8,128)(2,1)} %get-tuple-element.12.refs_3_) | copy-start | bytes 245764
  38.5 6.3 %collective-permute-start.10 = (bf16[8,160,256]{2,1,0:T(8,128)(2,1)S(1)}, bf16[8,160,256]{2,1,0:T(8,128)(2,1)}, u32[]{:S(2)}, u32[]{:S(2)}) collective-permute-start(bf16[8,160,256]{2,1,0:T(8,128)(2,1)S(1)} %stack_heads.1.pieces.heads_ref), channel_id=1, source_target_pairs={{0,1},{1,0},{2,3},{3,2},{4,5},{5,4},{6,7},{7,6},{8,9},{9,8},{10,11... | collective-permute-start | bytes 1966088 | tf_op jit(solution)/shard_map/ppermute | solution.py:224
  38.6 26.1 %collective-permute-start.11 = (bf16[128,768]{1,0:T(8,128)(2,1)}, bf16[128,768]{1,0:T(8,128)(2,1)S(1)}, u32[]{:S(2)}, u32[]{:S(2)}) collective-permute-start(bf16[128,768]{1,0:T(8,128)(2,1)} %get-tuple-element.11.refs_1_), channel_id=1, source_target_pairs={{0,2},{1,3},{2,0},{3,1},{4,6},{5,7},{6,4},{7,5},{8,10},{9,11},{10,... | collective-permute-start | bytes 589832 | tf_op jit(solution)/shard_map/ppermute | solution.py:224
  40.2 24.5 %collective-permute-start.14 = (bf16[128,768]{1,0:T(8,128)(2,1)S(1)}, bf16[128,768]{1,0:T(8,128)(2,1)}, u32[]{:S(2)}, u32[]{:S(2)}) collective-permute-start(bf16[128,768]{1,0:T(8,128)(2,1)S(1)} %collective-permute-done.2.refs_2_.refs_7_), channel_id=1, source_target_pairs={{0,2},{1,3},{2,0},{3,1},{4,6},{5,7},{6,4},{7,5},{8,10},{9,11},{10,... | collective-permute-start | bytes 589832 | tf_op jit(solution)/shard_map/ppermute | solution.py:224
  40.7 24.0 %collective-permute-start.13 = (bf16[128,768]{1,0:T(8,128)(2,1)}, bf16[128,768]{1,0:T(8,128)(2,1)}, u32[]{:S(2)}, u32[]{:S(2)}) collective-permute-start(bf16[128,768]{1,0:T(8,128)(2,1)} %collective-permute-done.1.refs_1_.refs_5_), channel_id=1, source_target_pairs={{0,2},{1,3},{2,0},{3,1},{4,6},{5,7},{6,4},{7,5},{8,10},{9,11},{10,... | collective-permute-start | bytes 589832 | tf_op jit(solution)/shard_map/ppermute | solution.py:224
  42.2 22.5 %collective-permute-start.12 = (bf16[128,768]{1,0:T(8,128)(2,1)}, bf16[128,768]{1,0:T(8,128)(2,1)}, u32[]{:S(2)}, u32[]{:S(2)}) collective-permute-start(bf16[128,768]{1,0:T(8,128)(2,1)} %collective-permute-done.refs_0_.refs_3_), channel_id=1, source_target_pairs={{0,2},{1,3},{2,0},{3,1},{4,6},{5,7},{6,4},{7,5},{8,10},{9,11},{10,... | collective-permute-start | bytes 589832 | tf_op jit(solution)/shard_map/ppermute | solution.py:224
  48.1 1.0 %copy-start.1 = (bf16[16,8,32,128]{3,2,1,0:T(8,128)(2,1)}, bf16[16,8,32,128]{3,2,1,0:T(8,128)(2,1)S(1)}, u32[]{:S(2)}) copy-start(bf16[16,8,32,128]{3,2,1,0:T(8,128)(2,1)S(1)} %get-tuple-element.14) | copy-start | bytes 3145732
  49.1 36.5 %all-to-all-start = ((bf16[16,8,32,128]{3,2,1,0:T(8,128)(2,1)}), bf16[16,8,32,128]{3,2,1,0:T(8,128)(2,1)S(1)}, u32[]{:S(2)}, u32[]{:S(2)}) async-start(bf16[16,8,32,128]{3,2,1,0:T(8,128)(2,1)} %copy-done.1), calls=%async_computation | async-start | bytes 2097152 | tf_op jit(solution)/shard_map/all_to_all | solution.py:315
  52.9 11.8 %copy-start.2 = (bf16[128,768]{1,0:T(8,128)(2,1)S(1)}, bf16[128,768]{1,0:T(8,128)(2,1)}, u32[]{:S(2)}) copy-start(bf16[128,768]{1,0:T(8,128)(2,1)} %get-tuple-element.11.refs_1_) | copy-start | bytes 589828
  66.1 3.5 %collective-permute-start.15 = (bf16[8,128,768]{2,1,0:T(8,128)(2,1)S(1)}, bf16[8,128,768]{2,1,0:T(8,128)(2,1)S(1)}, u32[]{:S(2)}, u32[]{:S(2)}) collective-permute-start(bf16[8,128,768]{2,1,0:T(8,128)(2,1)S(1)} %stack_tails.1.tails_ref), channel_id=1, source_target_pairs={{0,1},{1,0},{2,3},{3,2},{4,5},{5,4},{6,7},{7,6},{8,9},{9,8},{10,11... | collective-permute-start | bytes 4718600 | tf_op jit(solution)/shard_map/ppermute | solution.py:224
  67.4 17.3 %copy-start.4 = (s32[16,128]{1,0:T(8,128)S(1)}, s32[16,128]{1,0:T(8,128)}, u32[]{:S(2)}) copy-start(s32[16,128]{1,0:T(8,128)} %get-tuple-element.17.place_ref) | copy-start | bytes 24580
  67.4 18.3 %copy-start.5 = (s32[4,16]{1,0:T(4,128)S(1)}, s32[4,16]{1,0:T(4,128)}, u32[]{:S(2)}) copy-start(s32[4,16]{1,0:T(4,128)} %get-tuple-element.10.place_ref) | copy-start | bytes 772
  71.5 5.6 %collective-permute-start.18 = (f32[4,128]{1,0:T(4,128)S(1)}, f32[4,128]{1,0:T(4,128)S(1)}, u32[]{:S(2)}, u32[]{:S(2)}) collective-permute-start(f32[4,128]{1,0:T(4,128)S(1)} %get-tuple-element.19), channel_id=1, source_target_pairs={{0,12},{1,13},{2,14},{3,15},{4,8},{5,9},{6,10},{7,11},{8,4},{9,5},... | collective-permute-start | bytes 6152 | tf_op jit(solution)/shard_map/ppermute | solution.py:224
  75.2 4.5 %collective-permute-start.17 = (f32[4,128]{1,0:T(4,128)S(1)}, f32[4,128]{1,0:T(4,128)S(1)}, u32[]{:S(2)}, u32[]{:S(2)}) collective-permute-start(f32[4,128]{1,0:T(4,128)S(1)} %get-tuple-element.20), channel_id=1, source_target_pairs={{0,8},{1,9},{2,10},{3,11},{4,12},{5,13},{6,14},{7,15},{8,0},{9,1},... | collective-permute-start | bytes 6152 | tf_op jit(solution)/shard_map/ppermute | solution.py:224
  75.3 4.5 %collective-permute-start.16 = (f32[4,128]{1,0:T(4,128)S(1)}, f32[4,128]{1,0:T(4,128)S(1)}, u32[]{:S(2)}, u32[]{:S(2)}) collective-permute-start(f32[4,128]{1,0:T(4,128)S(1)} %get-tuple-element.21), channel_id=1, source_target_pairs={{0,4},{1,5},{2,6},{3,7},{4,0},{5,1},{6,2},{7,3},{8,12},{9,13},{10,... | collective-permute-start | bytes 6152 | tf_op jit(solution)/shard_map/ppermute | solution.py:224
  79.7 3.7 %collective-permute-start.19 = (f32[4,4,128]{2,1,0:T(4,128)S(1)}, f32[4,4,128]{2,1,0:T(4,128)S(1)}, u32[]{:S(2)}, u32[]{:S(2)}) collective-permute-start(f32[4,4,128]{2,1,0:T(4,128)S(1)} %pad_maximum_fusion.own_ref), channel_id=1, source_target_pairs={{0,2},{1,3},{2,0},{3,1},{4,6},{5,7},{6,4},{7,5},{8,10},{9,11},{10,... | collective-permute-start | bytes 24584 | tf_op jit(solution)/shard_map/ppermute | solution.py:224
  81.3 2.2 %collective-permute-start.20 = (f32[4,4,128]{2,1,0:T(4,128)S(1)}, f32[4,4,128]{2,1,0:T(4,128)S(1)}, u32[]{:S(2)}, u32[]{:S(2)}) collective-permute-start(f32[4,4,128]{2,1,0:T(4,128)S(1)} %pad_maximum_fusion.own_ref), channel_id=1, source_target_pairs={{0,1},{1,0},{2,3},{3,2},{4,5},{5,4},{6,7},{7,6},{8,9},{9,8},{10,11... | collective-permute-start | bytes 24584 | tf_op jit(solution)/shard_map/ppermute | solution.py:224
  83.5 1.2 %collective-permute-start.21 = (f32[4,4,128]{2,1,0:T(4,128)S(1)}, f32[4,4,128]{2,1,0:T(4,128)S(1)}, u32[]{:S(2)}, u32[]{:S(2)}) collective-permute-start(f32[4,4,128]{2,1,0:T(4,128)S(1)} %collective-permute-done.19.y_ref), channel_id=1, source_target_pairs={{0,1},{1,0},{2,3},{3,2},{4,5},{5,4},{6,7},{7,6},{8,9},{9,8},{10,11... | collective-permute-start | bytes 24584 | tf_op jit(solution)/shard_map/ppermute | solution.py:224

commit v4 on v3

--- a/solution.py
+++ b/solution.py
@@ -9,6 +9,7 @@
 
 LANES = 128
 MIB = 1 << 20
+TAIL_MIB = 58
 COARSE_COST, GATHER_COST, RERANK_COST = 3, 12, 1
 F32, BF16, I32 = jnp.float32, jnp.bfloat16, jnp.int32
 VMEM, SMEM, HBM, ANY = pltpu.VMEM, pltpu.SMEM, pltpu.HBM, pl.ANY
@@ -78,13 +79,11 @@
     return total
 
 
-def plan_kernel(shards, page_count, q_hbm, rot_hbm, probes_hbm, pages_hbm, rows_hbm, chunk_ref, tail_ref, probe_ref, place_ref, q_ref, held, probes_ref, pages_ref, rows_ref, sems):
+def plan_kernel(shards, page_count, q_hbm, rot_hbm, probes_hbm, pages_hbm, rows_hbm, chunk_ref, probe_ref, place_ref, q_ref, held, probes_ref, pages_ref, rows_ref, sems):
     cands, rows = pages_ref.shape
     blocks, probes = probes_ref.shape
-    width = chunk_ref.shape[1]
-    count = held.shape[0]
     pairs = [(pages_hbm, pages_ref), (rows_hbm, rows_ref), (probes_hbm, probes_ref), (q_hbm, q_ref)]
-    pairs += [(rot_hbm.at[:, pl.ds(i * width, width)], held.at[i]) for i in range(count)]
+    pairs.append((rot_hbm.at[:, pl.ds(0, held.shape[1])], held))
     copies = [pltpu.make_async_copy(source, target, sems.at[i]) for i, (source, target) in enumerate(pairs)]
     for copy in copies:
         copy.start()
@@ -109,19 +108,32 @@
     chunk_ref[rows:, :LANES] = table[: 2 * shards]
     chunk_ref[rows:, LANES : 2 * LANES] = table[2 * shards : 4 * shards]
     copies[3].wait()
+    copies[4].wait()
+    chunk_ref[:rows, :] = rotate(q_ref[...], held[...]).astype(BF16)
+
+
+def tail_kernel(q_hbm, rot_hbm, tail_ref, q_ref, held, sems):
+    count, _, width = held.shape
+    copies = [pltpu.make_async_copy(q_hbm, q_ref, sems.at[count])]
+    copies += [
+        pltpu.make_async_copy(rot_hbm.at[:, pl.ds((i + 1) * width, width)], held.at[i], sems.at[i]) for i in range(count)
+    ]
+    for copy in copies:
+        copy.start()
+    copies[0].wait()
     for i in range(count):
-        copies[4 + i].wait()
-        part = rotate(q_ref[...], held[i]).astype(BF16)
-        if i == 0:
-            chunk_ref[:rows, :] = part
-        else:
-            tail_ref[:, (i - 1) * width : i * width] = part
-
-
-def stack_kernel(others, *refs):
-    *parts, out_ref = refs[others:]
-    for i, part in enumerate(parts):
-        out_ref[i] = part[...]
+        copies[1 + i].wait()
+        tail_ref[:, i * width : (i + 1) * width] = rotate(q_ref[...], held[i]).astype(BF16)
+
+
+def stack_kernel(*refs):
+    out_ref = refs[-1]
+    for i in range(out_ref.shape[0]):
+        out_ref[i] = refs[i][...]
+
+
+def relay_kernel(*refs):
+    del refs
 
 
 def coarse_kernel(shards, order, block_rows, me_ref, pieces, codes, *refs):
@@ -180,23 +192,26 @@
             out_ref[m // half, m % half, g : g + 16, :] = jnp.concatenate(halves, axis=0).astype(BF16)
 
 
-def rerank_kernel(part, order, list_ref, rows_ref, heads_ref, tails_ref, *refs):
-    *before, out_ref, query_ref, sem = refs
+def rerank_kernel(part, order, list_ref, rows_ref, heads, *refs):
+    tails, before = refs[0], refs[1:-3]
+    out_ref, query_ref, sem = refs[-3:]
     capacity = rows_ref.shape[2]
-    queries, split = tails_ref.shape[1], heads_ref.shape[2]
+    queries = tails.shape[1]
+    split = heads.shape[2]
     copy = pltpu.make_async_copy(list_ref.at[1], query_ref, sem)
     copy.start()
     if before:
         out_ref[...] = before[0][...]
     copy.wait()
     for p, m in enumerate(order):
-        score = dot(heads_ref[p, :queries, :], rows_ref[part, p, :, :split], 1, 1)
-        score += dot(tails_ref[p], rows_ref[part, p, :, split:], 1, 1)
+        score = dot(heads[p, :queries, :], rows_ref[part, p, :, :split], 1, 1)
+        score += dot(tails[p], rows_ref[part, p, :, split:], 1, 1)
         picked = iota(score.shape, 0) == query_ref[p : p + 1, :capacity]
         out_ref[m // 4, m % 4 : m % 4 + 1, :] = jnp.sum(jnp.where(picked, score, 0.0), axis=0, keepdims=True)
 
 
-def pick_kernel(shards, me_ref, own_ref, y_ref, core_ref, both_ref, place_ref, out_ref, got):
+def pick_kernel(shards, me_ref, own_ref, y_ref, core_ref, both_ref, place_ref, placed_ref, out_ref, got):
+    del placed_ref
     cands, rows = out_ref.shape
     capacity = got.shape[1]
     for a in range(shards // 4):
@@ -212,21 +227,17 @@
         out_ref[c : c + 1, :] = jnp.sum(jnp.where(here, lines[:, c * rows : (c + 1) * rows], 0.0), axis=0, keepdims=True)
 
 
-def place_kernel(place_ref, got_ref, out_ref):
+def place_kernel(place_ref, got_ref, out_ref, done_ref):
     blocks, probes = place_ref.shape
     _, block_rows, page_rows = got_ref.shape
     for b in range(blocks):
         for p in range(probes):
             out_ref[b * block_rows : (b + 1) * block_rows, p * page_rows : (p + 1) * page_rows] = got_ref[place_ref[b, p]]
+    done_ref[...] = jnp.zeros_like(done_ref)
 
 
 def exchange(x, mask, shards):
     return lax.ppermute(x, "idx", [(i, i ^ mask) for i in range(shards)])
-
-
-def planes(x, shards):
-    along = {mask: exchange(x, mask, shards) if mask else x for mask in range(0, shards, 4)}
-    return along, lambda: {mask ^ 2: exchange(along[mask], 2, shards) for mask in along}
 
 
 def body(queries, rotation, codes, vectors, probes, cand_pages, cand_rows):
@@ -245,41 +256,69 @@
     assert 4 * shards <= LANES and block_count * page_count <= 256 and query_rows <= 256 and page_rows <= 256
 
     chunk_rows = query_rows + 2 * shards
-    chunk, tail, probe_place, cand_place = pl.pallas_call(
+    chunk, probe_place, cand_place = pl.pallas_call(
         functools.partial(plan_kernel, shards, page_count),
         in_specs=[whole(HBM)] * 5,
-        out_specs=[whole(VMEM)] * 4,
+        out_specs=[whole(VMEM)] * 3,
         out_shape=[
             jax.ShapeDtypeStruct((chunk_rows, proj_width), BF16),
-            jax.ShapeDtypeStruct((query_rows, rest), BF16),
             jax.ShapeDtypeStruct((block_count, probe_count), I32),
             jax.ShapeDtypeStruct((2 * cand_count, query_rows), I32),
         ],
         scratch_shapes=[
             pltpu.VMEM(queries.shape, BF16),
-            pltpu.VMEM((full_width // proj_width, full_width, proj_width), F32),
+            pltpu.VMEM((full_width, proj_width), F32),
             pltpu.VMEM(probes.shape, I32),
             pltpu.VMEM((cand_count, query_rows), I32),
             pltpu.VMEM((cand_count, query_rows), I32),
-            pltpu.SemaphoreType.DMA((4 + full_width // proj_width,)),
+            pltpu.SemaphoreType.DMA((5,)),
         ],
         compiler_params=params(61 * MIB),
         cost_estimate=cost(2),
         name="plan",
     )(queries, rotation, probes, cand_pages.T, cand_rows.T)
-    order = tuple(range(0, shards, 2))
+    tail = pl.pallas_call(
+        tail_kernel,
+        in_specs=[whole(ANY)] * 2,
+        out_specs=whole(VMEM),
+        out_shape=jax.ShapeDtypeStruct((query_rows, rest), BF16),
+        scratch_shapes=[
+            pltpu.VMEM(queries.shape, BF16),
+            pltpu.VMEM((rest // proj_width, full_width, proj_width), F32),
+            pltpu.SemaphoreType.DMA((rest // proj_width + 1,)),
+        ],
+        compiler_params=params(TAIL_MIB * MIB),
+        cost_estimate=cost(3),
+        name="rotate_tail",
+    )(queries, rotation)
+
+    masks = tuple(range(0, shards, 4))
+    order = masks + tuple(m ^ 2 for m in masks)
     other = tuple(m ^ 1 for m in order)
+    flat = vectors.reshape(page_count * page_rows, full_width)
 
     def stack(parts, waits, name):
         return pl.pallas_call(
-            functools.partial(stack_kernel, len(waits)),
-            in_specs=[whole(ANY)] * len(waits) + [whole(VMEM)] * len(parts),
+            stack_kernel,
+            in_specs=[whole(VMEM)] * len(parts) + [whole(ANY)] * len(waits),
             out_specs=whole(VMEM),
             out_shape=jax.ShapeDtypeStruct((len(parts), *parts[0].shape), BF16),
             compiler_params=params(10 * MIB),
             cost_estimate=cost(1),
             name=name,
-        )(*waits, *parts)
+        )(*parts, *waits)
+
+    def relay(x, *waits):
+        return pl.pallas_call(
+            relay_kernel,
+            in_specs=[whole(ANY)] * (1 + len(waits)),
+            out_specs=whole(ANY),
+            out_shape=jax.ShapeDtypeStruct(x.shape, x.dtype),
+            input_output_aliases={0: 0},
+            compiler_params=params(4 * MIB),
+            cost_estimate=cost(1),
+            name="relay",
+        )(x, *waits)
 
     def coarse_scores(order, pieces, waits, before):
         count = 3 + len(waits)
@@ -303,21 +342,17 @@
             name="coarse_scores",
         )(me, pieces, codes, *waits, *before)
 
-    along, across = planes(chunk, shards)
-    plane = along | across()
-    tail_along = {mask: exchange(tail, mask, shards) for mask in range(4, shards, 4)}
-    tail_across = {2: exchange(tail, 2, shards)}
-
-    heads_a = stack([plane[m] for m in order], list(tail_along.values()), "stack_heads")
+    heads = [exchange(chunk, m, shards) if m else chunk for m in masks]
+    heads += [exchange(x, 2, shards) for x in heads]
+    tail = relay(tail, *heads[1 : len(masks)])
+    tails = [exchange(tail, m, shards) if m else tail for m in masks]
+    heads_a = stack(heads, tails[1:], "stack_heads")
     heads_b = exchange(heads_a, 1, shards)
+    tails += [exchange(x, 2, shards) for x in tails]
     scored, list_a = coarse_scores(order, heads_a, [], [])
     scored, list_b = coarse_scores(other, heads_b, [], [scored])
     returned = lax.all_to_all(scored, "idx", split_axis=0, concat_axis=0, tiled=True)
 
-    tail_across |= {mask ^ 2: exchange(x, 2, shards) for mask, x in tail_along.items()}
-    tails = {0: tail} | tail_along | tail_across
-
-    flat = vectors.reshape(page_count * page_rows, full_width)
     found = pl.pallas_call(
         gather_kernel,
         in_specs=[whole(ANY)] * 3,
@@ -332,7 +367,7 @@
         cost_estimate=cost(GATHER_COST),
         name="gather_rows",
     )(list_a, list_b, flat)
-    tails_a = stack([tails[m] for m in order], [found], "stack_tails")
+    tails_a = stack(tails, [found], "stack_tails")
     tails_b = exchange(tails_a, 1, shards)
 
     def scores(part, order, list_ref, heads, tails, before):
@@ -351,25 +386,28 @@
     answers = scores(1, other, list_b, heads_b, tails_b, [answers])
     own = jnp.stack([exchange(answers[a], 4 * a, shards) if a else answers[a] for a in range(shards // 4)])
     across = exchange(own, 2, shards)
-    coarse = pl.pallas_call(
+    coarse, placed = pl.pallas_call(
         place_kernel,
         in_specs=[whole(SMEM), whole(VMEM)],
-        out_specs=whole(VMEM),
-        out_shape=jax.ShapeDtypeStruct((query_rows, probe_count * page_rows), BF16),
+        out_specs=[whole(VMEM)] * 2,
+        out_shape=[
+            jax.ShapeDtypeStruct((query_rows, probe_count * page_rows), BF16),
+            jax.ShapeDtypeStruct((8, LANES), F32),
+        ],
         compiler_params=params(10 * MIB),
         cost_estimate=cost(1),
         name="place_scores",
     )(probe_place, returned.reshape(shards * capacity, block_rows, page_rows))
     rerank = pl.pallas_call(
         functools.partial(pick_kernel, shards),
-        in_specs=[whole(SMEM)] + [whole(VMEM)] * 5,
+        in_specs=[whole(SMEM)] + [whole(VMEM)] * 6,
         out_specs=whole(VMEM),
         out_shape=jax.ShapeDtypeStruct((cand_count, query_rows), F32),
         scratch_shapes=[pltpu.VMEM((shards, row_capacity), F32)],
         compiler_params=params(10 * MIB),
         cost_estimate=cost(1),
         name="pick_answers",
-    )(me, own, across, exchange(own, 1, shards), exchange(across, 1, shards), cand_place).T
+    )(me, own, across, exchange(own, 1, shards), exchange(own, 3, shards), cand_place, placed).T
     return coarse, rerank
 
 

time: 87.5 us -> 82.1 us (0.938)
  starting transfers between devices: 33 us -> 29.3 us
  waiting for transfers between devices: 23.5 us -> 22.2 us
    ppermute x22, starting transfers between devices: 29.1 us -> 25.4 us  [exchange(): return lax.ppermute(x, 'idx', [(i, i ^ mask) for i in range(shards)])]
    pallas_call x2 -> x4, Pallas kernels: 1.43 us -> 4.73 us  [the longest x1 3.19 us: body(): pl.pallas_call(tail_kernel, in_specs=[whole(ANY)] * 2, out_specs=whole(VM...]
    pallas_call x1, Pallas kernels: 4.38 us -> 2.89 us  [body(): pl.pallas_call(functools.partial(plan_kernel, shards, page_count), in_spe...]
    ppermute x22, waiting for transfers between devices: 23.5 us -> 22.2 us  [exchange(): return lax.ppermute(x, 'idx', [(i, i ^ mask) for i in range(shards)])]
    pallas_call x2, Pallas kernels: 5.36 us -> 4.28 us  [coarse_scores(): pl.pallas_call(functools.partial(coarse_kernel, shards, order, block_rows...]
    pallas_call x2, Pallas kernels: 2.54 us -> 1.46 us  [scores(): pl.pallas_call(functools.partial(rerank_kernel, part, order), in_specs=[w...]
    unnamed x12 -> x16, local copies, waits for them, and re-layouts: 1.87 us -> 1.93 us
  transfers between devices with their start and end apart: 23 -> 23, of which waited for: 9 -> 10; matrix products, arithmetic and copies ran while one was open for 0% -> 0% of each run, Pallas kernels for 25% -> 29%
where the time goes in v4:
time: 82.1 us; the launch traced here: 81.9 us
  starting transfers between devices  29.3 us (36%)
  Pallas kernels  27.6 us (34%)
  waiting for transfers between devices  22.2 us (27%)
  local copies, waits for them, and re-layouts  1.93 us (2%)
  between operations  0.85 us (1%)
    ppermute x22, starting transfers between devices, exchange(): return lax.ppermute(x, 'idx', [(i, i ^ mask) for i in range(shards)])  25.4 us
    ppermute x22, waiting for transfers between devices, exchange(): return lax.ppermute(x, 'idx', [(i, i ^ mask) for i in range(shards)])  22.2 us
    pallas_call x1, Pallas kernels, body(): pl.pallas_call(gather_kernel, in_specs=[whole(ANY)] * 3, out_specs=whole(...  11.8 us
    pallas_call x2, Pallas kernels, coarse_scores(): pl.pallas_call(functools.partial(coarse_kernel, shards, order, block_rows...  4.28 us
    all_to_all x1, starting transfers between devices, body(): lax.all_to_all(scored, 'idx', split_axis=0, concat_axis=0, tiled=True)  3.88 us
    pallas_call x1, Pallas kernels, body(): pl.pallas_call(tail_kernel, in_specs=[whole(ANY)] * 2, out_specs=whole(VM...  3.19 us
    pallas_call x1, Pallas kernels, body(): pl.pallas_call(functools.partial(plan_kernel, shards, page_count), in_spe...  2.89 us
    unnamed x16, local copies, waits for them, and re-layouts  1.93 us
  transfers between devices with their start and end apart: 23, of which 10 were waited for; matrix products, arithmetic and copies ran while one was open for 0% of the time, Pallas kernels for 29%

profile of v4, /device:TPU:0, one launch (start us, length us, event | category | flops | bytes accessed | tf_op | source)
XLA Modules:
  0.0 81.9 jit_solution(9556300506665932868)
XLA Ops:
  0.6 2.9 %plan.1 = (bf16[160,256]{1,0:T(8,128)(2,1)}, s32[4,16]{1,0:T(4,128)}, s32[16,128]{1,0:T(8,128)}) custom-call(bf16[128,1024]{1,0:T(8,128)(2,1)} %q_hbm.3, f32[1024,1024]{1,0:T(8,128)} %rot_hbm.3, s32[4,16]{1,0:T(4,128)} %probes_hbm.1, s32[8,128]{1,0:T(8,128)} %bitcast.18, s32[8,128]{1,0:T(8,128)} %bitcast.19), custom_call_target="tpu_custom_call" | custom-call | bytes 6000000 | tf_op jit(solution)/shard_map/plan/pallas_call | solution.py:259
  3.6 5.1 %collective-permute-start.2 = (bf16[160,256]{1,0:T(8,128)(2,1)}, bf16[160,256]{1,0:T(8,128)(2,1)S(1)}, u32[]{:S(2)}, u32[]{:S(2)}) collective-permute-start(bf16[160,256]{1,0:T(8,128)(2,1)} %get-tuple-element.12.refs_0_), channel_id=1, source_target_pairs={{0,12},{1,13},{2,14},{3,15},{4,8},{5,9},{6,10},{7,11},{8,4},{9,5},... | collective-permute-start | bytes 245768 | tf_op jit(solution)/shard_map/ppermute | solution.py:240
  9.3 3.2 %rotate_tail.1.refs_0_ = bf16[128,768]{1,0:T(8,128)(2,1)} custom-call(bf16[128,1024]{1,0:T(8,128)(2,1)} %q_hbm.3, f32[1024,1024]{1,0:T(8,128)} %rot_hbm.3), custom_call_target="tpu_custom_call" | custom-call | bytes 9000000 | tf_op jit(solution)/shard_map/rotate_tail/pallas_call | solution.py:280
  12.5 3.2 %collective-permute-done.1.refs_2_ = bf16[160,256]{1,0:T(8,128)(2,1)S(1)} collective-permute-done((bf16[160,256]{1,0:T(8,128)(2,1)}, bf16[160,256]{1,0:T(8,128)(2,1)S(1)}, u32[]{:S(2)}, u32[]{:S(2)}) %collective-permute-start.1) | collective-permute-done | bytes 81952 | tf_op jit(solution)/shard_map/ppermute | solution.py:240
  15.7 0.9 %copy-done.2 = bf16[128,768]{1,0:T(8,128)(2,1)S(1)} copy-done((bf16[128,768]{1,0:T(8,128)(2,1)S(1)}, bf16[128,768]{1,0:T(8,128)(2,1)}, u32[]{:S(2)}) %copy-start.2) | copy-done | bytes 196632
  16.7 2.7 %collective-permute-start.9 = (bf16[128,768]{1,0:T(8,128)(2,1)S(1)}, bf16[128,768]{1,0:T(8,128)(2,1)}, u32[]{:S(2)}, u32[]{:S(2)}) collective-permute-start(bf16[128,768]{1,0:T(8,128)(2,1)S(1)} %relay.1.refs_0_), channel_id=1, source_target_pairs={{0,12},{1,13},{2,14},{3,15},{4,8},{5,9},{6,10},{7,11},{8,4},{9,5},... | collective-permute-start | bytes 589832 | tf_op jit(solution)/shard_map/ppermute | solution.py:240
  19.4 1.7 %collective-permute-start.7 = (bf16[128,768]{1,0:T(8,128)(2,1)S(1)}, bf16[128,768]{1,0:T(8,128)(2,1)}, u32[]{:S(2)}, u32[]{:S(2)}) collective-permute-start(bf16[128,768]{1,0:T(8,128)(2,1)S(1)} %relay.1.refs_0_), channel_id=1, source_target_pairs={{0,4},{1,5},{2,6},{3,7},{4,0},{5,1},{6,2},{7,3},{8,12},{9,13},{10,... | collective-permute-start | bytes 589832 | tf_op jit(solution)/shard_map/ppermute | solution.py:240
  21.1 1.5 %collective-permute-start.3 = (bf16[160,256]{1,0:T(8,128)(2,1)S(1)}, bf16[160,256]{1,0:T(8,128)(2,1)S(1)}, u32[]{:S(2)}, u32[]{:S(2)}) collective-permute-start(bf16[160,256]{1,0:T(8,128)(2,1)S(1)} %copy-done.5), channel_id=1, source_target_pairs={{0,2},{1,3},{2,0},{3,1},{4,6},{5,7},{6,4},{7,5},{8,10},{9,11},{10,... | collective-permute-start | bytes 245768 | tf_op jit(solution)/shard_map/ppermute | solution.py:240
  23.1 2.4 %collective-permute-done.3.refs_4_ = bf16[160,256]{1,0:T(8,128)(2,1)S(1)} collective-permute-done((bf16[160,256]{1,0:T(8,128)(2,1)S(1)}, bf16[160,256]{1,0:T(8,128)(2,1)S(1)}, u32[]{:S(2)}, u32[]{:S(2)}) %collective-permute-start.3) | collective-permute-done | bytes 81952 | tf_op jit(solution)/shard_map/ppermute | solution.py:240
  25.5 1.5 %collective-permute-start.5 = (bf16[160,256]{1,0:T(8,128)(2,1)S(1)}, bf16[160,256]{1,0:T(8,128)(2,1)S(1)}, u32[]{:S(2)}, u32[]{:S(2)}) collective-permute-start(bf16[160,256]{1,0:T(8,128)(2,1)S(1)} %collective-permute-done.1.refs_2_), channel_id=1, source_target_pairs={{0,2},{1,3},{2,0},{3,1},{4,6},{5,7},{6,4},{7,5},{8,10},{9,11},{10,... | collective-permute-start | bytes 245768 | tf_op jit(solution)/shard_map/ppermute | solution.py:240
  27.0 0.9 %collective-permute-done.6.refs_7_ = bf16[160,256]{1,0:T(8,128)(2,1)S(1)} collective-permute-done((bf16[160,256]{1,0:T(8,128)(2,1)S(1)}, bf16[160,256]{1,0:T(8,128)(2,1)S(1)}, u32[]{:S(2)}, u32[]{:S(2)}) %collective-permute-start.6) | collective-permute-done | bytes 81952 | tf_op jit(solution)/shard_map/ppermute | solution.py:240
  28.3 1.7 %collective-permute-done.5.refs_6_ = bf16[160,256]{1,0:T(8,128)(2,1)S(1)} collective-permute-done((bf16[160,256]{1,0:T(8,128)(2,1)S(1)}, bf16[160,256]{1,0:T(8,128)(2,1)S(1)}, u32[]{:S(2)}, u32[]{:S(2)}) %collective-permute-start.5) | collective-permute-done | bytes 81952 | tf_op jit(solution)/shard_map/ppermute | solution.py:240
  29.9 2.4 %collective-permute-done.4.refs_5_ = bf16[160,256]{1,0:T(8,128)(2,1)S(1)} collective-permute-done((bf16[160,256]{1,0:T(8,128)(2,1)S(1)}, bf16[160,256]{1,0:T(8,128)(2,1)S(1)}, u32[]{:S(2)}, u32[]{:S(2)}) %collective-permute-start.4) | collective-permute-done | bytes 81952 | tf_op jit(solution)/shard_map/ppermute | solution.py:240
  32.3 3.0 %collective-permute-done.8.refs_9_.refs_2_ = bf16[128,768]{1,0:T(8,128)(2,1)} collective-permute-done((bf16[128,768]{1,0:T(8,128)(2,1)S(1)}, bf16[128,768]{1,0:T(8,128)(2,1)}, u32[]{:S(2)}, u32[]{:S(2)}) %collective-permute-start.8) | collective-permute-done | bytes 196640 | tf_op jit(solution)/shard_map/ppermute | solution.py:240
  35.5 1.6 %collective-permute-start.11 = (bf16[128,768]{1,0:T(8,128)(2,1)}, bf16[128,768]{1,0:T(8,128)(2,1)}, u32[]{:S(2)}, u32[]{:S(2)}) collective-permute-start(bf16[128,768]{1,0:T(8,128)(2,1)} %copy-done.3), channel_id=1, source_target_pairs={{0,2},{1,3},{2,0},{3,1},{4,6},{5,7},{6,4},{7,5},{8,10},{9,11},{10,... | collective-permute-start | bytes 589832 | tf_op jit(solution)/shard_map/ppermute | solution.py:240
  37.6 1.5 %collective-permute-start.13 = (bf16[128,768]{1,0:T(8,128)(2,1)}, bf16[128,768]{1,0:T(8,128)(2,1)}, u32[]{:S(2)}, u32[]{:S(2)}) collective-permute-start(bf16[128,768]{1,0:T(8,128)(2,1)} %collective-permute-done.8.refs_9_.refs_2_), channel_id=1, source_target_pairs={{0,2},{1,3},{2,0},{3,1},{4,6},{5,7},{6,4},{7,5},{8,10},{9,11},{10,... | collective-permute-start | bytes 589832 | tf_op jit(solution)/shard_map/ppermute | solution.py:240
  39.6 2.1 %coarse_scores.2 = (bf16[16,8,32,128]{3,2,1,0:T(8,128)(2,1)S(1)}, s32[2,8,128]{2,1,0:T(8,128)S(1)}) custom-call(s32[1]{0:T(128)} %bitcast.2.me_ref, bf16[8,160,256]{2,1,0:T(8,128)(2,1)S(1)} %stack_heads.1.pieces.heads, bf16[32,128,256]{2,1,0:T(8,128)(2,1)S(1)} %copy-done), custom_call_target="tpu_custom_call" | custom-call | bytes 9000000 | tf_op jit(solution)/shard_map/coarse_scores/pallas_call | solution.py:325
  41.8 2.1 %coarse_scores.3 = (bf16[16,8,32,128]{3,2,1,0:T(8,128)(2,1)S(1)}, s32[2,8,128]{2,1,0:T(8,128)S(1)}) custom-call(s32[1]{0:T(128)} %bitcast.2.me_ref, bf16[8,160,256]{2,1,0:T(8,128)(2,1)S(1)} %collective-permute-done.10.pieces.heads, bf16[32,128,256]{2,1,0:T(8,128)(2,1)S(1)} %copy-done, ...), custom_call_target="tpu_custom_call", output_to_operand_aliasing={{0}: (3, {})} | custom-call | bytes 9000000 | tf_op jit(solution)/shard_map/coarse_scores/pallas_call | solution.py:325
  44.0 1.0 %copy-done.1 = bf16[16,8,32,128]{3,2,1,0:T(8,128)(2,1)} copy-done((bf16[16,8,32,128]{3,2,1,0:T(8,128)(2,1)}, bf16[16,8,32,128]{3,2,1,0:T(8,128)(2,1)S(1)}, u32[]{:S(2)}) %copy-start.1) | copy-done | bytes 1048600
  44.9 3.9 %all-to-all-start = ((bf16[16,8,32,128]{3,2,1,0:T(8,128)(2,1)}), bf16[16,8,32,128]{3,2,1,0:T(8,128)(2,1)S(1)}, u32[]{:S(2)}, u32[]{:S(2)}) async-start(bf16[16,8,32,128]{3,2,1,0:T(8,128)(2,1)} %copy-done.1), calls=%async_computation | async-start | bytes 2097152 | tf_op jit(solution)/shard_map/all_to_all | solution.py:354
  48.8 11.8 %gather_rows.1.refs_8_.rows_ref = bf16[2,8,128,1024]{3,2,1,0:T(8,128)(2,1)S(1)} custom-call(s32[2,8,128]{2,1,0:T(8,128)S(1)} %get-tuple-element.17.list_a.list_ref, s32[2,8,128]{2,1,0:T(8,128)S(1)} %get-tuple-element.16.list_b.list_ref, f32[4096,1024]{1,0:T(8,128)} %bitcast.16), custom_call_target="tpu_custom_call" | custom-call | bytes 36000000 | tf_op jit(solution)/shard_map/gather_rows/pallas_call | solution.py:356
  60.7 1.5 %stack_tails.1.refs_0_ = bf16[8,128,768]{2,1,0:T(8,128)(2,1)S(1)} custom-call(bf16[128,768]{1,0:T(8,128)(2,1)S(1)} %copy-done.4, bf16[128,768]{1,0:T(8,128)(2,1)} %collective-permute-done.7.refs_8_.refs_1_, bf16[128,768]{1,0:T(8,128)(2,1)} %collective-permute-done.8.refs_9_.refs_2_, bf16[128,768]{1,0:T(8,128)(2,1)} %collective-permute-done.9.refs_10_.refs_3_, ...), custom_call_target="tpu_custom_call" | custom-call | bytes 3000000 | tf_op jit(solution)/shard_map/stack_tails/pallas_call | solution.py:301
  62.6 0.7 rerank_scores.2.refs_1_
  63.4 2.3 %collective-permute-done.15.refs_0_ = bf16[8,128,768]{2,1,0:T(8,128)(2,1)S(1)} collective-permute-done((bf16[8,128,768]{2,1,0:T(8,128)(2,1)S(1)}, bf16[8,128,768]{2,1,0:T(8,128)(2,1)S(1)}, u32[]{:S(2)}, u32[]{:S(2)}) %collective-permute-start.15) | collective-permute-done | bytes 1572896 | tf_op jit(solution)/shard_map/ppermute | solution.py:240
  65.7 0.7 rerank_scores.3
  66.4 3.8 %collective-permute-start.18 = (f32[4,128]{1,0:T(4,128)S(1)}, f32[4,128]{1,0:T(4,128)S(1)}, u32[]{:S(2)}, u32[]{:S(2)}) collective-permute-start(f32[4,128]{1,0:T(4,128)S(1)} %get-tuple-element.21), channel_id=1, source_target_pairs={{0,12},{1,13},{2,14},{3,15},{4,8},{5,9},{6,10},{7,11},{8,4},{9,5},... | collective-permute-start | bytes 6152 | tf_op jit(solution)/shard_map/ppermute | solution.py:240
  70.9 1.1 %collective-permute-done.18 = f32[4,128]{1,0:T(4,128)S(1)} collective-permute-done((f32[4,128]{1,0:T(4,128)S(1)}, f32[4,128]{1,0:T(4,128)S(1)}, u32[]{:S(2)}, u32[]{:S(2)}) %collective-permute-start.18) | collective-permute-done | bytes 2080 | tf_op jit(solution)/shard_map/ppermute | solution.py:240
  72.0 3.5 %collective-permute-done.17 = f32[4,128]{1,0:T(4,128)S(1)} collective-permute-done((f32[4,128]{1,0:T(4,128)S(1)}, f32[4,128]{1,0:T(4,128)S(1)}, u32[]{:S(2)}, u32[]{:S(2)}) %collective-permute-start.17) | collective-permute-done | bytes 2080 | tf_op jit(solution)/shard_map/ppermute | solution.py:240
  76.0 1.2 %collective-permute-start.20 = (f32[4,4,128]{2,1,0:T(4,128)S(1)}, f32[4,4,128]{2,1,0:T(4,128)S(1)}, u32[]{:S(2)}, u32[]{:S(2)}) collective-permute-start(f32[4,4,128]{2,1,0:T(4,128)S(1)} %pad_maximum_fusion.own_ref), channel_id=1, source_target_pairs={{0,1},{1,0},{2,3},{3,2},{4,5},{5,4},{6,7},{7,6},{8,9},{9,8},{10,11... | collective-permute-start | bytes 24584 | tf_op jit(solution)/shard_map/ppermute | solution.py:240
  77.8 1.5 %place_scores.1 = (bf16[128,2048]{1,0:T(8,128)(2,1)}, f32[8,128]{1,0:T(8,128)S(1)}) custom-call(s32[4,16]{1,0:T(4,128)S(1)} %copy-done.7, bf16[128,32,128]{2,1,0:T(8,128)(2,1)S(1)} %bitcast.15), custom_call_target="tpu_custom_call" | custom-call | bytes 3000000 | tf_op jit(solution)/shard_map/place_scores/pallas_call | solution.py:389
  79.2 1.6 %collective-permute-done.19.y_ref = f32[4,4,128]{2,1,0:T(4,128)S(1)} collective-permute-done((f32[4,4,128]{2,1,0:T(4,128)S(1)}, f32[4,4,128]{2,1,0:T(4,128)S(1)}, u32[]{:S(2)}, u32[]{:S(2)}) %collective-permute-start.19) | collective-permute-done | bytes 8224 | tf_op jit(solution)/shard_map/ppermute | solution.py:240
  80.9 1.0 %pick_answers.1 = f32[8,128]{1,0:T(8,128)} custom-call(s32[1]{0:T(128)} %bitcast.2.me_ref, f32[4,4,128]{2,1,0:T(4,128)S(1)} %pad_maximum_fusion.own_ref, f32[4,4,128]{2,1,0:T(4,128)S(1)} %collective-permute-done.19.y_ref, f32[4,4,128]{2,1,0:T(4,128)S(1)} %collective-permute-done.20.core_ref, f32[4,4,128]{2,1,0:T(4,128)S(1)} %collective-permute-done.21.both_ref, ...), custom_call_target="tpu_custom_call" | custom-call | bytes 3000000 | tf_op jit(solution)/shard_map/pick_answers/pallas_call | solution.py:401
  (44 shorter events, 5.0 us)
Async XLA Ops:
  3.5 17.5 %copy-start.5 = (bf16[160,256]{1,0:T(8,128)(2,1)S(1)}, bf16[160,256]{1,0:T(8,128)(2,1)}, u32[]{:S(2)}) copy-start(bf16[160,256]{1,0:T(8,128)(2,1)} %get-tuple-element.12.refs_0_) | copy-start | bytes 245764
  3.5 36.1 %copy-start = (bf16[32,128,256]{2,1,0:T(8,128)(2,1)S(1)}, bf16[32,128,256]{2,1,0:T(8,128)(2,1)}, u32[]{:S(2)}) copy-start(bf16[32,128,256]{2,1,0:T(8,128)(2,1)} %codes.3) | copy-start | bytes 6291460
  3.6 9.0 %collective-permute-start.2 = (bf16[160,256]{1,0:T(8,128)(2,1)}, bf16[160,256]{1,0:T(8,128)(2,1)S(1)}, u32[]{:S(2)}, u32[]{:S(2)}) collective-permute-start(bf16[160,256]{1,0:T(8,128)(2,1)} %get-tuple-element.12.refs_0_), channel_id=1, source_target_pairs={{0,12},{1,13},{2,14},{3,15},{4,8},{5,9},{6,10},{7,11},{8,4},{9,5},... | collective-permute-start | bytes 245768 | tf_op jit(solution)/shard_map/ppermute | solution.py:240
  8.7 7.1 %collective-permute-start.1 = (bf16[160,256]{1,0:T(8,128)(2,1)}, bf16[160,256]{1,0:T(8,128)(2,1)S(1)}, u32[]{:S(2)}, u32[]{:S(2)}) collective-permute-start(bf16[160,256]{1,0:T(8,128)(2,1)} %get-tuple-element.12.refs_0_), channel_id=1, source_target_pairs={{0,8},{1,9},{2,10},{3,11},{4,12},{5,13},{6,14},{7,15},{8,0},{9,1},... | collective-permute-start | bytes 245768 | tf_op jit(solution)/shard_map/ppermute | solution.py:240
  8.7 7.1 %collective-permute-start = (bf16[160,256]{1,0:T(8,128)(2,1)}, bf16[160,256]{1,0:T(8,128)(2,1)S(1)}, u32[]{:S(2)}, u32[]{:S(2)}) collective-permute-start(bf16[160,256]{1,0:T(8,128)(2,1)} %get-tuple-element.12.refs_0_), channel_id=1, source_target_pairs={{0,4},{1,5},{2,6},{3,7},{4,0},{5,1},{6,2},{7,3},{8,12},{9,13},{10,... | collective-permute-start | bytes 245768 | tf_op jit(solution)/shard_map/ppermute | solution.py:240
  15.7 0.9 %copy-start.2 = (bf16[128,768]{1,0:T(8,128)(2,1)S(1)}, bf16[128,768]{1,0:T(8,128)(2,1)}, u32[]{:S(2)}) copy-start(bf16[128,768]{1,0:T(8,128)(2,1)} %rotate_tail.1.refs_0_) | copy-start | bytes 589828
  16.7 18.7 %copy-start.3 = (bf16[128,768]{1,0:T(8,128)(2,1)}, bf16[128,768]{1,0:T(8,128)(2,1)S(1)}, u32[]{:S(2)}) copy-start(bf16[128,768]{1,0:T(8,128)(2,1)S(1)} %relay.1.refs_0_) | copy-start | bytes 589828
  16.7 15.7 %collective-permute-start.9 = (bf16[128,768]{1,0:T(8,128)(2,1)S(1)}, bf16[128,768]{1,0:T(8,128)(2,1)}, u32[]{:S(2)}, u32[]{:S(2)}) collective-permute-start(bf16[128,768]{1,0:T(8,128)(2,1)S(1)} %relay.1.refs_0_), channel_id=1, source_target_pairs={{0,12},{1,13},{2,14},{3,15},{4,8},{5,9},{6,10},{7,11},{8,4},{9,5},... | collective-permute-start | bytes 589832 | tf_op jit(solution)/shard_map/ppermute | solution.py:240
  19.4 16.0 %collective-permute-start.8 = (bf16[128,768]{1,0:T(8,128)(2,1)S(1)}, bf16[128,768]{1,0:T(8,128)(2,1)}, u32[]{:S(2)}, u32[]{:S(2)}) collective-permute-start(bf16[128,768]{1,0:T(8,128)(2,1)S(1)} %relay.1.refs_0_), channel_id=1, source_target_pairs={{0,8},{1,9},{2,10},{3,11},{4,12},{5,13},{6,14},{7,15},{8,0},{9,1},... | collective-permute-start | bytes 589832 | tf_op jit(solution)/shard_map/ppermute | solution.py:240
  19.4 16.0 %collective-permute-start.7 = (bf16[128,768]{1,0:T(8,128)(2,1)S(1)}, bf16[128,768]{1,0:T(8,128)(2,1)}, u32[]{:S(2)}, u32[]{:S(2)}) collective-permute-start(bf16[128,768]{1,0:T(8,128)(2,1)S(1)} %relay.1.refs_0_), channel_id=1, source_target_pairs={{0,4},{1,5},{2,6},{3,7},{4,0},{5,1},{6,2},{7,3},{8,12},{9,13},{10,... | collective-permute-start | bytes 589832 | tf_op jit(solution)/shard_map/ppermute | solution.py:240
  21.1 4.4 %collective-permute-start.3 = (bf16[160,256]{1,0:T(8,128)(2,1)S(1)}, bf16[160,256]{1,0:T(8,128)(2,1)S(1)}, u32[]{:S(2)}, u32[]{:S(2)}) collective-permute-start(bf16[160,256]{1,0:T(8,128)(2,1)S(1)} %copy-done.5), channel_id=1, source_target_pairs={{0,2},{1,3},{2,0},{3,1},{4,6},{5,7},{6,4},{7,5},{8,10},{9,11},{10,... | collective-permute-start | bytes 245768 | tf_op jit(solution)/shard_map/ppermute | solution.py:240
  22.6 5.3 %collective-permute-start.6 = (bf16[160,256]{1,0:T(8,128)(2,1)S(1)}, bf16[160,256]{1,0:T(8,128)(2,1)S(1)}, u32[]{:S(2)}, u32[]{:S(2)}) collective-permute-start(bf16[160,256]{1,0:T(8,128)(2,1)S(1)} %collective-permute-done.2.refs_3_), channel_id=1, source_target_pairs={{0,2},{1,3},{2,0},{3,1},{4,6},{5,7},{6,4},{7,5},{8,10},{9,11},{10,... | collective-permute-start | bytes 245768 | tf_op jit(solution)/shard_map/ppermute | solution.py:240
  25.5 4.4 %collective-permute-start.5 = (bf16[160,256]{1,0:T(8,128)(2,1)S(1)}, bf16[160,256]{1,0:T(8,128)(2,1)S(1)}, u32[]{:S(2)}, u32[]{:S(2)}) collective-permute-start(bf16[160,256]{1,0:T(8,128)(2,1)S(1)} %collective-permute-done.1.refs_2_), channel_id=1, source_target_pairs={{0,2},{1,3},{2,0},{3,1},{4,6},{5,7},{6,4},{7,5},{8,10},{9,11},{10,... | collective-permute-start | bytes 245768 | tf_op jit(solution)/shard_map/ppermute | solution.py:240
  27.9 4.4 %collective-permute-start.4 = (bf16[160,256]{1,0:T(8,128)(2,1)S(1)}, bf16[160,256]{1,0:T(8,128)(2,1)S(1)}, u32[]{:S(2)}, u32[]{:S(2)}) collective-permute-start(bf16[160,256]{1,0:T(8,128)(2,1)S(1)} %collective-permute-done.refs_1_), channel_id=1, source_target_pairs={{0,2},{1,3},{2,0},{3,1},{4,6},{5,7},{6,4},{7,5},{8,10},{9,11},{10,... | collective-permute-start | bytes 245768 | tf_op jit(solution)/shard_map/ppermute | solution.py:240
  35.4 6.3 %collective-permute-start.10 = (bf16[8,160,256]{2,1,0:T(8,128)(2,1)S(1)}, bf16[8,160,256]{2,1,0:T(8,128)(2,1)S(1)}, u32[]{:S(2)}, u32[]{:S(2)}) collective-permute-start(bf16[8,160,256]{2,1,0:T(8,128)(2,1)S(1)} %stack_heads.1.pieces.heads), channel_id=1, source_target_pairs={{0,1},{1,0},{2,3},{3,2},{4,5},{5,4},{6,7},{7,6},{8,9},{9,8},{10,11... | collective-permute-start | bytes 1966088 | tf_op jit(solution)/shard_map/ppermute | solution.py:240
  35.5 25.1 %collective-permute-start.11 = (bf16[128,768]{1,0:T(8,128)(2,1)}, bf16[128,768]{1,0:T(8,128)(2,1)}, u32[]{:S(2)}, u32[]{:S(2)}) collective-permute-start(bf16[128,768]{1,0:T(8,128)(2,1)} %copy-done.3), channel_id=1, source_target_pairs={{0,2},{1,3},{2,0},{3,1},{4,6},{5,7},{6,4},{7,5},{8,10},{9,11},{10,... | collective-permute-start | bytes 589832 | tf_op jit(solution)/shard_map/ppermute | solution.py:240
  37.1 23.5 %collective-permute-start.14 = (bf16[128,768]{1,0:T(8,128)(2,1)}, bf16[128,768]{1,0:T(8,128)(2,1)}, u32[]{:S(2)}, u32[]{:S(2)}) collective-permute-start(bf16[128,768]{1,0:T(8,128)(2,1)} %collective-permute-done.9.refs_10_.refs_3_), channel_id=1, source_target_pairs={{0,2},{1,3},{2,0},{3,1},{4,6},{5,7},{6,4},{7,5},{8,10},{9,11},{10,... | collective-permute-start | bytes 589832 | tf_op jit(solution)/shard_map/ppermute | solution.py:240
  37.6 23.0 %collective-permute-start.13 = (bf16[128,768]{1,0:T(8,128)(2,1)}, bf16[128,768]{1,0:T(8,128)(2,1)}, u32[]{:S(2)}, u32[]{:S(2)}) collective-permute-start(bf16[128,768]{1,0:T(8,128)(2,1)} %collective-permute-done.8.refs_9_.refs_2_), channel_id=1, source_target_pairs={{0,2},{1,3},{2,0},{3,1},{4,6},{5,7},{6,4},{7,5},{8,10},{9,11},{10,... | collective-permute-start | bytes 589832 | tf_op jit(solution)/shard_map/ppermute | solution.py:240
  39.1 21.5 %collective-permute-start.12 = (bf16[128,768]{1,0:T(8,128)(2,1)}, bf16[128,768]{1,0:T(8,128)(2,1)}, u32[]{:S(2)}, u32[]{:S(2)}) collective-permute-start(bf16[128,768]{1,0:T(8,128)(2,1)} %collective-permute-done.7.refs_8_.refs_1_), channel_id=1, source_target_pairs={{0,2},{1,3},{2,0},{3,1},{4,6},{5,7},{6,4},{7,5},{8,10},{9,11},{10,... | collective-permute-start | bytes 589832 | tf_op jit(solution)/shard_map/ppermute | solution.py:240
  43.9 1.0 %copy-start.1 = (bf16[16,8,32,128]{3,2,1,0:T(8,128)(2,1)}, bf16[16,8,32,128]{3,2,1,0:T(8,128)(2,1)S(1)}, u32[]{:S(2)}) copy-start(bf16[16,8,32,128]{3,2,1,0:T(8,128)(2,1)S(1)} %get-tuple-element.14) | copy-start | bytes 3145732
  44.9 32.8 %all-to-all-start = ((bf16[16,8,32,128]{3,2,1,0:T(8,128)(2,1)}), bf16[16,8,32,128]{3,2,1,0:T(8,128)(2,1)S(1)}, u32[]{:S(2)}, u32[]{:S(2)}) async-start(bf16[16,8,32,128]{3,2,1,0:T(8,128)(2,1)} %copy-done.1), calls=%async_computation | async-start | bytes 2097152 | tf_op jit(solution)/shard_map/all_to_all | solution.py:354
  48.8 11.8 %copy-start.4 = (bf16[128,768]{1,0:T(8,128)(2,1)S(1)}, bf16[128,768]{1,0:T(8,128)(2,1)}, u32[]{:S(2)}) copy-start(bf16[128,768]{1,0:T(8,128)(2,1)} %copy-done.3) | copy-start | bytes 589828
  62.2 3.5 %collective-permute-start.15 = (bf16[8,128,768]{2,1,0:T(8,128)(2,1)S(1)}, bf16[8,128,768]{2,1,0:T(8,128)(2,1)S(1)}, u32[]{:S(2)}, u32[]{:S(2)}) collective-permute-start(bf16[8,128,768]{2,1,0:T(8,128)(2,1)S(1)} %stack_tails.1.refs_0_), channel_id=1, source_target_pairs={{0,1},{1,0},{2,3},{3,2},{4,5},{5,4},{6,7},{7,6},{8,9},{9,8},{10,11... | collective-permute-start | bytes 4718600 | tf_op jit(solution)/shard_map/ppermute | solution.py:240
  63.4 14.4 %copy-start.7 = (s32[4,16]{1,0:T(4,128)S(1)}, s32[4,16]{1,0:T(4,128)}, u32[]{:S(2)}) copy-start(s32[4,16]{1,0:T(4,128)} %get-tuple-element.11.place_ref) | copy-start | bytes 772
  63.4 17.5 %copy-start.6 = (s32[16,128]{1,0:T(8,128)S(1)}, s32[16,128]{1,0:T(8,128)}, u32[]{:S(2)}) copy-start(s32[16,128]{1,0:T(8,128)} %get-tuple-element.18.place_ref) | copy-start | bytes 24580
  66.4 5.6 %collective-permute-start.18 = (f32[4,128]{1,0:T(4,128)S(1)}, f32[4,128]{1,0:T(4,128)S(1)}, u32[]{:S(2)}, u32[]{:S(2)}) collective-permute-start(f32[4,128]{1,0:T(4,128)S(1)} %get-tuple-element.21), channel_id=1, source_target_pairs={{0,12},{1,13},{2,14},{3,15},{4,8},{5,9},{6,10},{7,11},{8,4},{9,5},... | collective-permute-start | bytes 6152 | tf_op jit(solution)/shard_map/ppermute | solution.py:240
  70.2 5.4 %collective-permute-start.17 = (f32[4,128]{1,0:T(4,128)S(1)}, f32[4,128]{1,0:T(4,128)S(1)}, u32[]{:S(2)}, u32[]{:S(2)}) collective-permute-start(f32[4,128]{1,0:T(4,128)S(1)} %get-tuple-element.22), channel_id=1, source_target_pairs={{0,8},{1,9},{2,10},{3,11},{4,12},{5,13},{6,14},{7,15},{8,0},{9,1},... | collective-permute-start | bytes 6152 | tf_op jit(solution)/shard_map/ppermute | solution.py:240
  70.2 5.4 %collective-permute-start.16 = (f32[4,128]{1,0:T(4,128)S(1)}, f32[4,128]{1,0:T(4,128)S(1)}, u32[]{:S(2)}, u32[]{:S(2)}) collective-permute-start(f32[4,128]{1,0:T(4,128)S(1)} %get-tuple-element.23), channel_id=1, source_target_pairs={{0,4},{1,5},{2,6},{3,7},{4,0},{5,1},{6,2},{7,3},{8,12},{9,13},{10,... | collective-permute-start | bytes 6152 | tf_op jit(solution)/shard_map/ppermute | solution.py:240
  75.5 3.7 %collective-permute-start.21 = (f32[4,4,128]{2,1,0:T(4,128)S(1)}, f32[4,4,128]{2,1,0:T(4,128)S(1)}, u32[]{:S(2)}, u32[]{:S(2)}) collective-permute-start(f32[4,4,128]{2,1,0:T(4,128)S(1)} %pad_maximum_fusion.own_ref), channel_id=1, source_target_pairs={{0,3},{1,2},{2,1},{3,0},{4,7},{5,6},{6,5},{7,4},{8,11},{9,10},{10,... | collective-permute-start | bytes 24584 | tf_op jit(solution)/shard_map/ppermute | solution.py:240
  76.0 3.2 %collective-permute-start.20 = (f32[4,4,128]{2,1,0:T(4,128)S(1)}, f32[4,4,128]{2,1,0:T(4,128)S(1)}, u32[]{:S(2)}, u32[]{:S(2)}) collective-permute-start(f32[4,4,128]{2,1,0:T(4,128)S(1)} %pad_maximum_fusion.own_ref), channel_id=1, source_target_pairs={{0,1},{1,0},{2,3},{3,2},{4,5},{5,4},{6,7},{7,6},{8,9},{9,8},{10,11... | collective-permute-start | bytes 24584 | tf_op jit(solution)/shard_map/ppermute | solution.py:240
  77.2 3.7 %collective-permute-start.19 = (f32[4,4,128]{2,1,0:T(4,128)S(1)}, f32[4,4,128]{2,1,0:T(4,128)S(1)}, u32[]{:S(2)}, u32[]{:S(2)}) collective-permute-start(f32[4,4,128]{2,1,0:T(4,128)S(1)} %pad_maximum_fusion.own_ref), channel_id=1, source_target_pairs={{0,2},{1,3},{2,0},{3,1},{4,6},{5,7},{6,4},{7,5},{8,10},{9,11},{10,... | collective-permute-start | bytes 24584 | tf_op jit(solution)/shard_map/ppermute | solution.py:240

commit v5 on v4

--- a/solution.py
+++ b/solution.py
@@ -344,7 +344,7 @@
 
     heads = [exchange(chunk, m, shards) if m else chunk for m in masks]
     heads += [exchange(x, 2, shards) for x in heads]
-    tail = relay(tail, *heads[1 : len(masks)])
+    tail = relay(tail, heads[1], heads[2])
     tails = [exchange(tail, m, shards) if m else tail for m in masks]
     heads_a = stack(heads, tails[1:], "stack_heads")
     heads_b = exchange(heads_a, 1, shards)

time: 82.1 us -> 81.3 us (level)
  waiting for transfers between devices: 22.2 us -> 19.9 us
  starting transfers between devices: 29.3 us -> 30.8 us
    ppermute x22, waiting for transfers between devices: 22.2 us -> 19.9 us  [exchange(): return lax.ppermute(x, 'idx', [(i, i ^ mask) for i in range(shards)])]
    all_to_all x1, starting transfers between devices: 3.88 us -> 5.06 us  [body(): lax.all_to_all(scored, 'idx', split_axis=0, concat_axis=0, tiled=True)]
  transfers between devices with their start and end apart: 23 -> 23, of which waited for: 10 -> 9; matrix products, arithmetic and copies ran while one was open for 0% -> 0% of each run, Pallas kernels for 29% -> 29%
where the time goes in v5:
time: 81.3 us; the launch traced here: 81 us
  starting transfers between devices  30.8 us (38%)
  Pallas kernels  27.6 us (34%)
  waiting for transfers between devices  19.9 us (24%)
  local copies, waits for them, and re-layouts  1.93 us (2%)
  between operations  0.86 us (1%)
    ppermute x22, starting transfers between devices, exchange(): return lax.ppermute(x, 'idx', [(i, i ^ mask) for i in range(shards)])  25.7 us
    ppermute x22, waiting for transfers between devices, exchange(): return lax.ppermute(x, 'idx', [(i, i ^ mask) for i in range(shards)])  19.9 us
    pallas_call x1, Pallas kernels, body(): pl.pallas_call(gather_kernel, in_specs=[whole(ANY)] * 3, out_specs=whole(...  11.8 us
    all_to_all x1, starting transfers between devices, body(): lax.all_to_all(scored, 'idx', split_axis=0, concat_axis=0, tiled=True)  5.06 us
    pallas_call x2, Pallas kernels, coarse_scores(): pl.pallas_call(functools.partial(coarse_kernel, shards, order, block_rows...  4.28 us
    pallas_call x1, Pallas kernels, body(): pl.pallas_call(tail_kernel, in_specs=[whole(ANY)] * 2, out_specs=whole(VM...  3.19 us
    pallas_call x1, Pallas kernels, body(): pl.pallas_call(functools.partial(plan_kernel, shards, page_count), in_spe...  2.89 us
    unnamed x16, local copies, waits for them, and re-layouts  1.92 us
  transfers between devices with their start and end apart: 23, of which 9 were waited for; matrix products, arithmetic and copies ran while one was open for 0% of the time, Pallas kernels for 29%

profile of v5, /device:TPU:0, one launch (start us, length us, event | category | flops | bytes accessed | tf_op | source)
XLA Modules:
  0.0 81.0 jit_solution(1218482530707182212)
XLA Ops:
  0.6 2.9 %plan.1 = (bf16[160,256]{1,0:T(8,128)(2,1)}, s32[4,16]{1,0:T(4,128)}, s32[16,128]{1,0:T(8,128)}) custom-call(bf16[128,1024]{1,0:T(8,128)(2,1)} %q_hbm.3, f32[1024,1024]{1,0:T(8,128)} %rot_hbm.3, s32[4,16]{1,0:T(4,128)} %probes_hbm.1, s32[8,128]{1,0:T(8,128)} %bitcast.18, s32[8,128]{1,0:T(8,128)} %bitcast.19), custom_call_target="tpu_custom_call" | custom-call | bytes 6000000 | tf_op jit(solution)/shard_map/plan/pallas_call | solution.py:259
  3.6 4.1 %collective-permute-start.1 = (bf16[160,256]{1,0:T(8,128)(2,1)}, bf16[160,256]{1,0:T(8,128)(2,1)S(1)}, u32[]{:S(2)}, u32[]{:S(2)}) collective-permute-start(bf16[160,256]{1,0:T(8,128)(2,1)} %get-tuple-element.12.refs_0_), channel_id=1, source_target_pairs={{0,8},{1,9},{2,10},{3,11},{4,12},{5,13},{6,14},{7,15},{8,0},{9,1},... | collective-permute-start | bytes 245768 | tf_op jit(solution)/shard_map/ppermute | solution.py:240
  7.6 1.6 %collective-permute-start = (bf16[160,256]{1,0:T(8,128)(2,1)}, bf16[160,256]{1,0:T(8,128)(2,1)S(1)}, u32[]{:S(2)}, u32[]{:S(2)}) collective-permute-start(bf16[160,256]{1,0:T(8,128)(2,1)} %get-tuple-element.12.refs_0_), channel_id=1, source_target_pairs={{0,4},{1,5},{2,6},{3,7},{4,0},{5,1},{6,2},{7,3},{8,12},{9,13},{10,... | collective-permute-start | bytes 245768 | tf_op jit(solution)/shard_map/ppermute | solution.py:240
  9.2 3.2 %rotate_tail.1.refs_0_ = bf16[128,768]{1,0:T(8,128)(2,1)} custom-call(bf16[128,1024]{1,0:T(8,128)(2,1)} %q_hbm.3, f32[1024,1024]{1,0:T(8,128)} %rot_hbm.3), custom_call_target="tpu_custom_call" | custom-call | bytes 9000000 | tf_op jit(solution)/shard_map/rotate_tail/pallas_call | solution.py:280
  12.5 0.9 %copy-done.2 = bf16[128,768]{1,0:T(8,128)(2,1)S(1)} copy-done((bf16[128,768]{1,0:T(8,128)(2,1)S(1)}, bf16[128,768]{1,0:T(8,128)(2,1)}, u32[]{:S(2)}) %copy-start.2) | copy-done | bytes 196632
  13.4 4.1 %collective-permute-start.9 = (bf16[128,768]{1,0:T(8,128)(2,1)S(1)}, bf16[128,768]{1,0:T(8,128)(2,1)}, u32[]{:S(2)}, u32[]{:S(2)}) collective-permute-start(bf16[128,768]{1,0:T(8,128)(2,1)S(1)} %relay.1.refs_0_), channel_id=1, source_target_pairs={{0,12},{1,13},{2,14},{3,15},{4,8},{5,9},{6,10},{7,11},{8,4},{9,5},... | collective-permute-start | bytes 589832 | tf_op jit(solution)/shard_map/ppermute | solution.py:240
  18.1 1.5 %collective-permute-start.3 = (bf16[160,256]{1,0:T(8,128)(2,1)S(1)}, bf16[160,256]{1,0:T(8,128)(2,1)S(1)}, u32[]{:S(2)}, u32[]{:S(2)}) collective-permute-start(bf16[160,256]{1,0:T(8,128)(2,1)S(1)} %copy-done.5), channel_id=1, source_target_pairs={{0,2},{1,3},{2,0},{3,1},{4,6},{5,7},{6,4},{7,5},{8,10},{9,11},{10,... | collective-permute-start | bytes 245768 | tf_op jit(solution)/shard_map/ppermute | solution.py:240
  20.1 2.4 %collective-permute-done.3.refs_4_ = bf16[160,256]{1,0:T(8,128)(2,1)S(1)} collective-permute-done((bf16[160,256]{1,0:T(8,128)(2,1)S(1)}, bf16[160,256]{1,0:T(8,128)(2,1)S(1)}, u32[]{:S(2)}, u32[]{:S(2)}) %collective-permute-start.3) | collective-permute-done | bytes 81952 | tf_op jit(solution)/shard_map/ppermute | solution.py:240
  22.5 1.5 %collective-permute-start.5 = (bf16[160,256]{1,0:T(8,128)(2,1)S(1)}, bf16[160,256]{1,0:T(8,128)(2,1)S(1)}, u32[]{:S(2)}, u32[]{:S(2)}) collective-permute-start(bf16[160,256]{1,0:T(8,128)(2,1)S(1)} %collective-permute-done.1.refs_2_), channel_id=1, source_target_pairs={{0,2},{1,3},{2,0},{3,1},{4,6},{5,7},{6,4},{7,5},{8,10},{9,11},{10,... | collective-permute-start | bytes 245768 | tf_op jit(solution)/shard_map/ppermute | solution.py:240
  24.0 0.9 %collective-permute-done.6.refs_7_ = bf16[160,256]{1,0:T(8,128)(2,1)S(1)} collective-permute-done((bf16[160,256]{1,0:T(8,128)(2,1)S(1)}, bf16[160,256]{1,0:T(8,128)(2,1)S(1)}, u32[]{:S(2)}, u32[]{:S(2)}) %collective-permute-start.6) | collective-permute-done | bytes 81952 | tf_op jit(solution)/shard_map/ppermute | solution.py:240
  25.4 1.6 %collective-permute-done.5.refs_6_ = bf16[160,256]{1,0:T(8,128)(2,1)S(1)} collective-permute-done((bf16[160,256]{1,0:T(8,128)(2,1)S(1)}, bf16[160,256]{1,0:T(8,128)(2,1)S(1)}, u32[]{:S(2)}, u32[]{:S(2)}) %collective-permute-start.5) | collective-permute-done | bytes 81952 | tf_op jit(solution)/shard_map/ppermute | solution.py:240
  26.9 2.4 %collective-permute-done.4.refs_5_ = bf16[160,256]{1,0:T(8,128)(2,1)S(1)} collective-permute-done((bf16[160,256]{1,0:T(8,128)(2,1)S(1)}, bf16[160,256]{1,0:T(8,128)(2,1)S(1)}, u32[]{:S(2)}, u32[]{:S(2)}) %collective-permute-start.4) | collective-permute-done | bytes 81952 | tf_op jit(solution)/shard_map/ppermute | solution.py:240
  29.3 4.0 %collective-permute-done.8.refs_9_.refs_2_ = bf16[128,768]{1,0:T(8,128)(2,1)} collective-permute-done((bf16[128,768]{1,0:T(8,128)(2,1)S(1)}, bf16[128,768]{1,0:T(8,128)(2,1)}, u32[]{:S(2)}, u32[]{:S(2)}) %collective-permute-start.8) | collective-permute-done | bytes 196640 | tf_op jit(solution)/shard_map/ppermute | solution.py:240
  33.5 1.6 %collective-permute-start.11 = (bf16[128,768]{1,0:T(8,128)(2,1)}, bf16[128,768]{1,0:T(8,128)(2,1)}, u32[]{:S(2)}, u32[]{:S(2)}) collective-permute-start(bf16[128,768]{1,0:T(8,128)(2,1)} %copy-done.3), channel_id=1, source_target_pairs={{0,2},{1,3},{2,0},{3,1},{4,6},{5,7},{6,4},{7,5},{8,10},{9,11},{10,... | collective-permute-start | bytes 589832 | tf_op jit(solution)/shard_map/ppermute | solution.py:240
  35.6 1.6 %collective-permute-start.13 = (bf16[128,768]{1,0:T(8,128)(2,1)}, bf16[128,768]{1,0:T(8,128)(2,1)}, u32[]{:S(2)}, u32[]{:S(2)}) collective-permute-start(bf16[128,768]{1,0:T(8,128)(2,1)} %collective-permute-done.8.refs_9_.refs_2_), channel_id=1, source_target_pairs={{0,2},{1,3},{2,0},{3,1},{4,6},{5,7},{6,4},{7,5},{8,10},{9,11},{10,... | collective-permute-start | bytes 589832 | tf_op jit(solution)/shard_map/ppermute | solution.py:240
  37.6 2.1 %coarse_scores.2 = (bf16[16,8,32,128]{3,2,1,0:T(8,128)(2,1)S(1)}, s32[2,8,128]{2,1,0:T(8,128)S(1)}) custom-call(s32[1]{0:T(128)} %bitcast.2.me_ref, bf16[8,160,256]{2,1,0:T(8,128)(2,1)S(1)} %stack_heads.1.pieces.heads, bf16[32,128,256]{2,1,0:T(8,128)(2,1)S(1)} %copy-done), custom_call_target="tpu_custom_call" | custom-call | bytes 9000000 | tf_op jit(solution)/shard_map/coarse_scores/pallas_call | solution.py:325
  39.8 2.1 %coarse_scores.3 = (bf16[16,8,32,128]{3,2,1,0:T(8,128)(2,1)S(1)}, s32[2,8,128]{2,1,0:T(8,128)S(1)}) custom-call(s32[1]{0:T(128)} %bitcast.2.me_ref, bf16[8,160,256]{2,1,0:T(8,128)(2,1)S(1)} %collective-permute-done.10.pieces.heads, bf16[32,128,256]{2,1,0:T(8,128)(2,1)S(1)} %copy-done, ...), custom_call_target="tpu_custom_call", output_to_operand_aliasing={{0}: (3, {})} | custom-call | bytes 9000000 | tf_op jit(solution)/shard_map/coarse_scores/pallas_call | solution.py:325
  41.9 1.0 %copy-done.1 = bf16[16,8,32,128]{3,2,1,0:T(8,128)(2,1)} copy-done((bf16[16,8,32,128]{3,2,1,0:T(8,128)(2,1)}, bf16[16,8,32,128]{3,2,1,0:T(8,128)(2,1)S(1)}, u32[]{:S(2)}) %copy-start.1) | copy-done | bytes 1048600
  42.9 5.1 %all-to-all-start = ((bf16[16,8,32,128]{3,2,1,0:T(8,128)(2,1)}), bf16[16,8,32,128]{3,2,1,0:T(8,128)(2,1)S(1)}, u32[]{:S(2)}, u32[]{:S(2)}) async-start(bf16[16,8,32,128]{3,2,1,0:T(8,128)(2,1)} %copy-done.1), calls=%async_computation | async-start | bytes 2097152 | tf_op jit(solution)/shard_map/all_to_all | solution.py:354
  48.0 11.8 %gather_rows.1.refs_8_.rows_ref = bf16[2,8,128,1024]{3,2,1,0:T(8,128)(2,1)S(1)} custom-call(s32[2,8,128]{2,1,0:T(8,128)S(1)} %get-tuple-element.17.list_a.list_ref, s32[2,8,128]{2,1,0:T(8,128)S(1)} %get-tuple-element.16.list_b.list_ref, f32[4096,1024]{1,0:T(8,128)} %bitcast.16), custom_call_target="tpu_custom_call" | custom-call | bytes 36000000 | tf_op jit(solution)/shard_map/gather_rows/pallas_call | solution.py:356
  59.8 1.5 %stack_tails.1.refs_0_ = bf16[8,128,768]{2,1,0:T(8,128)(2,1)S(1)} custom-call(bf16[128,768]{1,0:T(8,128)(2,1)S(1)} %copy-done.4, bf16[128,768]{1,0:T(8,128)(2,1)} %collective-permute-done.7.refs_8_.refs_1_, bf16[128,768]{1,0:T(8,128)(2,1)} %collective-permute-done.8.refs_9_.refs_2_, bf16[128,768]{1,0:T(8,128)(2,1)} %collective-permute-done.9.refs_10_.refs_3_, ...), custom_call_target="tpu_custom_call" | custom-call | bytes 3000000 | tf_op jit(solution)/shard_map/stack_tails/pallas_call | solution.py:301
  61.8 0.7 rerank_scores.2.refs_1_
  62.6 2.3 %collective-permute-done.15.refs_0_ = bf16[8,128,768]{2,1,0:T(8,128)(2,1)S(1)} collective-permute-done((bf16[8,128,768]{2,1,0:T(8,128)(2,1)S(1)}, bf16[8,128,768]{2,1,0:T(8,128)(2,1)S(1)}, u32[]{:S(2)}, u32[]{:S(2)}) %collective-permute-start.15) | collective-permute-done | bytes 1572896 | tf_op jit(solution)/shard_map/ppermute | solution.py:240
  64.8 0.7 rerank_scores.3
  65.6 3.8 %collective-permute-start.18 = (f32[4,128]{1,0:T(4,128)S(1)}, f32[4,128]{1,0:T(4,128)S(1)}, u32[]{:S(2)}, u32[]{:S(2)}) collective-permute-start(f32[4,128]{1,0:T(4,128)S(1)} %get-tuple-element.21), channel_id=1, source_target_pairs={{0,12},{1,13},{2,14},{3,15},{4,8},{5,9},{6,10},{7,11},{8,4},{9,5},... | collective-permute-start | bytes 6152 | tf_op jit(solution)/shard_map/ppermute | solution.py:240
  69.4 0.7 collective-permute-start.16
  70.1 1.1 %collective-permute-done.18 = f32[4,128]{1,0:T(4,128)S(1)} collective-permute-done((f32[4,128]{1,0:T(4,128)S(1)}, f32[4,128]{1,0:T(4,128)S(1)}, u32[]{:S(2)}, u32[]{:S(2)}) %collective-permute-start.18) | collective-permute-done | bytes 2080 | tf_op jit(solution)/shard_map/ppermute | solution.py:240
  71.2 3.5 %collective-permute-done.17 = f32[4,128]{1,0:T(4,128)S(1)} collective-permute-done((f32[4,128]{1,0:T(4,128)S(1)}, f32[4,128]{1,0:T(4,128)S(1)}, u32[]{:S(2)}, u32[]{:S(2)}) %collective-permute-start.17) | collective-permute-done | bytes 2080 | tf_op jit(solution)/shard_map/ppermute | solution.py:240
  75.2 1.2 %collective-permute-start.20 = (f32[4,4,128]{2,1,0:T(4,128)S(1)}, f32[4,4,128]{2,1,0:T(4,128)S(1)}, u32[]{:S(2)}, u32[]{:S(2)}) collective-permute-start(f32[4,4,128]{2,1,0:T(4,128)S(1)} %pad_maximum_fusion.own_ref), channel_id=1, source_target_pairs={{0,1},{1,0},{2,3},{3,2},{4,5},{5,4},{6,7},{7,6},{8,9},{9,8},{10,11... | collective-permute-start | bytes 24584 | tf_op jit(solution)/shard_map/ppermute | solution.py:240
  76.9 1.5 %place_scores.1 = (bf16[128,2048]{1,0:T(8,128)(2,1)}, f32[8,128]{1,0:T(8,128)S(1)}) custom-call(s32[4,16]{1,0:T(4,128)S(1)} %copy-done.7, bf16[128,32,128]{2,1,0:T(8,128)(2,1)S(1)} %bitcast.15), custom_call_target="tpu_custom_call" | custom-call | bytes 3000000 | tf_op jit(solution)/shard_map/place_scores/pallas_call | solution.py:389
  78.4 1.6 %collective-permute-done.19.y_ref = f32[4,4,128]{2,1,0:T(4,128)S(1)} collective-permute-done((f32[4,4,128]{2,1,0:T(4,128)S(1)}, f32[4,4,128]{2,1,0:T(4,128)S(1)}, u32[]{:S(2)}, u32[]{:S(2)}) %collective-permute-start.19) | collective-permute-done | bytes 8224 | tf_op jit(solution)/shard_map/ppermute | solution.py:240
  80.0 1.0 %pick_answers.1 = f32[8,128]{1,0:T(8,128)} custom-call(s32[1]{0:T(128)} %bitcast.2.me_ref, f32[4,4,128]{2,1,0:T(4,128)S(1)} %pad_maximum_fusion.own_ref, f32[4,4,128]{2,1,0:T(4,128)S(1)} %collective-permute-done.19.y_ref, f32[4,4,128]{2,1,0:T(4,128)S(1)} %collective-permute-done.20.core_ref, f32[4,4,128]{2,1,0:T(4,128)S(1)} %collective-permute-done.21.both_ref, ...), custom_call_target="tpu_custom_call" | custom-call | bytes 3000000 | tf_op jit(solution)/shard_map/pick_answers/pallas_call | solution.py:401
  (44 shorter events, 4.2 us)
Async XLA Ops:
  3.5 14.5 %copy-start.5 = (bf16[160,256]{1,0:T(8,128)(2,1)S(1)}, bf16[160,256]{1,0:T(8,128)(2,1)}, u32[]{:S(2)}) copy-start(bf16[160,256]{1,0:T(8,128)(2,1)} %get-tuple-element.12.refs_0_) | copy-start | bytes 245764
  3.5 34.1 %copy-start = (bf16[32,128,256]{2,1,0:T(8,128)(2,1)S(1)}, bf16[32,128,256]{2,1,0:T(8,128)(2,1)}, u32[]{:S(2)}) copy-start(bf16[32,128,256]{2,1,0:T(8,128)(2,1)} %codes.3) | copy-start | bytes 6291460
  3.6 8.9 %collective-permute-start.1 = (bf16[160,256]{1,0:T(8,128)(2,1)}, bf16[160,256]{1,0:T(8,128)(2,1)S(1)}, u32[]{:S(2)}, u32[]{:S(2)}) collective-permute-start(bf16[160,256]{1,0:T(8,128)(2,1)} %get-tuple-element.12.refs_0_), channel_id=1, source_target_pairs={{0,8},{1,9},{2,10},{3,11},{4,12},{5,13},{6,14},{7,15},{8,0},{9,1},... | collective-permute-start | bytes 245768 | tf_op jit(solution)/shard_map/ppermute | solution.py:240
  7.6 4.8 %collective-permute-start = (bf16[160,256]{1,0:T(8,128)(2,1)}, bf16[160,256]{1,0:T(8,128)(2,1)S(1)}, u32[]{:S(2)}, u32[]{:S(2)}) collective-permute-start(bf16[160,256]{1,0:T(8,128)(2,1)} %get-tuple-element.12.refs_0_), channel_id=1, source_target_pairs={{0,4},{1,5},{2,6},{3,7},{4,0},{5,1},{6,2},{7,3},{8,12},{9,13},{10,... | collective-permute-start | bytes 245768 | tf_op jit(solution)/shard_map/ppermute | solution.py:240
  9.2 10.4 %collective-permute-start.2 = (bf16[160,256]{1,0:T(8,128)(2,1)}, bf16[160,256]{1,0:T(8,128)(2,1)S(1)}, u32[]{:S(2)}, u32[]{:S(2)}) collective-permute-start(bf16[160,256]{1,0:T(8,128)(2,1)} %get-tuple-element.12.refs_0_), channel_id=1, source_target_pairs={{0,12},{1,13},{2,14},{3,15},{4,8},{5,9},{6,10},{7,11},{8,4},{9,5},... | collective-permute-start | bytes 245768 | tf_op jit(solution)/shard_map/ppermute | solution.py:240
  12.4 0.9 %copy-start.2 = (bf16[128,768]{1,0:T(8,128)(2,1)S(1)}, bf16[128,768]{1,0:T(8,128)(2,1)}, u32[]{:S(2)}) copy-start(bf16[128,768]{1,0:T(8,128)(2,1)} %rotate_tail.1.refs_0_) | copy-start | bytes 589828
  13.4 20.0 %copy-start.3 = (bf16[128,768]{1,0:T(8,128)(2,1)}, bf16[128,768]{1,0:T(8,128)(2,1)S(1)}, u32[]{:S(2)}) copy-start(bf16[128,768]{1,0:T(8,128)(2,1)S(1)} %relay.1.refs_0_) | copy-start | bytes 589828
  13.4 16.0 %collective-permute-start.9 = (bf16[128,768]{1,0:T(8,128)(2,1)S(1)}, bf16[128,768]{1,0:T(8,128)(2,1)}, u32[]{:S(2)}, u32[]{:S(2)}) collective-permute-start(bf16[128,768]{1,0:T(8,128)(2,1)S(1)} %relay.1.refs_0_), channel_id=1, source_target_pairs={{0,12},{1,13},{2,14},{3,15},{4,8},{5,9},{6,10},{7,11},{8,4},{9,5},... | collective-permute-start | bytes 589832 | tf_op jit(solution)/shard_map/ppermute | solution.py:240
  17.5 15.9 %collective-permute-start.8 = (bf16[128,768]{1,0:T(8,128)(2,1)S(1)}, bf16[128,768]{1,0:T(8,128)(2,1)}, u32[]{:S(2)}, u32[]{:S(2)}) collective-permute-start(bf16[128,768]{1,0:T(8,128)(2,1)S(1)} %relay.1.refs_0_), channel_id=1, source_target_pairs={{0,8},{1,9},{2,10},{3,11},{4,12},{5,13},{6,14},{7,15},{8,0},{9,1},... | collective-permute-start | bytes 589832 | tf_op jit(solution)/shard_map/ppermute | solution.py:240
  17.5 15.9 %collective-permute-start.7 = (bf16[128,768]{1,0:T(8,128)(2,1)S(1)}, bf16[128,768]{1,0:T(8,128)(2,1)}, u32[]{:S(2)}, u32[]{:S(2)}) collective-permute-start(bf16[128,768]{1,0:T(8,128)(2,1)S(1)} %relay.1.refs_0_), channel_id=1, source_target_pairs={{0,4},{1,5},{2,6},{3,7},{4,0},{5,1},{6,2},{7,3},{8,12},{9,13},{10,... | collective-permute-start | bytes 589832 | tf_op jit(solution)/shard_map/ppermute | solution.py:240
  18.1 4.4 %collective-permute-start.3 = (bf16[160,256]{1,0:T(8,128)(2,1)S(1)}, bf16[160,256]{1,0:T(8,128)(2,1)S(1)}, u32[]{:S(2)}, u32[]{:S(2)}) collective-permute-start(bf16[160,256]{1,0:T(8,128)(2,1)S(1)} %copy-done.5), channel_id=1, source_target_pairs={{0,2},{1,3},{2,0},{3,1},{4,6},{5,7},{6,4},{7,5},{8,10},{9,11},{10,... | collective-permute-start | bytes 245768 | tf_op jit(solution)/shard_map/ppermute | solution.py:240
  19.6 5.3 %collective-permute-start.6 = (bf16[160,256]{1,0:T(8,128)(2,1)S(1)}, bf16[160,256]{1,0:T(8,128)(2,1)S(1)}, u32[]{:S(2)}, u32[]{:S(2)}) collective-permute-start(bf16[160,256]{1,0:T(8,128)(2,1)S(1)} %collective-permute-done.2.refs_3_), channel_id=1, source_target_pairs={{0,2},{1,3},{2,0},{3,1},{4,6},{5,7},{6,4},{7,5},{8,10},{9,11},{10,... | collective-permute-start | bytes 245768 | tf_op jit(solution)/shard_map/ppermute | solution.py:240
  22.5 4.4 %collective-permute-start.5 = (bf16[160,256]{1,0:T(8,128)(2,1)S(1)}, bf16[160,256]{1,0:T(8,128)(2,1)S(1)}, u32[]{:S(2)}, u32[]{:S(2)}) collective-permute-start(bf16[160,256]{1,0:T(8,128)(2,1)S(1)} %collective-permute-done.1.refs_2_), channel_id=1, source_target_pairs={{0,2},{1,3},{2,0},{3,1},{4,6},{5,7},{6,4},{7,5},{8,10},{9,11},{10,... | collective-permute-start | bytes 245768 | tf_op jit(solution)/shard_map/ppermute | solution.py:240
  24.9 4.4 %collective-permute-start.4 = (bf16[160,256]{1,0:T(8,128)(2,1)S(1)}, bf16[160,256]{1,0:T(8,128)(2,1)S(1)}, u32[]{:S(2)}, u32[]{:S(2)}) collective-permute-start(bf16[160,256]{1,0:T(8,128)(2,1)S(1)} %collective-permute-done.refs_1_), channel_id=1, source_target_pairs={{0,2},{1,3},{2,0},{3,1},{4,6},{5,7},{6,4},{7,5},{8,10},{9,11},{10,... | collective-permute-start | bytes 245768 | tf_op jit(solution)/shard_map/ppermute | solution.py:240
  33.4 6.3 %collective-permute-start.10 = (bf16[8,160,256]{2,1,0:T(8,128)(2,1)S(1)}, bf16[8,160,256]{2,1,0:T(8,128)(2,1)S(1)}, u32[]{:S(2)}, u32[]{:S(2)}) collective-permute-start(bf16[8,160,256]{2,1,0:T(8,128)(2,1)S(1)} %stack_heads.1.pieces.heads), channel_id=1, source_target_pairs={{0,1},{1,0},{2,3},{3,2},{4,5},{5,4},{6,7},{7,6},{8,9},{9,8},{10,11... | collective-permute-start | bytes 1966088 | tf_op jit(solution)/shard_map/ppermute | solution.py:240
  33.5 26.3 %collective-permute-start.11 = (bf16[128,768]{1,0:T(8,128)(2,1)}, bf16[128,768]{1,0:T(8,128)(2,1)}, u32[]{:S(2)}, u32[]{:S(2)}) collective-permute-start(bf16[128,768]{1,0:T(8,128)(2,1)} %copy-done.3), channel_id=1, source_target_pairs={{0,2},{1,3},{2,0},{3,1},{4,6},{5,7},{6,4},{7,5},{8,10},{9,11},{10,... | collective-permute-start | bytes 589832 | tf_op jit(solution)/shard_map/ppermute | solution.py:240
  35.1 24.7 %collective-permute-start.14 = (bf16[128,768]{1,0:T(8,128)(2,1)}, bf16[128,768]{1,0:T(8,128)(2,1)}, u32[]{:S(2)}, u32[]{:S(2)}) collective-permute-start(bf16[128,768]{1,0:T(8,128)(2,1)} %collective-permute-done.9.refs_10_.refs_3_), channel_id=1, source_target_pairs={{0,2},{1,3},{2,0},{3,1},{4,6},{5,7},{6,4},{7,5},{8,10},{9,11},{10,... | collective-permute-start | bytes 589832 | tf_op jit(solution)/shard_map/ppermute | solution.py:240
  35.6 24.2 %collective-permute-start.13 = (bf16[128,768]{1,0:T(8,128)(2,1)}, bf16[128,768]{1,0:T(8,128)(2,1)}, u32[]{:S(2)}, u32[]{:S(2)}) collective-permute-start(bf16[128,768]{1,0:T(8,128)(2,1)} %collective-permute-done.8.refs_9_.refs_2_), channel_id=1, source_target_pairs={{0,2},{1,3},{2,0},{3,1},{4,6},{5,7},{6,4},{7,5},{8,10},{9,11},{10,... | collective-permute-start | bytes 589832 | tf_op jit(solution)/shard_map/ppermute | solution.py:240
  37.1 22.7 %collective-permute-start.12 = (bf16[128,768]{1,0:T(8,128)(2,1)}, bf16[128,768]{1,0:T(8,128)(2,1)}, u32[]{:S(2)}, u32[]{:S(2)}) collective-permute-start(bf16[128,768]{1,0:T(8,128)(2,1)} %collective-permute-done.7.refs_8_.refs_1_), channel_id=1, source_target_pairs={{0,2},{1,3},{2,0},{3,1},{4,6},{5,7},{6,4},{7,5},{8,10},{9,11},{10,... | collective-permute-start | bytes 589832 | tf_op jit(solution)/shard_map/ppermute | solution.py:240
  41.9 1.0 %copy-start.1 = (bf16[16,8,32,128]{3,2,1,0:T(8,128)(2,1)}, bf16[16,8,32,128]{3,2,1,0:T(8,128)(2,1)S(1)}, u32[]{:S(2)}) copy-start(bf16[16,8,32,128]{3,2,1,0:T(8,128)(2,1)S(1)} %get-tuple-element.14) | copy-start | bytes 3145732
  42.9 34.0 %all-to-all-start = ((bf16[16,8,32,128]{3,2,1,0:T(8,128)(2,1)}), bf16[16,8,32,128]{3,2,1,0:T(8,128)(2,1)S(1)}, u32[]{:S(2)}, u32[]{:S(2)}) async-start(bf16[16,8,32,128]{3,2,1,0:T(8,128)(2,1)} %copy-done.1), calls=%async_computation | async-start | bytes 2097152 | tf_op jit(solution)/shard_map/all_to_all | solution.py:354
  48.0 11.8 %copy-start.4 = (bf16[128,768]{1,0:T(8,128)(2,1)S(1)}, bf16[128,768]{1,0:T(8,128)(2,1)}, u32[]{:S(2)}) copy-start(bf16[128,768]{1,0:T(8,128)(2,1)} %copy-done.3) | copy-start | bytes 589828
  61.3 3.5 %collective-permute-start.15 = (bf16[8,128,768]{2,1,0:T(8,128)(2,1)S(1)}, bf16[8,128,768]{2,1,0:T(8,128)(2,1)S(1)}, u32[]{:S(2)}, u32[]{:S(2)}) collective-permute-start(bf16[8,128,768]{2,1,0:T(8,128)(2,1)S(1)} %stack_tails.1.refs_0_), channel_id=1, source_target_pairs={{0,1},{1,0},{2,3},{3,2},{4,5},{5,4},{6,7},{7,6},{8,9},{9,8},{10,11... | collective-permute-start | bytes 4718600 | tf_op jit(solution)/shard_map/ppermute | solution.py:240
  62.5 14.4 %copy-start.7 = (s32[4,16]{1,0:T(4,128)S(1)}, s32[4,16]{1,0:T(4,128)}, u32[]{:S(2)}) copy-start(s32[4,16]{1,0:T(4,128)} %get-tuple-element.11.place_ref) | copy-start | bytes 772
  62.6 17.5 %copy-start.6 = (s32[16,128]{1,0:T(8,128)S(1)}, s32[16,128]{1,0:T(8,128)}, u32[]{:S(2)}) copy-start(s32[16,128]{1,0:T(8,128)} %get-tuple-element.18.place_ref) | copy-start | bytes 24580
  65.6 5.6 %collective-permute-start.18 = (f32[4,128]{1,0:T(4,128)S(1)}, f32[4,128]{1,0:T(4,128)S(1)}, u32[]{:S(2)}, u32[]{:S(2)}) collective-permute-start(f32[4,128]{1,0:T(4,128)S(1)} %get-tuple-element.21), channel_id=1, source_target_pairs={{0,12},{1,13},{2,14},{3,15},{4,8},{5,9},{6,10},{7,11},{8,4},{9,5},... | collective-permute-start | bytes 6152 | tf_op jit(solution)/shard_map/ppermute | solution.py:240
  69.4 5.4 %collective-permute-start.17 = (f32[4,128]{1,0:T(4,128)S(1)}, f32[4,128]{1,0:T(4,128)S(1)}, u32[]{:S(2)}, u32[]{:S(2)}) collective-permute-start(f32[4,128]{1,0:T(4,128)S(1)} %get-tuple-element.22), channel_id=1, source_target_pairs={{0,8},{1,9},{2,10},{3,11},{4,12},{5,13},{6,14},{7,15},{8,0},{9,1},... | collective-permute-start | bytes 6152 | tf_op jit(solution)/shard_map/ppermute | solution.py:240
  69.4 5.4 %collective-permute-start.16 = (f32[4,128]{1,0:T(4,128)S(1)}, f32[4,128]{1,0:T(4,128)S(1)}, u32[]{:S(2)}, u32[]{:S(2)}) collective-permute-start(f32[4,128]{1,0:T(4,128)S(1)} %get-tuple-element.23), channel_id=1, source_target_pairs={{0,4},{1,5},{2,6},{3,7},{4,0},{5,1},{6,2},{7,3},{8,12},{9,13},{10,... | collective-permute-start | bytes 6152 | tf_op jit(solution)/shard_map/ppermute | solution.py:240
  74.7 3.7 %collective-permute-start.21 = (f32[4,4,128]{2,1,0:T(4,128)S(1)}, f32[4,4,128]{2,1,0:T(4,128)S(1)}, u32[]{:S(2)}, u32[]{:S(2)}) collective-permute-start(f32[4,4,128]{2,1,0:T(4,128)S(1)} %pad_maximum_fusion.own_ref), channel_id=1, source_target_pairs={{0,3},{1,2},{2,1},{3,0},{4,7},{5,6},{6,5},{7,4},{8,11},{9,10},{10,... | collective-permute-start | bytes 24584 | tf_op jit(solution)/shard_map/ppermute | solution.py:240
  75.2 3.2 %collective-permute-start.20 = (f32[4,4,128]{2,1,0:T(4,128)S(1)}, f32[4,4,128]{2,1,0:T(4,128)S(1)}, u32[]{:S(2)}, u32[]{:S(2)}) collective-permute-start(f32[4,4,128]{2,1,0:T(4,128)S(1)} %pad_maximum_fusion.own_ref), channel_id=1, source_target_pairs={{0,1},{1,0},{2,3},{3,2},{4,5},{5,4},{6,7},{7,6},{8,9},{9,8},{10,11... | collective-permute-start | bytes 24584 | tf_op jit(solution)/shard_map/ppermute | solution.py:240
  76.4 3.7 %collective-permute-start.19 = (f32[4,4,128]{2,1,0:T(4,128)S(1)}, f32[4,4,128]{2,1,0:T(4,128)S(1)}, u32[]{:S(2)}, u32[]{:S(2)}) collective-permute-start(f32[4,4,128]{2,1,0:T(4,128)S(1)} %pad_maximum_fusion.own_ref), channel_id=1, source_target_pairs={{0,2},{1,3},{2,0},{3,1},{4,6},{5,7},{6,4},{7,5},{8,10},{9,11},{10,... | collective-permute-start | bytes 24584 | tf_op jit(solution)/shard_map/ppermute | solution.py:240

commit v6 on v5

--- a/solution.py
+++ b/solution.py
@@ -132,8 +132,8 @@
         out_ref[i] = refs[i][...]
 
 
-def relay_kernel(*refs):
-    del refs
+def relay_kernel(in_ref, *refs):
+    refs[-1][...] = in_ref[...]
 
 
 def coarse_kernel(shards, order, block_rows, me_ref, pieces, codes, *refs):
@@ -311,10 +311,9 @@
     def relay(x, *waits):
         return pl.pallas_call(
             relay_kernel,
-            in_specs=[whole(ANY)] * (1 + len(waits)),
-            out_specs=whole(ANY),
+            in_specs=[whole(VMEM)] + [whole(ANY)] * len(waits),
+            out_specs=whole(VMEM),
             out_shape=jax.ShapeDtypeStruct(x.shape, x.dtype),
-            input_output_aliases={0: 0},
             compiler_params=params(4 * MIB),
             cost_estimate=cost(1),
             name="relay",
@@ -344,8 +343,8 @@
 
     heads = [exchange(chunk, m, shards) if m else chunk for m in masks]
     heads += [exchange(x, 2, shards) for x in heads]
-    tail = relay(tail, heads[1], heads[2])
-    tails = [exchange(tail, m, shards) if m else tail for m in masks]
+    sent = relay(tail, heads[1], heads[2])
+    tails = [exchange(sent, m, shards) if m else tail for m in masks]
     heads_a = stack(heads, tails[1:], "stack_heads")
     heads_b = exchange(heads_a, 1, shards)
     tails += [exchange(x, 2, shards) for x in tails]

time: 81.3 us -> 81.3 us (level)
    unnamed x16 -> x14, local copies, waits for them, and re-layouts: 1.92 us -> 1.92 us
where the time goes in v6:
time: 81.3 us; the launch traced here: 81 us
  starting transfers between devices  30.8 us (38%)
  Pallas kernels  27.6 us (34%)
  waiting for transfers between devices  19.8 us (24%)
  local copies, waits for them, and re-layouts  1.93 us (2%)
  between operations  0.87 us (1%)
    ppermute x22, starting transfers between devices, exchange(): return lax.ppermute(x, 'idx', [(i, i ^ mask) for i in range(shards)])  25.8 us
    ppermute x22, waiting for transfers between devices, exchange(): return lax.ppermute(x, 'idx', [(i, i ^ mask) for i in range(shards)])  19.8 us
    pallas_call x1, Pallas kernels, body(): pl.pallas_call(gather_kernel, in_specs=[whole(ANY)] * 3, out_specs=whole(...  11.8 us
    all_to_all x1, starting transfers between devices, body(): lax.all_to_all(scored, 'idx', split_axis=0, concat_axis=0, tiled=True)  4.98 us
    pallas_call x2, Pallas kernels, coarse_scores(): pl.pallas_call(functools.partial(coarse_kernel, shards, order, block_rows...  4.28 us
    pallas_call x1, Pallas kernels, body(): pl.pallas_call(tail_kernel, in_specs=[whole(ANY)] * 2, out_specs=whole(VM...  3.19 us
    pallas_call x1, Pallas kernels, body(): pl.pallas_call(functools.partial(plan_kernel, shards, page_count), in_spe...  2.89 us
    unnamed x14, local copies, waits for them, and re-layouts  1.92 us
  transfers between devices with their start and end apart: 23, of which 9 were waited for; matrix products, arithmetic and copies ran while one was open for 0% of the time, Pallas kernels for 29%

profile of v6, /device:TPU:0, one launch (start us, length us, event | category | flops | bytes accessed | tf_op | source)
XLA Modules:
  0.0 81.0 jit_solution(4878493711608375860)
XLA Ops:
  0.6 2.9 %plan.1 = (bf16[160,256]{1,0:T(8,128)(2,1)}, s32[4,16]{1,0:T(4,128)}, s32[16,128]{1,0:T(8,128)}) custom-call(bf16[128,1024]{1,0:T(8,128)(2,1)} %q_hbm.3, f32[1024,1024]{1,0:T(8,128)} %rot_hbm.3, s32[4,16]{1,0:T(4,128)} %probes_hbm.1, s32[8,128]{1,0:T(8,128)} %bitcast.18, s32[8,128]{1,0:T(8,128)} %bitcast.19), custom_call_target="tpu_custom_call" | custom-call | bytes 6000000 | tf_op jit(solution)/shard_map/plan/pallas_call | solution.py:259
  3.5 4.1 %collective-permute-start.1 = (bf16[160,256]{1,0:T(8,128)(2,1)}, bf16[160,256]{1,0:T(8,128)(2,1)S(1)}, u32[]{:S(2)}, u32[]{:S(2)}) collective-permute-start(bf16[160,256]{1,0:T(8,128)(2,1)} %get-tuple-element.12.refs_0_), channel_id=1, source_target_pairs={{0,8},{1,9},{2,10},{3,11},{4,12},{5,13},{6,14},{7,15},{8,0},{9,1},... | collective-permute-start | bytes 245768 | tf_op jit(solution)/shard_map/ppermute | solution.py:240
  7.6 1.6 %collective-permute-start = (bf16[160,256]{1,0:T(8,128)(2,1)}, bf16[160,256]{1,0:T(8,128)(2,1)S(1)}, u32[]{:S(2)}, u32[]{:S(2)}) collective-permute-start(bf16[160,256]{1,0:T(8,128)(2,1)} %get-tuple-element.12.refs_0_), channel_id=1, source_target_pairs={{0,4},{1,5},{2,6},{3,7},{4,0},{5,1},{6,2},{7,3},{8,12},{9,13},{10,... | collective-permute-start | bytes 245768 | tf_op jit(solution)/shard_map/ppermute | solution.py:240
  9.2 3.2 %rotate_tail.1.in_ref.refs_0_ = bf16[128,768]{1,0:T(8,128)(2,1)} custom-call(bf16[128,1024]{1,0:T(8,128)(2,1)} %q_hbm.3, f32[1024,1024]{1,0:T(8,128)} %rot_hbm.3), custom_call_target="tpu_custom_call" | custom-call | bytes 9000000 | tf_op jit(solution)/shard_map/rotate_tail/pallas_call | solution.py:280
  12.5 0.9 %copy-done.2 = bf16[128,768]{1,0:T(8,128)(2,1)S(1)} copy-done((bf16[128,768]{1,0:T(8,128)(2,1)S(1)}, bf16[128,768]{1,0:T(8,128)(2,1)}, u32[]{:S(2)}) %copy-start.2) | copy-done | bytes 196632
  13.4 4.2 %collective-permute-start.9 = (bf16[128,768]{1,0:T(8,128)(2,1)S(1)}, bf16[128,768]{1,0:T(8,128)(2,1)}, u32[]{:S(2)}, u32[]{:S(2)}) collective-permute-start(bf16[128,768]{1,0:T(8,128)(2,1)S(1)} %relay.1), channel_id=1, source_target_pairs={{0,12},{1,13},{2,14},{3,15},{4,8},{5,9},{6,10},{7,11},{8,4},{9,5},... | collective-permute-start | bytes 589832 | tf_op jit(solution)/shard_map/ppermute | solution.py:240
  18.2 1.5 %collective-permute-start.3 = (bf16[160,256]{1,0:T(8,128)(2,1)S(1)}, bf16[160,256]{1,0:T(8,128)(2,1)S(1)}, u32[]{:S(2)}, u32[]{:S(2)}) collective-permute-start(bf16[160,256]{1,0:T(8,128)(2,1)S(1)} %copy-done.4), channel_id=1, source_target_pairs={{0,2},{1,3},{2,0},{3,1},{4,6},{5,7},{6,4},{7,5},{8,10},{9,11},{10,... | collective-permute-start | bytes 245768 | tf_op jit(solution)/shard_map/ppermute | solution.py:240
  20.2 2.4 %collective-permute-done.3.refs_4_ = bf16[160,256]{1,0:T(8,128)(2,1)S(1)} collective-permute-done((bf16[160,256]{1,0:T(8,128)(2,1)S(1)}, bf16[160,256]{1,0:T(8,128)(2,1)S(1)}, u32[]{:S(2)}, u32[]{:S(2)}) %collective-permute-start.3) | collective-permute-done | bytes 81952 | tf_op jit(solution)/shard_map/ppermute | solution.py:240
  22.7 1.5 %collective-permute-start.5 = (bf16[160,256]{1,0:T(8,128)(2,1)S(1)}, bf16[160,256]{1,0:T(8,128)(2,1)S(1)}, u32[]{:S(2)}, u32[]{:S(2)}) collective-permute-start(bf16[160,256]{1,0:T(8,128)(2,1)S(1)} %collective-permute-done.1.refs_1_.refs_2_), channel_id=1, source_target_pairs={{0,2},{1,3},{2,0},{3,1},{4,6},{5,7},{6,4},{7,5},{8,10},{9,11},{10,... | collective-permute-start | bytes 245768 | tf_op jit(solution)/shard_map/ppermute | solution.py:240
  24.2 0.9 %collective-permute-done.6.refs_7_ = bf16[160,256]{1,0:T(8,128)(2,1)S(1)} collective-permute-done((bf16[160,256]{1,0:T(8,128)(2,1)S(1)}, bf16[160,256]{1,0:T(8,128)(2,1)S(1)}, u32[]{:S(2)}, u32[]{:S(2)}) %collective-permute-start.6) | collective-permute-done | bytes 81952 | tf_op jit(solution)/shard_map/ppermute | solution.py:240
  25.5 1.6 %collective-permute-done.5.refs_6_ = bf16[160,256]{1,0:T(8,128)(2,1)S(1)} collective-permute-done((bf16[160,256]{1,0:T(8,128)(2,1)S(1)}, bf16[160,256]{1,0:T(8,128)(2,1)S(1)}, u32[]{:S(2)}, u32[]{:S(2)}) %collective-permute-start.5) | collective-permute-done | bytes 81952 | tf_op jit(solution)/shard_map/ppermute | solution.py:240
  27.1 2.4 %collective-permute-done.4.refs_5_ = bf16[160,256]{1,0:T(8,128)(2,1)S(1)} collective-permute-done((bf16[160,256]{1,0:T(8,128)(2,1)S(1)}, bf16[160,256]{1,0:T(8,128)(2,1)S(1)}, u32[]{:S(2)}, u32[]{:S(2)}) %collective-permute-start.4) | collective-permute-done | bytes 81952 | tf_op jit(solution)/shard_map/ppermute | solution.py:240
  29.5 3.9 %collective-permute-done.8.refs_9_.refs_2_ = bf16[128,768]{1,0:T(8,128)(2,1)} collective-permute-done((bf16[128,768]{1,0:T(8,128)(2,1)S(1)}, bf16[128,768]{1,0:T(8,128)(2,1)}, u32[]{:S(2)}, u32[]{:S(2)}) %collective-permute-start.8) | collective-permute-done | bytes 196640 | tf_op jit(solution)/shard_map/ppermute | solution.py:240
  33.6 1.6 %collective-permute-start.11 = (bf16[128,768]{1,0:T(8,128)(2,1)}, bf16[128,768]{1,0:T(8,128)(2,1)}, u32[]{:S(2)}, u32[]{:S(2)}) collective-permute-start(bf16[128,768]{1,0:T(8,128)(2,1)} %rotate_tail.1.in_ref.refs_0_), channel_id=1, source_target_pairs={{0,2},{1,3},{2,0},{3,1},{4,6},{5,7},{6,4},{7,5},{8,10},{9,11},{10,... | collective-permute-start | bytes 589832 | tf_op jit(solution)/shard_map/ppermute | solution.py:240
  35.7 1.6 %collective-permute-start.13 = (bf16[128,768]{1,0:T(8,128)(2,1)}, bf16[128,768]{1,0:T(8,128)(2,1)}, u32[]{:S(2)}, u32[]{:S(2)}) collective-permute-start(bf16[128,768]{1,0:T(8,128)(2,1)} %collective-permute-done.8.refs_9_.refs_2_), channel_id=1, source_target_pairs={{0,2},{1,3},{2,0},{3,1},{4,6},{5,7},{6,4},{7,5},{8,10},{9,11},{10,... | collective-permute-start | bytes 589832 | tf_op jit(solution)/shard_map/ppermute | solution.py:240
  37.7 2.1 %coarse_scores.2 = (bf16[16,8,32,128]{3,2,1,0:T(8,128)(2,1)S(1)}, s32[2,8,128]{2,1,0:T(8,128)S(1)}) custom-call(s32[1]{0:T(128)} %bitcast.2.me_ref, bf16[8,160,256]{2,1,0:T(8,128)(2,1)S(1)} %stack_heads.1.pieces.heads, bf16[32,128,256]{2,1,0:T(8,128)(2,1)S(1)} %copy-done), custom_call_target="tpu_custom_call" | custom-call | bytes 9000000 | tf_op jit(solution)/shard_map/coarse_scores/pallas_call | solution.py:324
  39.9 2.1 %coarse_scores.3 = (bf16[16,8,32,128]{3,2,1,0:T(8,128)(2,1)S(1)}, s32[2,8,128]{2,1,0:T(8,128)S(1)}) custom-call(s32[1]{0:T(128)} %bitcast.2.me_ref, bf16[8,160,256]{2,1,0:T(8,128)(2,1)S(1)} %collective-permute-done.10.pieces.heads, bf16[32,128,256]{2,1,0:T(8,128)(2,1)S(1)} %copy-done, ...), custom_call_target="tpu_custom_call", output_to_operand_aliasing={{0}: (3, {})} | custom-call | bytes 9000000 | tf_op jit(solution)/shard_map/coarse_scores/pallas_call | solution.py:324
  42.0 1.0 %copy-done.1 = bf16[16,8,32,128]{3,2,1,0:T(8,128)(2,1)} copy-done((bf16[16,8,32,128]{3,2,1,0:T(8,128)(2,1)}, bf16[16,8,32,128]{3,2,1,0:T(8,128)(2,1)S(1)}, u32[]{:S(2)}) %copy-start.1) | copy-done | bytes 1048600
  43.0 5.0 %all-to-all-start = ((bf16[16,8,32,128]{3,2,1,0:T(8,128)(2,1)}), bf16[16,8,32,128]{3,2,1,0:T(8,128)(2,1)S(1)}, u32[]{:S(2)}, u32[]{:S(2)}) async-start(bf16[16,8,32,128]{3,2,1,0:T(8,128)(2,1)} %copy-done.1), calls=%async_computation | async-start | bytes 2097152 | tf_op jit(solution)/shard_map/all_to_all | solution.py:353
  48.0 11.8 %gather_rows.1.refs_8_.rows_ref = bf16[2,8,128,1024]{3,2,1,0:T(8,128)(2,1)S(1)} custom-call(s32[2,8,128]{2,1,0:T(8,128)S(1)} %get-tuple-element.17.list_a.list_ref, s32[2,8,128]{2,1,0:T(8,128)S(1)} %get-tuple-element.16.list_b.list_ref, f32[4096,1024]{1,0:T(8,128)} %bitcast.16), custom_call_target="tpu_custom_call" | custom-call | bytes 36000000 | tf_op jit(solution)/shard_map/gather_rows/pallas_call | solution.py:355
  59.8 1.5 %stack_tails.1.refs_0_ = bf16[8,128,768]{2,1,0:T(8,128)(2,1)S(1)} custom-call(bf16[128,768]{1,0:T(8,128)(2,1)S(1)} %copy-done.3, bf16[128,768]{1,0:T(8,128)(2,1)} %collective-permute-done.7.refs_8_.refs_1_, bf16[128,768]{1,0:T(8,128)(2,1)} %collective-permute-done.8.refs_9_.refs_2_, bf16[128,768]{1,0:T(8,128)(2,1)} %collective-permute-done.9.refs_10_.refs_3_, ...), custom_call_target="tpu_custom_call" | custom-call | bytes 3000000 | tf_op jit(solution)/shard_map/stack_tails/pallas_call | solution.py:301
  61.8 0.7 rerank_scores.2.refs_1_
  62.6 2.3 %collective-permute-done.15.refs_0_ = bf16[8,128,768]{2,1,0:T(8,128)(2,1)S(1)} collective-permute-done((bf16[8,128,768]{2,1,0:T(8,128)(2,1)S(1)}, bf16[8,128,768]{2,1,0:T(8,128)(2,1)S(1)}, u32[]{:S(2)}, u32[]{:S(2)}) %collective-permute-start.15) | collective-permute-done | bytes 1572896 | tf_op jit(solution)/shard_map/ppermute | solution.py:240
  64.8 0.7 rerank_scores.3
  65.6 3.8 %collective-permute-start.18 = (f32[4,128]{1,0:T(4,128)S(1)}, f32[4,128]{1,0:T(4,128)S(1)}, u32[]{:S(2)}, u32[]{:S(2)}) collective-permute-start(f32[4,128]{1,0:T(4,128)S(1)} %get-tuple-element.21), channel_id=1, source_target_pairs={{0,12},{1,13},{2,14},{3,15},{4,8},{5,9},{6,10},{7,11},{8,4},{9,5},... | collective-permute-start | bytes 6152 | tf_op jit(solution)/shard_map/ppermute | solution.py:240
  69.3 0.7 collective-permute-start.16
  70.1 1.1 %collective-permute-done.18 = f32[4,128]{1,0:T(4,128)S(1)} collective-permute-done((f32[4,128]{1,0:T(4,128)S(1)}, f32[4,128]{1,0:T(4,128)S(1)}, u32[]{:S(2)}, u32[]{:S(2)}) %collective-permute-start.18) | collective-permute-done | bytes 2080 | tf_op jit(solution)/shard_map/ppermute | solution.py:240
  71.2 3.5 %collective-permute-done.17 = f32[4,128]{1,0:T(4,128)S(1)} collective-permute-done((f32[4,128]{1,0:T(4,128)S(1)}, f32[4,128]{1,0:T(4,128)S(1)}, u32[]{:S(2)}, u32[]{:S(2)}) %collective-permute-start.17) | collective-permute-done | bytes 2080 | tf_op jit(solution)/shard_map/ppermute | solution.py:240
  75.2 1.2 %collective-permute-start.20 = (f32[4,4,128]{2,1,0:T(4,128)S(1)}, f32[4,4,128]{2,1,0:T(4,128)S(1)}, u32[]{:S(2)}, u32[]{:S(2)}) collective-permute-start(f32[4,4,128]{2,1,0:T(4,128)S(1)} %pad_maximum_fusion.own_ref), channel_id=1, source_target_pairs={{0,1},{1,0},{2,3},{3,2},{4,5},{5,4},{6,7},{7,6},{8,9},{9,8},{10,11... | collective-permute-start | bytes 24584 | tf_op jit(solution)/shard_map/ppermute | solution.py:240
  76.9 1.5 %place_scores.1 = (bf16[128,2048]{1,0:T(8,128)(2,1)}, f32[8,128]{1,0:T(8,128)S(1)}) custom-call(s32[4,16]{1,0:T(4,128)S(1)} %copy-done.6, bf16[128,32,128]{2,1,0:T(8,128)(2,1)S(1)} %bitcast.15), custom_call_target="tpu_custom_call" | custom-call | bytes 3000000 | tf_op jit(solution)/shard_map/place_scores/pallas_call | solution.py:388
  78.4 1.6 %collective-permute-done.19.y_ref = f32[4,4,128]{2,1,0:T(4,128)S(1)} collective-permute-done((f32[4,4,128]{2,1,0:T(4,128)S(1)}, f32[4,4,128]{2,1,0:T(4,128)S(1)}, u32[]{:S(2)}, u32[]{:S(2)}) %collective-permute-start.19) | collective-permute-done | bytes 8224 | tf_op jit(solution)/shard_map/ppermute | solution.py:240
  80.0 1.0 %pick_answers.1 = f32[8,128]{1,0:T(8,128)} custom-call(s32[1]{0:T(128)} %bitcast.2.me_ref, f32[4,4,128]{2,1,0:T(4,128)S(1)} %pad_maximum_fusion.own_ref, f32[4,4,128]{2,1,0:T(4,128)S(1)} %collective-permute-done.19.y_ref, f32[4,4,128]{2,1,0:T(4,128)S(1)} %collective-permute-done.20.core_ref, f32[4,4,128]{2,1,0:T(4,128)S(1)} %collective-permute-done.21.both_ref, ...), custom_call_target="tpu_custom_call" | custom-call | bytes 3000000 | tf_op jit(solution)/shard_map/pick_answers/pallas_call | solution.py:400
  (42 shorter events, 4.3 us)
Async XLA Ops:
  3.5 14.7 %copy-start.4 = (bf16[160,256]{1,0:T(8,128)(2,1)S(1)}, bf16[160,256]{1,0:T(8,128)(2,1)}, u32[]{:S(2)}) copy-start(bf16[160,256]{1,0:T(8,128)(2,1)} %get-tuple-element.12.refs_0_) | copy-start | bytes 245764
  3.5 34.2 %copy-start = (bf16[32,128,256]{2,1,0:T(8,128)(2,1)S(1)}, bf16[32,128,256]{2,1,0:T(8,128)(2,1)}, u32[]{:S(2)}) copy-start(bf16[32,128,256]{2,1,0:T(8,128)(2,1)} %codes.3) | copy-start | bytes 6291460
  3.5 8.9 %collective-permute-start.1 = (bf16[160,256]{1,0:T(8,128)(2,1)}, bf16[160,256]{1,0:T(8,128)(2,1)S(1)}, u32[]{:S(2)}, u32[]{:S(2)}) collective-permute-start(bf16[160,256]{1,0:T(8,128)(2,1)} %get-tuple-element.12.refs_0_), channel_id=1, source_target_pairs={{0,8},{1,9},{2,10},{3,11},{4,12},{5,13},{6,14},{7,15},{8,0},{9,1},... | collective-permute-start | bytes 245768 | tf_op jit(solution)/shard_map/ppermute | solution.py:240
  7.6 4.8 %collective-permute-start = (bf16[160,256]{1,0:T(8,128)(2,1)}, bf16[160,256]{1,0:T(8,128)(2,1)S(1)}, u32[]{:S(2)}, u32[]{:S(2)}) collective-permute-start(bf16[160,256]{1,0:T(8,128)(2,1)} %get-tuple-element.12.refs_0_), channel_id=1, source_target_pairs={{0,4},{1,5},{2,6},{3,7},{4,0},{5,1},{6,2},{7,3},{8,12},{9,13},{10,... | collective-permute-start | bytes 245768 | tf_op jit(solution)/shard_map/ppermute | solution.py:240
  9.2 10.5 %collective-permute-start.2 = (bf16[160,256]{1,0:T(8,128)(2,1)}, bf16[160,256]{1,0:T(8,128)(2,1)S(1)}, u32[]{:S(2)}, u32[]{:S(2)}) collective-permute-start(bf16[160,256]{1,0:T(8,128)(2,1)} %get-tuple-element.12.refs_0_), channel_id=1, source_target_pairs={{0,12},{1,13},{2,14},{3,15},{4,8},{5,9},{6,10},{7,11},{8,4},{9,5},... | collective-permute-start | bytes 245768 | tf_op jit(solution)/shard_map/ppermute | solution.py:240
  12.4 0.9 %copy-start.2 = (bf16[128,768]{1,0:T(8,128)(2,1)S(1)}, bf16[128,768]{1,0:T(8,128)(2,1)}, u32[]{:S(2)}) copy-start(bf16[128,768]{1,0:T(8,128)(2,1)} %rotate_tail.1.in_ref.refs_0_) | copy-start | bytes 589828
  13.4 16.1 %collective-permute-start.9 = (bf16[128,768]{1,0:T(8,128)(2,1)S(1)}, bf16[128,768]{1,0:T(8,128)(2,1)}, u32[]{:S(2)}, u32[]{:S(2)}) collective-permute-start(bf16[128,768]{1,0:T(8,128)(2,1)S(1)} %relay.1), channel_id=1, source_target_pairs={{0,12},{1,13},{2,14},{3,15},{4,8},{5,9},{6,10},{7,11},{8,4},{9,5},... | collective-permute-start | bytes 589832 | tf_op jit(solution)/shard_map/ppermute | solution.py:240
  17.6 15.9 %collective-permute-start.8 = (bf16[128,768]{1,0:T(8,128)(2,1)S(1)}, bf16[128,768]{1,0:T(8,128)(2,1)}, u32[]{:S(2)}, u32[]{:S(2)}) collective-permute-start(bf16[128,768]{1,0:T(8,128)(2,1)S(1)} %relay.1), channel_id=1, source_target_pairs={{0,8},{1,9},{2,10},{3,11},{4,12},{5,13},{6,14},{7,15},{8,0},{9,1},... | collective-permute-start | bytes 589832 | tf_op jit(solution)/shard_map/ppermute | solution.py:240
  17.6 15.9 %collective-permute-start.7 = (bf16[128,768]{1,0:T(8,128)(2,1)S(1)}, bf16[128,768]{1,0:T(8,128)(2,1)}, u32[]{:S(2)}, u32[]{:S(2)}) collective-permute-start(bf16[128,768]{1,0:T(8,128)(2,1)S(1)} %relay.1), channel_id=1, source_target_pairs={{0,4},{1,5},{2,6},{3,7},{4,0},{5,1},{6,2},{7,3},{8,12},{9,13},{10,... | collective-permute-start | bytes 589832 | tf_op jit(solution)/shard_map/ppermute | solution.py:240
  18.2 4.4 %collective-permute-start.3 = (bf16[160,256]{1,0:T(8,128)(2,1)S(1)}, bf16[160,256]{1,0:T(8,128)(2,1)S(1)}, u32[]{:S(2)}, u32[]{:S(2)}) collective-permute-start(bf16[160,256]{1,0:T(8,128)(2,1)S(1)} %copy-done.4), channel_id=1, source_target_pairs={{0,2},{1,3},{2,0},{3,1},{4,6},{5,7},{6,4},{7,5},{8,10},{9,11},{10,... | collective-permute-start | bytes 245768 | tf_op jit(solution)/shard_map/ppermute | solution.py:240
  19.7 5.3 %collective-permute-start.6 = (bf16[160,256]{1,0:T(8,128)(2,1)S(1)}, bf16[160,256]{1,0:T(8,128)(2,1)S(1)}, u32[]{:S(2)}, u32[]{:S(2)}) collective-permute-start(bf16[160,256]{1,0:T(8,128)(2,1)S(1)} %collective-permute-done.2.refs_3_), channel_id=1, source_target_pairs={{0,2},{1,3},{2,0},{3,1},{4,6},{5,7},{6,4},{7,5},{8,10},{9,11},{10,... | collective-permute-start | bytes 245768 | tf_op jit(solution)/shard_map/ppermute | solution.py:240
  22.7 4.4 %collective-permute-start.5 = (bf16[160,256]{1,0:T(8,128)(2,1)S(1)}, bf16[160,256]{1,0:T(8,128)(2,1)S(1)}, u32[]{:S(2)}, u32[]{:S(2)}) collective-permute-start(bf16[160,256]{1,0:T(8,128)(2,1)S(1)} %collective-permute-done.1.refs_1_.refs_2_), channel_id=1, source_target_pairs={{0,2},{1,3},{2,0},{3,1},{4,6},{5,7},{6,4},{7,5},{8,10},{9,11},{10,... | collective-permute-start | bytes 245768 | tf_op jit(solution)/shard_map/ppermute | solution.py:240
  25.1 4.4 %collective-permute-start.4 = (bf16[160,256]{1,0:T(8,128)(2,1)S(1)}, bf16[160,256]{1,0:T(8,128)(2,1)S(1)}, u32[]{:S(2)}, u32[]{:S(2)}) collective-permute-start(bf16[160,256]{1,0:T(8,128)(2,1)S(1)} %collective-permute-done.refs_0_.refs_1_), channel_id=1, source_target_pairs={{0,2},{1,3},{2,0},{3,1},{4,6},{5,7},{6,4},{7,5},{8,10},{9,11},{10,... | collective-permute-start | bytes 245768 | tf_op jit(solution)/shard_map/ppermute | solution.py:240
  33.5 6.3 %collective-permute-start.10 = (bf16[8,160,256]{2,1,0:T(8,128)(2,1)S(1)}, bf16[8,160,256]{2,1,0:T(8,128)(2,1)S(1)}, u32[]{:S(2)}, u32[]{:S(2)}) collective-permute-start(bf16[8,160,256]{2,1,0:T(8,128)(2,1)S(1)} %stack_heads.1.pieces.heads), channel_id=1, source_target_pairs={{0,1},{1,0},{2,3},{3,2},{4,5},{5,4},{6,7},{7,6},{8,9},{9,8},{10,11... | collective-permute-start | bytes 1966088 | tf_op jit(solution)/shard_map/ppermute | solution.py:240
  33.6 26.2 %collective-permute-start.11 = (bf16[128,768]{1,0:T(8,128)(2,1)}, bf16[128,768]{1,0:T(8,128)(2,1)}, u32[]{:S(2)}, u32[]{:S(2)}) collective-permute-start(bf16[128,768]{1,0:T(8,128)(2,1)} %rotate_tail.1.in_ref.refs_0_), channel_id=1, source_target_pairs={{0,2},{1,3},{2,0},{3,1},{4,6},{5,7},{6,4},{7,5},{8,10},{9,11},{10,... | collective-permute-start | bytes 589832 | tf_op jit(solution)/shard_map/ppermute | solution.py:240
  35.2 24.6 %collective-permute-start.14 = (bf16[128,768]{1,0:T(8,128)(2,1)}, bf16[128,768]{1,0:T(8,128)(2,1)}, u32[]{:S(2)}, u32[]{:S(2)}) collective-permute-start(bf16[128,768]{1,0:T(8,128)(2,1)} %collective-permute-done.9.refs_10_.refs_3_), channel_id=1, source_target_pairs={{0,2},{1,3},{2,0},{3,1},{4,6},{5,7},{6,4},{7,5},{8,10},{9,11},{10,... | collective-permute-start | bytes 589832 | tf_op jit(solution)/shard_map/ppermute | solution.py:240
  35.7 24.1 %collective-permute-start.13 = (bf16[128,768]{1,0:T(8,128)(2,1)}, bf16[128,768]{1,0:T(8,128)(2,1)}, u32[]{:S(2)}, u32[]{:S(2)}) collective-permute-start(bf16[128,768]{1,0:T(8,128)(2,1)} %collective-permute-done.8.refs_9_.refs_2_), channel_id=1, source_target_pairs={{0,2},{1,3},{2,0},{3,1},{4,6},{5,7},{6,4},{7,5},{8,10},{9,11},{10,... | collective-permute-start | bytes 589832 | tf_op jit(solution)/shard_map/ppermute | solution.py:240
  37.2 22.6 %collective-permute-start.12 = (bf16[128,768]{1,0:T(8,128)(2,1)}, bf16[128,768]{1,0:T(8,128)(2,1)}, u32[]{:S(2)}, u32[]{:S(2)}) collective-permute-start(bf16[128,768]{1,0:T(8,128)(2,1)} %collective-permute-done.7.refs_8_.refs_1_), channel_id=1, source_target_pairs={{0,2},{1,3},{2,0},{3,1},{4,6},{5,7},{6,4},{7,5},{8,10},{9,11},{10,... | collective-permute-start | bytes 589832 | tf_op jit(solution)/shard_map/ppermute | solution.py:240
  42.0 1.0 %copy-start.1 = (bf16[16,8,32,128]{3,2,1,0:T(8,128)(2,1)}, bf16[16,8,32,128]{3,2,1,0:T(8,128)(2,1)S(1)}, u32[]{:S(2)}) copy-start(bf16[16,8,32,128]{3,2,1,0:T(8,128)(2,1)S(1)} %get-tuple-element.14) | copy-start | bytes 3145732
  43.0 33.9 %all-to-all-start = ((bf16[16,8,32,128]{3,2,1,0:T(8,128)(2,1)}), bf16[16,8,32,128]{3,2,1,0:T(8,128)(2,1)S(1)}, u32[]{:S(2)}, u32[]{:S(2)}) async-start(bf16[16,8,32,128]{3,2,1,0:T(8,128)(2,1)} %copy-done.1), calls=%async_computation | async-start | bytes 2097152 | tf_op jit(solution)/shard_map/all_to_all | solution.py:353
  48.0 11.8 %copy-start.3 = (bf16[128,768]{1,0:T(8,128)(2,1)S(1)}, bf16[128,768]{1,0:T(8,128)(2,1)}, u32[]{:S(2)}) copy-start(bf16[128,768]{1,0:T(8,128)(2,1)} %rotate_tail.1.in_ref.refs_0_) | copy-start | bytes 589828
  61.3 3.5 %collective-permute-start.15 = (bf16[8,128,768]{2,1,0:T(8,128)(2,1)S(1)}, bf16[8,128,768]{2,1,0:T(8,128)(2,1)S(1)}, u32[]{:S(2)}, u32[]{:S(2)}) collective-permute-start(bf16[8,128,768]{2,1,0:T(8,128)(2,1)S(1)} %stack_tails.1.refs_0_), channel_id=1, source_target_pairs={{0,1},{1,0},{2,3},{3,2},{4,5},{5,4},{6,7},{7,6},{8,9},{9,8},{10,11... | collective-permute-start | bytes 4718600 | tf_op jit(solution)/shard_map/ppermute | solution.py:240
  62.5 14.4 %copy-start.6 = (s32[4,16]{1,0:T(4,128)S(1)}, s32[4,16]{1,0:T(4,128)}, u32[]{:S(2)}) copy-start(s32[4,16]{1,0:T(4,128)} %get-tuple-element.11.place_ref) | copy-start | bytes 772
  62.5 17.5 %copy-start.5 = (s32[16,128]{1,0:T(8,128)S(1)}, s32[16,128]{1,0:T(8,128)}, u32[]{:S(2)}) copy-start(s32[16,128]{1,0:T(8,128)} %get-tuple-element.18.place_ref) | copy-start | bytes 24580
  65.6 5.6 %collective-permute-start.18 = (f32[4,128]{1,0:T(4,128)S(1)}, f32[4,128]{1,0:T(4,128)S(1)}, u32[]{:S(2)}, u32[]{:S(2)}) collective-permute-start(f32[4,128]{1,0:T(4,128)S(1)} %get-tuple-element.21), channel_id=1, source_target_pairs={{0,12},{1,13},{2,14},{3,15},{4,8},{5,9},{6,10},{7,11},{8,4},{9,5},... | collective-permute-start | bytes 6152 | tf_op jit(solution)/shard_map/ppermute | solution.py:240
  69.3 5.4 %collective-permute-start.17 = (f32[4,128]{1,0:T(4,128)S(1)}, f32[4,128]{1,0:T(4,128)S(1)}, u32[]{:S(2)}, u32[]{:S(2)}) collective-permute-start(f32[4,128]{1,0:T(4,128)S(1)} %get-tuple-element.22), channel_id=1, source_target_pairs={{0,8},{1,9},{2,10},{3,11},{4,12},{5,13},{6,14},{7,15},{8,0},{9,1},... | collective-permute-start | bytes 6152 | tf_op jit(solution)/shard_map/ppermute | solution.py:240
  69.3 5.4 %collective-permute-start.16 = (f32[4,128]{1,0:T(4,128)S(1)}, f32[4,128]{1,0:T(4,128)S(1)}, u32[]{:S(2)}, u32[]{:S(2)}) collective-permute-start(f32[4,128]{1,0:T(4,128)S(1)} %get-tuple-element.23), channel_id=1, source_target_pairs={{0,4},{1,5},{2,6},{3,7},{4,0},{5,1},{6,2},{7,3},{8,12},{9,13},{10,... | collective-permute-start | bytes 6152 | tf_op jit(solution)/shard_map/ppermute | solution.py:240
  74.7 3.7 %collective-permute-start.21 = (f32[4,4,128]{2,1,0:T(4,128)S(1)}, f32[4,4,128]{2,1,0:T(4,128)S(1)}, u32[]{:S(2)}, u32[]{:S(2)}) collective-permute-start(f32[4,4,128]{2,1,0:T(4,128)S(1)} %pad_maximum_fusion.own_ref), channel_id=1, source_target_pairs={{0,3},{1,2},{2,1},{3,0},{4,7},{5,6},{6,5},{7,4},{8,11},{9,10},{10,... | collective-permute-start | bytes 24584 | tf_op jit(solution)/shard_map/ppermute | solution.py:240
  75.2 3.2 %collective-permute-start.20 = (f32[4,4,128]{2,1,0:T(4,128)S(1)}, f32[4,4,128]{2,1,0:T(4,128)S(1)}, u32[]{:S(2)}, u32[]{:S(2)}) collective-permute-start(f32[4,4,128]{2,1,0:T(4,128)S(1)} %pad_maximum_fusion.own_ref), channel_id=1, source_target_pairs={{0,1},{1,0},{2,3},{3,2},{4,5},{5,4},{6,7},{7,6},{8,9},{9,8},{10,11... | collective-permute-start | bytes 24584 | tf_op jit(solution)/shard_map/ppermute | solution.py:240
  76.4 3.7 %collective-permute-start.19 = (f32[4,4,128]{2,1,0:T(4,128)S(1)}, f32[4,4,128]{2,1,0:T(4,128)S(1)}, u32[]{:S(2)}, u32[]{:S(2)}) collective-permute-start(f32[4,4,128]{2,1,0:T(4,128)S(1)} %pad_maximum_fusion.own_ref), channel_id=1, source_target_pairs={{0,2},{1,3},{2,0},{3,1},{4,6},{5,7},{6,4},{7,5},{8,10},{9,11},{10,... | collective-permute-start | bytes 24584 | tf_op jit(solution)/shard_map/ppermute | solution.py:240
